TPU v7x, 256 devices: a whole 4x4x8 slice. The times are simulated.
256 devices in a mesh: dp: 64 (over y_lo, z, x), tensor: 4 (over y_hi, core).
Axes of the slice: x: 4, y: 4 (y_hi: 2, y_lo: 2; y = y_hi * 2 + y_lo), z: 8, core: 2. Of those that a mesh axis runs over, the one named last changes fastest.
Arguments:
- img_feats: bfloat16 [16384, 1792], P('dp')
- txt_feats: bfloat16 [49152, 1024], P('dp')
- img_gain: float32 [1792], replicated, may hold values from 0.5 to 1.5
- txt_gain: float32 [1024], replicated, may hold values from 0.5 to 1.5
- img_weight: bfloat16 [1792, 1024], P(None, 'tensor')
- txt_weight: bfloat16 [1024, 1024], P(None, 'tensor')
- log_scale: float32 [1], replicated, may hold values from 2.5 to 2.9
- bias: float32 [1], replicated, may hold values from -10 to -8
- pair_perm: int32 [12288], replicated, may hold values from 0 to 12287, as said below
Outputs:
- loss: float32 [1], replicated
- img_weight_grad: float32 [1792, 1024], P(None, 'tensor')
- txt_weight_grad: float32 [1024, 1024], P(None, 'tensor')
- img_gain_grad: float32 [1792], replicated
- txt_gain_grad: float32 [1024], replicated
- scale_grad: float32 [1], replicated
- bias_grad: float32 [1], replicated
Inputs may be any that keep to these rules, and one draw needn't show every extreme that they name: `pair_perm`: each text is the partner of exactly one image.
All inputs are finite; a program needn't handle non-finite values.
Results may differ from a plain program's by a relative error of at most 0.0046.
The roundings to bfloat16 on the way count: a program that leaves them out, or rounds other values in their place, can miss the bound.
Values may be sent and summed in bfloat16 or wider, within the bound.
No kernel may reach another device: no remote copies, remote signals or barrier semaphores. Data moves between devices by JAX's collectives and lax.ppermute only.
A program may use at most 128 MiB of HBM per device.

v0:
```python
import math

import jax
import jax.numpy as jnp
from jax import lax
from jax.sharding import PartitionSpec as P

EPS = 1e-06


def normalize_rows(features, gain_vec):
    values = features.astype(jnp.float32)
    center = jnp.mean(values, axis=1, keepdims=True)
    spread = jnp.mean(values * values, axis=1, keepdims=True) - center * center
    scaled = (values - center) * lax.rsqrt(spread + EPS)
    return ((scaled * gain_vec).astype(jnp.bfloat16), scaled)


def row_gradient(grad_full, embedded, row_norms):
    values = embedded.astype(jnp.float32)
    inner_dot = jnp.sum(values * grad_full, axis=1, keepdims=True)
    return ((grad_full - values * inner_dot) / row_norms).astype(jnp.bfloat16)


def head_grads(hidden, scaled, weight, grad_round):
    weight_grad = lax.dot_general(
        hidden, grad_round, (((0,), (0,)), ((), ())), preferred_element_type=jnp.float32
    )
    hidden_grad = lax.dot_general(
        grad_round, weight, (((1,), (1,)), ((), ())), preferred_element_type=jnp.float32
    )
    return (weight_grad, jnp.sum(hidden_grad * scaled, axis=0))


def local(
    img_feats, txt_feats, img_gain, txt_gain, img_weight, txt_weight, log_scale, bias, pair_perm
):
    groups = lax.axis_size("dp")
    tensor_ways = lax.axis_size("tensor")
    dp_index = lax.axis_index("dp")
    tp_index = lax.axis_index("tensor")
    text_devices = groups // 4
    image_devices = groups - text_devices
    img_count = img_feats.shape[0]
    txt_count = txt_feats.shape[0]
    text_share = txt_count // tensor_ways
    text_piece = text_share // groups
    block_cols = text_devices * text_piece
    pair_count = pair_perm.shape[0]
    image_hidden, image_hat = normalize_rows(img_feats, img_gain)
    text_hidden, text_hat = normalize_rows(txt_feats, txt_gain)
    image_proj = jnp.dot(image_hidden, img_weight, preferred_element_type=jnp.float32)
    text_proj = jnp.dot(text_hidden, txt_weight, preferred_element_type=jnp.float32)
    image_sq, text_sq = lax.psum(
        (
            jnp.sum(image_proj * image_proj, axis=1, keepdims=True),
            jnp.sum(text_proj * text_proj, axis=1, keepdims=True),
        ),
        "tensor",
    )
    image_norm = jnp.sqrt(image_sq + EPS)
    text_norm = jnp.sqrt(text_sq + EPS)
    image_emb, text_emb = (
        lax.all_gather(
            (image_proj / image_norm).astype(jnp.bfloat16), "tensor", axis=1, tiled=True
        ),
        lax.all_gather((text_proj / text_norm).astype(jnp.bfloat16), "tensor", axis=1, tiled=True),
    )
    text_mine = lax.dynamic_slice_in_dim(text_emb, tp_index * text_share, text_share, 0)
    logit_scale = jnp.exp(log_scale[0])
    logit_bias = bias[0]
    got_texts = lax.all_to_all(text_mine, "dp", split_axis=0, concat_axis=0, tiled=True)
    row_ids = jnp.minimum(
        dp_index * img_count + jnp.arange(img_count, dtype=jnp.int32), pair_count - 1
    )
    row_weight = jnp.where(dp_index < image_devices, 1.0, 0.0).astype(jnp.float32)
    partner = jnp.take(pair_perm, row_ids)
    text_block = got_texts[image_devices * text_piece :]

    def column_ids(offset, length):
        col_index = offset + jnp.arange(length, dtype=jnp.int32)
        source = col_index // block_cols
        within = col_index % block_cols
        return (
            within // text_piece * txt_count
            + tp_index * text_share
            + source * text_piece
            + within % text_piece
        )

    def tile_terms(columns, offset):
        similar = lax.dot_general(
            columns, image_emb, (((1,), (1,)), ((), ())), preferred_element_type=jnp.float32
        )
        logits = logit_scale * similar + logit_bias
        labels = jnp.where(
            column_ids(offset, columns.shape[0])[:, None] == partner[None, :], 1.0, -1.0
        ).astype(jnp.float32)
        grad_tile = -labels * jax.nn.sigmoid(-labels * logits) * row_weight
        return (similar, logits, labels, grad_tile)

    gathered = lax.all_gather(text_block, "dp", axis=0, tiled=True)
    span_limit = 1 << max(1, 1024 // block_cols).bit_length() - 1
    tile_cols = math.gcd(groups, span_limit) * block_cols
    turn_count = gathered.shape[0] // tile_cols
    initial = (
        jnp.zeros((), jnp.float32),
        jnp.zeros((), jnp.float32),
        jnp.zeros((), jnp.float32),
        jnp.zeros(image_emb.shape, jnp.float32),
    )

    def forward(state, turn_idx):
        loss_sum, scale_sum, bias_sum, grad_rows = state
        offset = turn_idx * tile_cols
        columns = lax.dynamic_slice_in_dim(gathered, offset, tile_cols, 0)
        similar, logits, labels, grad_tile = tile_terms(columns, offset)
        loss_sum = loss_sum - jnp.sum(jax.nn.log_sigmoid(labels * logits) * row_weight)
        scale_sum = scale_sum + jnp.sum(grad_tile * similar)
        bias_sum = bias_sum + jnp.sum(grad_tile)
        grad_round = grad_tile.astype(jnp.bfloat16)
        grad_rows = grad_rows + lax.dot_general(
            grad_round, columns, (((0,), (0,)), ((), ())), preferred_element_type=jnp.float32
        )
        return (
            (loss_sum, scale_sum, bias_sum, grad_rows),
            jnp.dot(grad_round, image_emb, preferred_element_type=jnp.float32),
        )

    turn_ids = jnp.arange(turn_count, dtype=jnp.int32)
    (loss_sum, scale_sum, bias_sum, grad_rows), stacked = lax.scan(
        lambda state, turn_idx: forward(state, turn_idx), initial, turn_ids
    )
    grad_cols = stacked.reshape(gathered.shape[0], stacked.shape[2])
    text_grad = lax.psum_scatter(grad_cols, "dp", scatter_dimension=0, tiled=True) * logit_scale
    grad_rows = grad_rows * logit_scale
    text_padded = jnp.concatenate(
        [jnp.zeros((image_devices * text_piece, text_grad.shape[1]), jnp.float32), text_grad],
        axis=0,
    )
    text_dz = lax.all_to_all(text_padded, "dp", split_axis=0, concat_axis=0, tiled=True)
    image_quarter = img_count // tensor_ways
    image_dz_rows = lax.psum_scatter(grad_rows, "tensor", scatter_dimension=0, tiled=True)
    image_du = row_gradient(
        image_dz_rows,
        lax.dynamic_slice_in_dim(image_emb, tp_index * image_quarter, image_quarter, 0),
        lax.dynamic_slice_in_dim(image_norm, tp_index * image_quarter, image_quarter, 0),
    )
    text_du = row_gradient(
        text_dz,
        text_mine,
        lax.dynamic_slice_in_dim(text_norm, tp_index * text_share, text_share, 0),
    )
    image_back, text_back = (
        lax.all_to_all(image_du, "tensor", split_axis=1, concat_axis=0, tiled=True),
        lax.all_to_all(text_du, "tensor", split_axis=1, concat_axis=0, tiled=True),
    )
    img_weight_grad, img_gain_part = head_grads(image_hidden, image_hat, img_weight, image_back)
    txt_weight_grad, txt_gain_part = head_grads(text_hidden, text_hat, txt_weight, text_back)
    loss_sum, scale_sum, bias_sum, img_gain_grad, txt_gain_grad = lax.psum(
        (loss_sum, scale_sum * logit_scale, bias_sum, img_gain_part, txt_gain_part),
        ("dp", "tensor"),
    )
    img_weight_grad, txt_weight_grad = lax.psum((img_weight_grad, txt_weight_grad), "dp")
    loss = jnp.reshape(loss_sum / pair_count, (1,))
    return (
        loss,
        img_weight_grad,
        txt_weight_grad,
        img_gain_grad,
        txt_gain_grad,
        jnp.reshape(scale_sum, (1,)),
        jnp.reshape(bias_sum, (1,)),
    )


def solution(mesh):
    return jax.shard_map(
        local,
        mesh=mesh,
        in_specs=(
            P("dp", None),
            P("dp", None),
            P(),
            P(),
            P(None, "tensor"),
            P(None, "tensor"),
            P(),
            P(),
            P(),
        ),
        out_specs=(P(), P(None, "tensor"), P(None, "tensor"), P(), P(), P(), P()),
        check_vma=False,
    )
```

profile of v0, /device:TPU:32, one launch (start us, length us, event | category | flops | bytes accessed | tf_op | source)
XLA Modules:
  0.0 1479.9 jit_solution(7387449348738328744)
XLA Ops:
  15.1 10.1 all-reduce.3
  26.1 26.8 %all-gather.3.cloned.1.call-done = bf16[768,1024]{0,1:T(8,128)(2,1)} async-done(((bf16[768,256]{0,1:T(8,128)(2,1)}), bf16[768,1024]{0,1:T(8,128)(2,1)}) %all-gather.3.cloned.1.call-update) | async-done | bytes 1572880 | tf_op jit(solution)/shard_map/all_gather | solution.py:67
  54.7 29.1 %all_to_all.59 = bf16[64,3,1024]{2,1,0:T(4,128)(2,1)S(1)} all-to-all(bf16[64,3,1024]{2,1,0:T(4,128)(2,1)S(1)} %all_to_all.42), channel_id=1, replica_groups=mesh['dp'=64,'tensor'=4] {'dp'}, dimensions={0} | all-to-all | bytes 786432 | tf_op jit(solution)/shard_map/all_to_all | solution.py:72
  85.5 8.0 all_gather.11
  96.3 287.8 %all-gather.5.cloned.1.call-done = bf16[3072,1024]{1,0:T(8,128)(2,1)} async-done(((bf16[48,1024]{1,0:T(8,128)(2,1)}), bf16[3072,1024]{1,0:T(8,128)(2,1)}) %all-gather.5.cloned.1.call-update) | async-done | bytes 6291472 | tf_op jit(solution)/shard_map/all_gather | solution.py:102
  384.1 63.1 %while.22 = (s32[]{:T(128)}, f32[]{:T(128)}, f32[]{:T(128)}, f32[]{:T(128)}, f32[256,1024]{1,0:T(8,128)}, /*index=5*/f32[4,768,1024]{2,1,0:T(8,128)}, s32[4]{0:T...) while((s32[]{:T(128)}, f32[]{:T(128)}, f32[]{:T(128)}, ...), condition=%wide.region_12.13_spmd.clone, body=%wide.region_8.12_spmd.clone.sunk | while | flops 1218140672 | bytes 17059692 | solution.py:131
  385.4 5.1 fusion.92
  392.3 4.3 fusion.93
  396.6 3.1 bitcast_dynamic-update-slice_fusion.2
  400.9 5.1 fusion.92
  407.8 4.6 fusion.93
  412.4 3.1 bitcast_dynamic-update-slice_fusion.2
  416.8 5.1 fusion.92
  423.7 4.6 fusion.93
  428.3 3.1 bitcast_dynamic-update-slice_fusion.2
  432.7 5.1 fusion.92
  439.6 4.6 fusion.93
  444.2 3.0 bitcast_dynamic-update-slice_fusion.2
  447.3 2.5 copy.28
  452.1 2.5 copy.33
  454.7 334.0 %reduce-scatter.5.cloned.1.call-done = f32[48,1024]{1,0:T(8,128)} async-done(((f32[3072,1024]{1,0:T(8,128)}), f32[48,1024]{1,0:T(8,128)}) %reduce-scatter.5.cloned.1.call-update) | async-done | bytes 196624 | tf_op jit(solution)/shard_map/reduce_scatter | solution.py:135
  792.9 13.3 all-to-all-start.2
  806.9 24.0 %reduce-scatter.7.cloned.1.call-done = f32[64,1024]{1,0:T(8,128)} async-done(((f32[256,1024]{1,0:T(8,128)}), f32[64,1024]{1,0:T(8,128)}) %reduce-scatter.7.cloned.1.call-update) | async-done | bytes 262160
  835.5 4.1 all-to-all-start.1
  839.6 2.3 all_to_all.50
  849.1 4.6 all-to-all-start.3
  853.6 3.0 fusion.61
  856.7 5.9 all-to-all-done.3
  863.3 3.0 fusion.65
  869.7 78.0 %all-reduce.1 = (f32[]{:T(128)}, f32[1792]{0:T(1024)}, f32[1024]{0:T(1024)}, f32[1]{0:T(128)}, f32[1]{0:T(128)}) all-reduce(f32[]{:T(128)} %get-tuple-element.240, f32[1792]{0:T(1024)S(1)} %fusion.50, f32[1024]{0:T(1024)S(1)} %fusion.44, f32[1]{0:T(128)} %bitcast.17, f32[1]{0:T(128)} %bitcast.18), channel_id=1, replica_groups=mesh['dp'=64,'tensor'=4] {'dp','tensor'}, use_global_device_ids=true, to_apply=%region_13.14 | all-reduce | flops 2819 | bytes 22552 | tf_op jit(solution)/shard_map/psum | solution.py:160
  948.3 520.0 %all-reduce.6.cloned.1.call-done = (f32[1792,256]{1,0:T(8,128)}, f32[1024,256]{1,0:T(8,128)}) async-done(((f32[1792,256]{1,0:T(8,128)}, f32[1024,256]{1,0:T(8,128)}), (f32[1792,256]{1,0:T(8,128)}, f32[1024,256]{1,0:T(8,128)})) %all-reduce.6.cloned.1.call-update) | async-done | bytes 2883600 | tf_op jit(solution)/shard_map/psum | solution.py:164
  1468.3 2.9 copy.57
  (110 shorter events, 40.6 us)
Async XLA Ops:
  7.2 5.5 copy-start
  7.2 3.8 copy-start.2
  7.2 3.8 copy-start.13
  7.2 45.7 %all-gather.3.cloned.1.call-start = ((), (), s32[]{:S(2)}) async-start(), calls=%async_computation.6 | async-start | bytes 1966080 | tf_op jit(solution)/shard_map/all_gather | solution.py:67
  10.9 1.0 copy-start.8
  12.0 3.1 copy-start.3
  12.0 1.7 copy-start.5
  12.0 1.7 copy-start.16
  12.7 13.3 copy-start.14
  26.0 358.0 %all-gather.5.cloned.1.call-start = ((), (), s32[]{:S(2)}) async-start(), calls=%async_computation.7 | async-start | bytes 6389760 | tf_op jit(solution)/shard_map/all_gather | solution.py:102
  54.7 30.7 %copy-start.12 = (f32[256,256]{0,1:T(8,128)S(1)}, f32[256,256]{0,1:T(8,128)}, u32[]{:S(2)}) copy-start(f32[256,256]{0,1:T(8,128)} %get-tuple-element.386) | copy-start | bytes 786436
  54.7 39.8 %copy-start.1 = (s32[12288]{0:T(1024)S(1)}, s32[12288]{0:T(1024)}, u32[]{:S(2)}) copy-start(s32[12288]{0:T(1024)} %param.19) | copy-start | bytes 147460
  84.7 704.0 %reduce-scatter.5.cloned.1.call-start = ((), (), s32[]{:S(2)}) async-start(), calls=%async_computation.8 | async-start | bytes 12779520 | tf_op jit(solution)/shard_map/reduce_scatter | solution.py:135
  392.2 4.3 copy-start.7
  392.2 4.3 copy-start.17
  407.8 4.6 copy-start.7
  407.8 4.6 copy-start.17
  423.7 4.6 copy-start.7
  423.7 4.6 copy-start.17
  439.6 4.6 copy-start.7
  439.6 4.6 copy-start.17
  447.3 383.6 %reduce-scatter.7.cloned.1.call-start = ((), (), s32[]{:S(2)}) async-start(), calls=%async_computation.9 | async-start | bytes 1310720
  792.9 42.6 %all-to-all-start.2 = ((f32[64,3,1024]{2,1,0:T(4,128)}), f32[64,3,1024]{2,1,0:T(4,128)}, u32[]{:S(2)}, u32[]{:S(2)}) async-start(f32[64,3,1024]{2,1,0:T(4,128)} %all_to_all.48), calls=%async_computation.3 | async-start | bytes 2097152 | tf_op jit(solution)/shard_map/all_to_all | solution.py:141
  835.5 13.6 all-to-all-start.1
  849.1 13.5 all-to-all-start.3
  853.6 614.7 %all-reduce.6.cloned.1.call-start = ((), (), s32[]{:S(2)}) async-start(), calls=%async_computation.10 | async-start | bytes 5767168 | tf_op jit(solution)/shard_map/psum | solution.py:164
  862.6 0.8 copy-start.10
  866.3 1.2 copy-start.6
  866.3 1.2 copy-start.15
  867.5 1.5 copy-start.9
  867.5 1.5 copy-start.11
  1468.3 2.9 copy-start.4
Sparse Core Ops, SparseCore 0:
  26.2 26.7 all-gather.2
  84.8 299.2 all-gather.4
  447.4 341.2 reduce-scatter.4
  791.9 38.9 reduce-scatter.6
  866.5 601.8 all-reduce.5
where the time goes:
time: 1490 us; the launch traced here: 1480 us
  waiting for transfers between devices  1200 us (81%)
  blocking collectives  125 us (8%)
  matrix products  60.9 us (4%)
  local copies, waits for them, and re-layouts  32.6 us (2%)
  starting transfers between devices  22.1 us (1%)
  between operations  16.6 us (1%)
    psum x1, waiting for transfers between devices, local(): lax.psum((img_weight_grad, txt_weight_grad), 'dp')  520 us
    reduce_scatter x1, waiting for transfers between devices, local(): lax.psum_scatter(grad_cols, 'dp', scatter_dimension=0, tiled=True)  334 us
    all_gather x1, waiting for transfers between devices, local(): gathered = lax.all_gather(text_block, 'dp', axis=0, tiled=True)  288 us
    psum x1, blocking collectives, local(): lax.psum((loss_sum, scale_sum * logit_scale, bias_sum, img_gain_part, txt...  78 us
  transfers between devices with their start and end apart: 8, of which 6 were waited for; matrix products, arithmetic and copies ran while one was open for 2% of the time, Pallas kernels for 0%

commit v1 on v0

v1 whole, which is shorter than its diff:
```python
import jax
import jax.numpy as jnp
from jax import lax
from jax.experimental import pallas as pl
from jax.experimental.pallas import tpu as pltpu
from jax.sharding import Mesh, PartitionSpec as P

EPS = 1e-06
F32 = jnp.float32
BF16 = jnp.bfloat16
Z = 8
TEXT_Z = 4
DP = ("yl", "z", "x")
STEPS = 4


def hidden_rows(features, gain_vec):
    values = features.astype(F32)
    center = jnp.mean(values, axis=1, keepdims=True)
    spread = jnp.mean(values * values, axis=1, keepdims=True) - center * center
    scaled = (values - center) * lax.rsqrt(spread + EPS)
    return (scaled * gain_vec).astype(BF16)


def swap(value, axis):
    return lax.ppermute(value, axis, [(0, 1), (1, 0)])


def exchange(value, axes):
    return lax.all_to_all(value, axes, split_axis=0, concat_axis=0, tiled=True)


def split3(value):
    high = value.astype(BF16)
    rest = value - high.astype(F32)
    middle = rest.astype(BF16)
    return high, middle, (rest - middle.astype(F32)).astype(BF16)


def tile_kernel(
    factors, valid, partner, columns, emb_i, emb_t, out_i, out_t, out_s, acc, sums
):
    step = pl.program_id(0)
    scale, shift = factors[0], factors[1]

    @pl.when(step == 0)
    def _():
        acc[...] = jnp.zeros_like(acc)
        sums[...] = jnp.zeros_like(sums)

    @pl.when(valid[step] == 0)
    def _():
        out_i[...] = jnp.zeros_like(out_i)

    @pl.when(valid[step] != 0)
    def _():
        rows = jnp.concatenate(
            [
                jnp.concatenate([emb_i[0], emb_i[1]], axis=1),
                jnp.concatenate([emb_i[2], emb_i[3]], axis=1),
            ],
            axis=0,
        )
        texts = emb_t[...]
        similar = lax.dot_general(rows, texts, (((1,), (1,)), ((), ())), preferred_element_type=F32)
        logits = scale * similar + shift
        pair = partner[...] == columns[...]
        signed = jnp.where(pair, -logits, logits)
        small = jnp.exp(-jnp.abs(signed))
        total = 1.0 + small
        inverse = 1.0 / total
        sigmoid = jnp.where(signed >= 0, inverse, small * inverse)
        soft = jnp.maximum(signed, 0.0) + jnp.log(total) + (small - (total - 1.0)) * inverse
        grad = jnp.where(pair, -sigmoid, sigmoid)
        sums[0:1] += jnp.sum(soft, axis=0, keepdims=True)
        sums[1:2] += jnp.sum(grad * similar, axis=0, keepdims=True)
        sums[2:3] += jnp.sum(grad, axis=0, keepdims=True)
        rounded = grad.astype(BF16)
        acc[...] += lax.dot_general(rounded, rows, (((0,), (0,)), ((), ())), preferred_element_type=F32)
        grad_rows = jnp.dot(rounded, texts, preferred_element_type=F32)
        wide = rows.astype(F32)
        inner = jnp.sum(wide * grad_rows, axis=1, keepdims=True)
        result = (scale * (grad_rows - wide * inner)).astype(BF16)
        half = result.shape[1] // 2
        high = result.shape[0] // 2
        out_i[0] = result[:high, :half]
        out_i[1] = result[:high, half:]
        out_i[2] = result[high:, :half]
        out_i[3] = result[high:, half:]

    @pl.when(step == STEPS - 1)
    def _():
        texts = emb_t[...].astype(F32)
        grads = acc[...]
        inner = jnp.sum(texts * grads, axis=1, keepdims=True)
        out_t[...] = (scale * (grads - texts * inner)).astype(BF16)
        out_s[...] = jnp.broadcast_to(jnp.sum(sums[...], axis=1, keepdims=True), out_s.shape)


def tile_grads(factors, valid, partner, columns, emb_i, emb_t):
    slabs, high, half = emb_i.shape
    block = slabs // STEPS
    count, width = emb_t.shape
    return pl.pallas_call(
        tile_kernel,
        grid=(STEPS,),
        in_specs=[
            pl.BlockSpec(memory_space=pltpu.SMEM),
            pl.BlockSpec(memory_space=pltpu.SMEM),
            pl.BlockSpec((partner.shape[0] // STEPS, 1), lambda i: (i, 0)),
            pl.BlockSpec((1, count), lambda i: (0, 0)),
            pl.BlockSpec((block, high, half), lambda i: (i, 0, 0)),
            pl.BlockSpec((count, width), lambda i: (0, 0)),
        ],
        out_specs=[
            pl.BlockSpec((block, high, half), lambda i: (i, 0, 0)),
            pl.BlockSpec((count, width), lambda i: (0, 0)),
            pl.BlockSpec((8, 128), lambda i: (0, 0)),
        ],
        out_shape=[
            jax.ShapeDtypeStruct(emb_i.shape, BF16),
            jax.ShapeDtypeStruct(emb_t.shape, BF16),
            jax.ShapeDtypeStruct((8, 128), F32),
        ],
        scratch_shapes=[pltpu.VMEM((count, width), F32), pltpu.VMEM((8, count), F32)],
        compiler_params=pltpu.CompilerParams(vmem_limit_bytes=40 * 1024 * 1024),
    )(factors, valid, partner, columns, emb_i, emb_t)


def half_place(half, j):
    return TEXT_Z + j if half else TEXT_Z - 1 - j


def turn(k):
    return [
        (half_place(half, j), half_place(half, (j + k) % TEXT_Z))
        for half in range(2)
        for j in range(TEXT_Z)
    ]


def local(
    img_feats, txt_feats, img_gain, txt_gain, img_weight, txt_weight, log_scale, bias, pair_perm
):
    yl, z, x = lax.axis_index("yl"), lax.axis_index("z"), lax.axis_index("x")
    yh, core = lax.axis_index("yh"), lax.axis_index("co")
    pair_count = pair_perm.shape[0]
    img_count, txt_count = img_feats.shape[0], txt_feats.shape[0]
    is_text = (yl == 1) & (z >= TEXT_Z)
    near = jnp.where(z >= TEXT_Z, z - TEXT_Z, TEXT_Z - 1 - z)

    text_hidden = hidden_rows(txt_feats, txt_gain)
    image_hidden = hidden_rows(img_feats, img_gain)
    text_proj = jnp.dot(text_hidden, txt_weight, preferred_element_type=F32)
    image_proj = jnp.dot(image_hidden, img_weight, preferred_element_type=F32)
    squares = jnp.concatenate(
        [jnp.sum(text_proj * text_proj, axis=1), jnp.sum(image_proj * image_proj, axis=1)]
    )
    squares = squares + swap(squares, "co")
    squares = squares + swap(squares, "yh")
    norms = jnp.sqrt(squares + EPS)[:, None]
    text_norm, image_norm = norms[:txt_count], norms[txt_count:]
    text_emb = (text_proj / text_norm).astype(BF16)
    image_emb = (image_proj / image_norm).astype(BF16)

    image_half = lax.all_to_all(image_emb, "co", split_axis=0, concat_axis=1, tiled=True)
    image_all = lax.all_gather(image_half, ("yl", "x", "yh"), axis=0, tiled=False)

    piece = txt_count // 8
    text_half = lax.all_to_all(text_emb, "co", split_axis=0, concat_axis=1, tiled=True)
    width = text_half.shape[1]
    text_half = text_half.reshape(4, piece, width)

    def part(q):
        return lax.dynamic_index_in_dim(text_half, q, 0, keepdims=False)

    def y_index(pairs):
        return [(a[0] * 2 + a[1], b[0] * 2 + b[1]) for a, b in pairs]

    across = y_index([((1, 0), (1, 1)), ((1, 1), (1, 0))])
    straight = y_index([((1, 0), (0, 0)), ((1, 1), (0, 1))])
    diagonal = y_index([((1, 0), (0, 1)), ((1, 1), (0, 0))])
    ys = ("yl", "yh")
    got_across = lax.ppermute(part(2 + (1 - yh)), ys, across)
    got_straight = lax.ppermute(part(yh), ys, straight)
    got_diagonal = lax.ppermute(part(1 - yh), ys, diagonal)
    mine = jnp.where(yl == 1, part(2 + yh), got_straight)
    other = jnp.where(yl == 1, got_across, got_diagonal)
    chunk = jnp.where(
        yh == 0,
        jnp.concatenate([mine, other], axis=1),
        jnp.concatenate([other, mine], axis=1),
    )
    mirror = [(a, Z - 1 - a) for a in range(TEXT_Z, Z)]
    got_mirror = lax.ppermute(chunk, "z", mirror)
    chunk = jnp.where(z >= TEXT_Z, chunk, got_mirror)
    chunks = jnp.stack([chunk] + [lax.ppermute(chunk, "z", turn(k)) for k in range(1, TEXT_Z)])
    text_tile = lax.all_gather(chunks, "co", axis=0, tiled=False)
    text_tile = text_tile.reshape(2 * TEXT_Z * piece, 2 * width)

    quarter = yl * 2 + yh
    order = jnp.arange(TEXT_Z, dtype=jnp.int32)
    group = jnp.mod(near - order + TEXT_Z, TEXT_Z) * 4 + x
    columns = (
        group[None, :, None] * txt_count
        + jnp.arange(2, dtype=jnp.int32)[:, None, None] * (4 * piece)
        + quarter * piece
        + jnp.arange(piece, dtype=jnp.int32)[None, None, :]
    ).reshape(1, -1)
    padded = jnp.concatenate(
        [pair_perm, jnp.full((16 * img_count,), -1, jnp.int32)]
    ).reshape(2, Z, 4, 2, img_count // 2)
    partner = lax.dynamic_index_in_dim(
        lax.dynamic_index_in_dim(padded, z, 1, keepdims=False), core, 2, keepdims=False
    ).reshape(-1, 1)
    valid = jnp.concatenate(
        [jnp.ones((2,), jnp.int32), jnp.full((2,), 1, jnp.int32) * (z < TEXT_Z).astype(jnp.int32)]
    )
    logit_scale = jnp.exp(log_scale[0])
    factors = jnp.stack([logit_scale, bias[0]])
    image_part, text_part, part_sums = tile_grads(
        factors,
        valid,
        partner,
        columns,
        image_all.reshape(16, img_count // 2, width),
        text_tile,
    )

    image_sum = jnp.sum(
        exchange(image_part, ("yl", "x", "yh")).astype(F32), axis=0
    )
    half_norm = lax.dynamic_slice_in_dim(image_norm, core * (img_count // 2), img_count // 2, 0)
    image_du = lax.all_to_all(
        (image_sum / half_norm).astype(BF16), "co", split_axis=1, concat_axis=0, tiled=True
    )

    text_part = text_part.reshape(2, TEXT_Z, piece, 2 * width)
    kept = lax.dynamic_index_in_dim(text_part, core, 0, keepdims=False)
    sent = lax.dynamic_index_in_dim(text_part, 1 - core, 0, keepdims=False)
    both = kept.astype(F32) + swap(sent, "co").astype(F32)
    rounded = both.astype(BF16)
    text_sum = both[0]
    for k in range(1, TEXT_Z):
        text_sum = text_sum + lax.ppermute(rounded[k], "z", turn(TEXT_Z - k)).astype(F32)
    text_sum = text_sum + lax.ppermute(
        text_sum.astype(BF16), "z", [(b, a) for a, b in mirror]
    ).astype(F32)
    text_sum = text_sum.astype(BF16)
    text_low, text_high = text_sum[:, :width], text_sum[:, width:]
    same = jnp.where(yh == 0, text_low, text_high)
    cross = jnp.where(yh == 0, text_high, text_low)

    def back(pairs):
        return [(b, a) for a, b in pairs]

    back_across = lax.ppermute(cross, ys, back(across))
    back_straight = lax.ppermute(same, ys, back(straight))
    back_diagonal = lax.ppermute(cross, ys, back(diagonal))
    text_rows = jnp.where(
        yh == 0,
        jnp.concatenate([back_straight, back_diagonal, same, back_across], axis=0),
        jnp.concatenate([back_diagonal, back_straight, back_across, same], axis=0),
    )
    text_back = lax.all_to_all(text_rows, "co", split_axis=1, concat_axis=0, tiled=True)
    text_du = jnp.where(is_text, text_back.astype(F32) / text_norm, 0.0).astype(BF16)

    transposed = (((0,), (0,)), ((), ()))
    weight_part = jnp.concatenate(
        [
            lax.dot_general(image_hidden, image_du, transposed, preferred_element_type=F32),
            lax.dot_general(text_hidden, text_du, transposed, preferred_element_type=F32),
        ],
        axis=0,
    )
    total_rows, cols = weight_part.shape
    share = total_rows // 64
    loss_parts = part_sums[:3, 0]

    def small_rows(values, lead):
        parts = jnp.stack(split3(values), axis=0)
        parts = jnp.pad(parts, ((0, 1), (0, cols - values.shape[0])))
        return jnp.broadcast_to(parts, (*lead, 4, cols))

    def join(rows):
        return rows[0] + rows[1] + rows[2]

    sent = jnp.concatenate(
        [weight_part.astype(BF16).reshape(4, 16, share, cols), small_rows(loss_parts, (4, 16))],
        axis=2,
    )
    reduced = jnp.sum(exchange(sent, "x").astype(F32), axis=0)
    loss_parts = join(reduced[0, share:])[:3]
    sent = jnp.concatenate(
        [reduced[:, :share].astype(BF16), small_rows(loss_parts, (16,))], axis=1
    )
    reduced = jnp.sum(exchange(sent, ("yl", "z")).astype(F32), axis=0)
    loss_parts = join(reduced[share:])[:3]
    weight_sum = reduced[:share]
    own = (x * 16 + yl * Z + z) * share
    own_weight = lax.dynamic_slice_in_dim(
        jnp.concatenate([img_weight, txt_weight], axis=0), own, share, 0
    )
    own_gain = lax.dynamic_slice_in_dim(jnp.concatenate([img_gain, txt_gain]), own, share, 0)
    gain_sum = jnp.sum(weight_sum * own_weight.astype(F32), axis=1) / own_gain
    small = jnp.concatenate([gain_sum, loss_parts])
    small = small + swap(small, "co")
    small = small + swap(small, "yh")
    gain_sum, loss_parts = small[:share], small[share:]
    ready = jnp.concatenate([weight_sum.astype(BF16), small_rows(gain_sum, ())], axis=0)
    gathered = exchange(jnp.broadcast_to(ready, (16, *ready.shape)), ("yl", "z"))
    gathered = exchange(jnp.broadcast_to(gathered, (4, *gathered.shape)), "x").astype(F32)
    weight_grad = gathered[:, :, :share].reshape(total_rows, cols)
    gain_grad = jnp.sum(gathered[:, :, share:, :share], axis=2).reshape(total_rows)
    split = img_weight.shape[0]
    return (
        loss_parts[0:1] / pair_count,
        weight_grad[:split],
        weight_grad[split:],
        gain_grad[:split],
        gain_grad[split:],
        loss_parts[1:2] * logit_scale,
        loss_parts[2:3],
    )


def solution(mesh):
    inner = Mesh(mesh.devices.reshape(2, Z, 4, 2, 2), ("yl", "z", "x", "yh", "co"))
    tensor = ("yh", "co")
    return jax.shard_map(
        local,
        mesh=inner,
        in_specs=(
            P(DP, None),
            P(DP, None),
            P(),
            P(),
            P(None, tensor),
            P(None, tensor),
            P(),
            P(),
            P(),
        ),
        out_specs=(P(), P(None, tensor), P(None, tensor), P(), P(), P(), P()),
        check_vma=False,
    )
```

time: 1490 us -> 397 us (0.27)
  waiting for transfers between devices: 1200 us -> 213 us
  blocking collectives: 125 us -> 58.8 us
  matrix products: 60.9 us -> 4.67 us
  starting transfers between devices: 22.1 us -> 54.4 us
    psum x1 -> x0, waiting for transfers between devices: 520 us -> none  [local(): lax.psum((img_weight_grad, txt_weight_grad), 'dp')]
    reduce_scatter x1 -> x0, waiting for transfers between devices: 334 us -> none  [local(): lax.psum_scatter(grad_cols, 'dp', scatter_dimension=0, tiled=True)]
    all_gather x2, waiting for transfers between devices: 315 us -> 92.1 us  [the longest x1 85 us: local(): lax.all_gather(image_half, ('yl', 'x', 'yh'), axis=0, tiled=False)]
    psum x2 -> x0, blocking collectives: 88 us -> none  [the longest x1 78 us: local(): lax.psum((loss_sum, scale_sum * logit_scale, bias_sum, img_gain_part, txt...]
    ppermute x0 -> x19, waiting for transfers between devices: none -> 62.4 us  [the longest x3 15.6 us: local(): lax.ppermute(chunk, 'z', turn(k))]
    dot_general x18 -> x4, matrix products: 60.9 us -> 4.67 us  [the longest x1 2.83 us: local(): lax.dot_general(text_hidden, text_du, transposed, preferred_element_type=...]
    all_to_all x3, waiting for transfers between devices: 5.9 us -> 58.9 us  [exchange(): return lax.all_to_all(value, axes, split_axis=0, concat_axis=0, tiled=True)]
    ppermute x0 -> x19, starting transfers between devices: none -> 31.5 us  [the longest x3 7.21 us: local(): lax.ppermute(chunk, 'z', turn(k))]
  transfers between devices with their start and end apart: 8 -> 24, of which waited for: 6 -> 20; matrix products, arithmetic and copies ran while one was open for 2% -> 1% of each run, Pallas kernels for 0% -> 0%
where the time goes in v1:
time: 397 us; the launch traced here: 395 us
  waiting for transfers between devices  213 us (54%)
  blocking collectives  58.8 us (15%)
  starting transfers between devices  54.4 us (14%)
  local copies, waits for them, and re-layouts  22.2 us (6%)
  between operations  19.6 us (5%)
  Pallas kernels  12.8 us (3%)
  other arithmetic  9.43 us (2%)
  matrix products  4.67 us (1%)
    all_gather x1, waiting for transfers between devices, local(): lax.all_gather(image_half, ('yl', 'x', 'yh'), axis=0, tiled=False)  85 us
    all_to_all x3, waiting for transfers between devices, exchange(): return lax.all_to_all(value, axes, split_axis=0, concat_axis=0, tiled=True)  58.9 us
    all_to_all x2, blocking collectives, exchange(): return lax.all_to_all(value, axes, split_axis=0, concat_axis=0, tiled=True)  42.9 us
    all_to_all x3, starting transfers between devices, exchange(): return lax.all_to_all(value, axes, split_axis=0, concat_axis=0, tiled=True)  22.8 us
    ppermute x3, waiting for transfers between devices, local(): lax.ppermute(chunk, 'z', turn(k))  15.6 us
    ppermute x3, waiting for transfers between devices, local(): lax.ppermute(rounded[k], 'z', turn(TEXT_Z - k)).astype(F32)  14.1 us
    pallas_call x1, Pallas kernels, tile_grads(): pl.pallas_call(tile_kernel, grid=(STEPS,), in_specs=[pl.BlockSpec(memory_...  12.8 us
    ppermute x1, waiting for transfers between devices, local(): got_mirror = lax.ppermute(chunk, 'z', mirror)  10.3 us
  transfers between devices with their start and end apart: 24, of which 20 were waited for; matrix products, arithmetic and copies ran while one was open for 1% of the time, Pallas kernels for 0%

profile of v1, /device:TPU:32, one launch (start us, length us, event | category | flops | bytes accessed | tf_op | source)
XLA Modules:
  0.0 395.4 jit_solution(10078748100057865737)
XLA Ops:
  15.8 3.2 collective-permute-start.1
  21.1 4.0 %all_to_all.83 = bf16[2,384,256]{2,1,0:T(8,128)(2,1)S(1)} all-to-all(bf16[2,384,256]{2,1,0:T(8,128)(2,1)S(1)} %bitcast.114), channel_id=1, replica_groups=mesh['yl'=2,'z'=8,'x'=4,'yh'=2,'co'=2] {'co'}, dimensions={0} | all-to-all | bytes 786432 | tf_op jit(solution)/shard_map/all_to_all | solution.py:170
  29.1 3.4 collective-permute-done.2
  32.6 3.0 collective-permute-done.4
  37.0 10.3 %collective-permute-done.5 = bf16[96,1024]{1,0:T(8,128)(2,1)S(1)} collective-permute-done((bf16[96,1024]{1,0:T(8,128)(2,1)S(1)}, bf16[96,1024]{1,0:T(8,128)(2,1)S(1)}, u32[]{:S(2)}, u32[]{:S(2)}) %collective-permute-start.5) | collective-permute-done | bytes 196640 | tf_op jit(solution)/shard_map/ppermute | solution.py:195
  48.9 5.1 %collective-permute-start.7 = (bf16[96,1024]{1,0:T(8,128)(2,1)S(1)}, bf16[96,1024]{1,0:T(8,128)(2,1)S(1)}, u32[]{:S(2)}, u32[]{:S(2)}) collective-permute-start(bf16[96,1024]{1,0:T(8,128)(2,1)S(1)} %broadcast_select_fusion), channel_id=1, source_target_pairs={{48,16},{32,0},{16,48},{0,32},{64,96},{80,112},{96,64},{112,80},{4... | collective-permute-start | bytes 589832 | tf_op jit(solution)/shard_map/ppermute | solution.py:197
  54.6 2.9 collective-permute-done.8
  57.4 8.6 %collective-permute-done.7 = bf16[96,1024]{1,0:T(8,128)(2,1)S(1)} collective-permute-done((bf16[96,1024]{1,0:T(8,128)(2,1)S(1)}, bf16[96,1024]{1,0:T(8,128)(2,1)S(1)}, u32[]{:S(2)}, u32[]{:S(2)}) %collective-permute-start.7) | collective-permute-done | bytes 196640 | tf_op jit(solution)/shard_map/ppermute | solution.py:197
  66.0 4.2 %collective-permute-done.6 = bf16[96,1024]{1,0:T(8,128)(2,1)S(1)} collective-permute-done((bf16[96,1024]{1,0:T(8,128)(2,1)S(1)}, bf16[96,1024]{1,0:T(8,128)(2,1)S(1)}, u32[]{:S(2)}, u32[]{:S(2)}) %collective-permute-start.6) | collective-permute-done | bytes 196640 | tf_op jit(solution)/shard_map/ppermute | solution.py:197
  71.4 3.8 all_to_all.84
  78.2 7.1 %all-gather.6.cloned.1.call-done = bf16[8,96,1024]{2,1,0:T(8,128)(2,1)} async-done(((bf16[4,96,1024]{2,1,0:T(8,128)(2,1)}), bf16[8,96,1024]{2,1,0:T(8,128)(2,1)}) %all-gather.6.cloned.1.call-update) | async-done | bytes 1572880 | tf_op jit(solution)/shard_map/all_gather | solution.py:198
  85.2 85.0 %all-gather.4.cloned.1.call-done.emb_i = bf16[16,128,512]{2,1,0:T(8,128)(2,1)} async-done(((bf16[1,128,512]{2,1,0:T(8,128)(2,1)}), bf16[16,128,512]{2,1,0:T(8,128)(2,1)}) %all-gather.4.cloned.1.call-update) | async-done | bytes 2097168 | tf_op jit(solution)/shard_map/all_gather | solution.py:167
  173.3 12.8 %shard_map.144 = (bf16[16,128,512]{2,1,0:T(8,128)(2,1)}, bf16[768,1024]{1,0:T(8,128)(2,1)S(1)}, f32[8,128]{1,0:T(8,128)S(1)}) custom-call(f32[2]{0:T(128)S(1)} %pad_maximum_fusion.6.factors, s32[4]{0:T(128)S(1)} %concatenate.53.valid, s32[1024,1]{1,0:T(8,128)S(1)} %copy.63.partner, s32[1,768]{1,0:T(1,128)S(1)} %add.237.columns, ...), custom_call_target="tpu_custom_call" | custom-call | tf_op jit(solution)/shard_map/pallas_call | solution.py:104
  193.7 10.7 %collective-permute-done.10 = bf16[96,1024]{1,0:T(8,128)(2,1)S(1)} collective-permute-done((bf16[96,1024]{1,0:T(8,128)(2,1)S(1)}, bf16[96,1024]{1,0:T(8,128)(2,1)S(1)}, u32[]{:S(2)}, u32[]{:S(2)}) %collective-permute-start.10) | collective-permute-done | bytes 196640 | tf_op jit(solution)/shard_map/ppermute | solution.py:245
  204.5 3.4 collective-permute-done.11
  209.3 3.9 collective-permute-done.13
  213.4 2.7 collective-permute-start.14
  216.7 5.2 %collective-permute-start.15 = (bf16[96,512]{1,0:T(8,128)(2,1)S(1)}, bf16[96,512]{1,0:T(8,128)(2,1)S(1)}, u32[]{:S(2)}, u32[]{:S(2)}) collective-permute-start(bf16[96,512]{1,0:T(8,128)(2,1)S(1)} %get-tuple-element.31), channel_id=1, source_target_pairs={{2,128},{0,130},{3,129},{1,131},{6,132},{4,134},{7,133},{5,135},{1... | collective-permute-start | bytes 294920 | tf_op jit(solution)/shard_map/ppermute | solution.py:259
  224.2 4.0 %all_to_all.85 = bf16[384,2,256]{2,0,1:T(8,128)(2,1)S(1)} all-to-all(bf16[384,2,256]{2,0,1:T(8,128)(2,1)S(1)} %maximum_select_fusion), channel_id=1, replica_groups=mesh['yl'=2,'z'=8,'x'=4,'yh'=2,'co'=2] {'co'}, dimensions={1} | all-to-all | bytes 786432 | tf_op jit(solution)/shard_map/all_to_all | solution.py:265
  228.3 6.5 %all-to-all-start.2 = ((bf16[16,128,512]{2,1,0:T(8,128)(2,1)}), bf16[16,128,512]{2,1,0:T(8,128)(2,1)S(1)}, u32[]{:S(2)}, u32[]{:S(2)}) async-start(bf16[16,128,512]{2,1,0:T(8,128)(2,1)} %get-tuple-element.10), calls=%async_computation.2 | async-start | bytes 4194304 | tf_op jit(solution)/shard_map/all_to_all | solution.py:30
  235.2 2.8 convolution_convert_fusion.1
  238.0 29.2 %all-to-all-done.2 = bf16[16,128,512]{2,1,0:T(8,128)(2,1)S(1)} async-done(((bf16[16,128,512]{2,1,0:T(8,128)(2,1)}), bf16[16,128,512]{2,1,0:T(8,128)(2,1)S(1)}, u32[]{:S(2)}, u32[]{:S(2)}) %all-to-all-start.2) | async-done | bytes 2097184 | tf_op jit(solution)/shard_map/all_to_all | solution.py:30
  267.8 4.0 %all_to_all.86 = bf16[128,2,256]{0,2,1:T(8,128)(2,1)S(1)} all-to-all(bf16[128,2,256]{0,2,1:T(8,128)(2,1)S(1)} %divide_convert_fusion.1), channel_id=1, replica_groups=mesh['yl'=2,'z'=8,'x'=4,'yh'=2,'co'=2] {'co'}, dimensions={1} | all-to-all | bytes 262144 | tf_op jit(solution)/shard_map/all_to_all | solution.py:234
  273.2 26.6 %all_to_all.87 = bf16[4,16,48,256]{3,2,1,0:T(8,128)(2,1)S(1)} all-to-all(bf16[4,16,48,256]{3,2,1,0:T(8,128)(2,1)S(1)} %pad_maximum_fusion), channel_id=1, replica_groups=mesh['yl'=2,'z'=8,'x'=4,'yh'=2,'co'=2] {'x'}, dimensions={0} | all-to-all | bytes 3145728 | tf_op jit(solution)/shard_map/all_to_all | solution.py:30
  301.0 12.7 %all-to-all-start.6 = ((bf16[16,48,256]{2,1,0:T(8,128)(2,1)}), bf16[16,48,256]{2,1,0:T(8,128)(2,1)S(1)}, u32[]{:S(2)}, u32[]{:S(2)}) async-start(bf16[16,48,256]{2,1,0:T(8,128)(2,1)} %pad_maximum_fusion.3), calls=%async_computation.6 | async-start | bytes 786432 | tf_op jit(solution)/shard_map/all_to_all | solution.py:30
  313.7 11.5 %all-to-all-done.6 = bf16[16,48,256]{2,1,0:T(8,128)(2,1)S(1)} async-done(((bf16[16,48,256]{2,1,0:T(8,128)(2,1)}), bf16[16,48,256]{2,1,0:T(8,128)(2,1)S(1)}, u32[]{:S(2)}, u32[]{:S(2)}) %all-to-all-start.6) | async-done | bytes 393248 | tf_op jit(solution)/shard_map/all_to_all | solution.py:30
  328.6 3.4 collective-permute-done.18
  332.0 16.3 %all_to_all.88 = bf16[16,48,256]{2,1,0:T(8,128)(2,1)S(1)} all-to-all(bf16[16,48,256]{2,1,0:T(8,128)(2,1)S(1)} %broadcast_in_dim.15), channel_id=1, replica_groups=mesh['yl'=2,'z'=8,'x'=4,'yh'=2,'co'=2] {'yl','z'}, dimensions={0} | all-to-all | bytes 786432 | tf_op jit(solution)/shard_map/all_to_all | solution.py:30
  349.5 3.6 all-to-all-start.8
  355.0 18.2 %all-to-all-done.8 = bf16[4,16,48,256]{3,2,1,0:T(8,128)(2,1)S(1)} async-done(((bf16[4,16,48,256]{3,2,1,0:T(8,128)(2,1)}), bf16[4,16,48,256]{3,2,1,0:T(8,128)(2,1)S(1)}, u32[]{:S(2)}, u32[]{:S(2)}) %all-to-all-start.8) | async-done | bytes 1572896 | tf_op jit(solution)/shard_map/all_to_all | solution.py:30
  375.2 4.1 %reshape.263 = f32[2816,256]{1,0:T(8,128)} reshape(f32[4,16,44,256]{3,2,1,0:T(8,128)} %slice.162) | data formatting | bytes 5767168 | tf_op jit(solution)/shard_map/reshape | solution.py:313
  381.6 2.8 slice.163
  (145 shorter events, 50.5 us)
Async XLA Ops:
  7.2 3.7 copy-start.2
  7.2 3.7 copy-start.11
  7.2 78.1 %all-gather.6.cloned.1.call-start = ((), (), s32[]{:S(2)}) async-start(), calls=%async_computation.10 | async-start | bytes 2359296 | tf_op jit(solution)/shard_map/all_gather | solution.py:198
  11.9 2.6 copy-start.3
  11.9 2.0 copy-start.12
  14.5 1.3 collective-permute-start
  15.8 5.1 %collective-permute-start.1 = (f32[1024]{0:T(1024)S(1)}, f32[1024]{0:T(1024)S(1)}, u32[]{:S(2)}, u32[]{:S(2)}) collective-permute-start(f32[1024]{0:T(1024)S(1)} %fusion.65), channel_id=1, source_target_pairs={{0,2},{2,0},{1,3},{3,1},{4,6},{6,4},{5,7},{7,5},{8,10},{10,8},{9,1... | collective-permute-start | bytes 12296 | tf_op jit(solution)/shard_map/ppermute | solution.py:26
  25.9 6.7 %collective-permute-start.2 = (bf16[96,512]{1,0:T(8,128)(2,1)S(1)}, bf16[96,512]{1,0:T(8,128)(2,1)S(1)}, u32[]{:S(2)}, u32[]{:S(2)}) collective-permute-start(bf16[96,512]{1,0:T(8,128)(2,1)S(1)} %get-tuple-element.27), channel_id=1, source_target_pairs={{128,0},{130,2},{129,1},{131,3},{132,4},{134,6},{133,5},{135,7},{1... | collective-permute-start | bytes 294920 | tf_op jit(solution)/shard_map/ppermute | solution.py:185
  27.2 8.5 %collective-permute-start.4 = (bf16[96,512]{1,0:T(8,128)(2,1)S(1)}, bf16[96,512]{1,0:T(8,128)(2,1)S(1)}, u32[]{:S(2)}, u32[]{:S(2)}) collective-permute-start(bf16[96,512]{1,0:T(8,128)(2,1)S(1)} %get-tuple-element.28), channel_id=1, source_target_pairs={{128,2},{130,0},{129,3},{131,1},{132,6},{134,4},{133,7},{135,5},{1... | collective-permute-start | bytes 294920 | tf_op jit(solution)/shard_map/ppermute | solution.py:186
  28.5 7.2 %collective-permute-start.3 = (bf16[96,512]{1,0:T(8,128)(2,1)S(1)}, bf16[96,512]{1,0:T(8,128)(2,1)S(1)}, u32[]{:S(2)}, u32[]{:S(2)}) collective-permute-start(bf16[96,512]{1,0:T(8,128)(2,1)S(1)} %get-tuple-element.29), channel_id=1, source_target_pairs={{128,130},{130,128},{129,131},{131,129},{132,134},{134,132},{133,1... | collective-permute-start | bytes 294920 | tf_op jit(solution)/shard_map/ppermute | solution.py:184
  35.7 11.6 %collective-permute-start.5 = (bf16[96,1024]{1,0:T(8,128)(2,1)S(1)}, bf16[96,1024]{1,0:T(8,128)(2,1)S(1)}, u32[]{:S(2)}, u32[]{:S(2)}) collective-permute-start(bf16[96,1024]{1,0:T(8,128)(2,1)S(1)} %maximum_select_fusion.1), channel_id=1, source_target_pairs={{64,48},{80,32},{96,16},{112,0},{65,49},{81,33},{97,17},{113,1},{6... | collective-permute-start | bytes 589832 | tf_op jit(solution)/shard_map/ppermute | solution.py:195
  47.3 10.1 %collective-permute-start.8 = (bf16[96,1024]{1,0:T(8,128)(2,1)S(1)}, bf16[96,1024]{1,0:T(8,128)(2,1)S(1)}, u32[]{:S(2)}, u32[]{:S(2)}) collective-permute-start(bf16[96,1024]{1,0:T(8,128)(2,1)S(1)} %broadcast_select_fusion), channel_id=1, source_target_pairs={{48,0},{32,48},{16,32},{0,16},{64,112},{80,64},{96,80},{112,96},{4... | collective-permute-start | bytes 589832 | tf_op jit(solution)/shard_map/ppermute | solution.py:197
  48.9 17.1 %collective-permute-start.7 = (bf16[96,1024]{1,0:T(8,128)(2,1)S(1)}, bf16[96,1024]{1,0:T(8,128)(2,1)S(1)}, u32[]{:S(2)}, u32[]{:S(2)}) collective-permute-start(bf16[96,1024]{1,0:T(8,128)(2,1)S(1)} %broadcast_select_fusion), channel_id=1, source_target_pairs={{48,16},{32,0},{16,48},{0,32},{64,96},{80,112},{96,64},{112,80},{4... | collective-permute-start | bytes 589832 | tf_op jit(solution)/shard_map/ppermute | solution.py:197
  54.0 16.2 %collective-permute-start.6 = (bf16[96,1024]{1,0:T(8,128)(2,1)S(1)}, bf16[96,1024]{1,0:T(8,128)(2,1)S(1)}, u32[]{:S(2)}, u32[]{:S(2)}) collective-permute-start(bf16[96,1024]{1,0:T(8,128)(2,1)S(1)} %broadcast_select_fusion), channel_id=1, source_target_pairs={{48,32},{32,16},{16,0},{0,48},{64,80},{80,96},{96,112},{112,64},{4... | collective-permute-start | bytes 589832 | tf_op jit(solution)/shard_map/ppermute | solution.py:197
  70.2 7.6 %copy-start.10 = (s32[12288]{0:T(1024)S(1)}, s32[12288]{0:T(1024)}, u32[]{:S(2)}) copy-start(s32[12288]{0:T(1024)} %param.17) | copy-start | bytes 147460
  71.2 99.1 %all-gather.4.cloned.1.call-start = ((), (), s32[]{:S(2)}) async-start(), calls=%async_computation.9 | async-start | bytes 2228224 | tf_op jit(solution)/shard_map/all_gather | solution.py:167
  186.2 2.6 collective-permute-start.9
  189.1 15.4 %collective-permute-start.10 = (bf16[96,1024]{1,0:T(8,128)(2,1)S(1)}, bf16[96,1024]{1,0:T(8,128)(2,1)S(1)}, u32[]{:S(2)}, u32[]{:S(2)}) collective-permute-start(bf16[96,1024]{1,0:T(8,128)(2,1)S(1)} %get-tuple-element.24), channel_id=1, source_target_pairs={{48,0},{32,48},{16,32},{0,16},{64,112},{80,64},{96,80},{112,96},{4... | collective-permute-start | bytes 589832 | tf_op jit(solution)/shard_map/ppermute | solution.py:245
  190.8 13.7 %collective-permute-start.12 = (bf16[96,1024]{1,0:T(8,128)(2,1)S(1)}, bf16[96,1024]{1,0:T(8,128)(2,1)S(1)}, u32[]{:S(2)}, u32[]{:S(2)}) collective-permute-start(bf16[96,1024]{1,0:T(8,128)(2,1)S(1)} %get-tuple-element.25), channel_id=1, source_target_pairs={{48,32},{32,16},{16,0},{0,48},{64,80},{80,96},{96,112},{112,64},{4... | collective-permute-start | bytes 589832 | tf_op jit(solution)/shard_map/ppermute | solution.py:245
  191.2 16.7 %collective-permute-start.11 = (bf16[96,1024]{1,0:T(8,128)(2,1)S(1)}, bf16[96,1024]{1,0:T(8,128)(2,1)S(1)}, u32[]{:S(2)}, u32[]{:S(2)}) collective-permute-start(bf16[96,1024]{1,0:T(8,128)(2,1)S(1)} %get-tuple-element.26), channel_id=1, source_target_pairs={{48,16},{32,0},{16,48},{0,32},{64,96},{80,112},{96,64},{112,80},{4... | collective-permute-start | bytes 589832 | tf_op jit(solution)/shard_map/ppermute | solution.py:245
  208.0 5.2 %collective-permute-start.13 = (bf16[96,1024]{1,0:T(8,128)(2,1)S(1)}, bf16[96,1024]{1,0:T(8,128)(2,1)S(1)}, u32[]{:S(2)}, u32[]{:S(2)}) collective-permute-start(bf16[96,1024]{1,0:T(8,128)(2,1)S(1)} %fusion.14), channel_id=1, source_target_pairs={{48,64},{32,80},{16,96},{0,112},{49,65},{33,81},{17,97},{1,113},{5... | collective-permute-start | bytes 589832 | tf_op jit(solution)/shard_map/ppermute | solution.py:246
  213.4 8.6 %collective-permute-start.14 = (bf16[96,512]{1,0:T(8,128)(2,1)S(1)}, bf16[96,512]{1,0:T(8,128)(2,1)S(1)}, u32[]{:S(2)}, u32[]{:S(2)}) collective-permute-start(bf16[96,512]{1,0:T(8,128)(2,1)S(1)} %get-tuple-element.30), channel_id=1, source_target_pairs={{0,128},{2,130},{1,129},{3,131},{4,132},{6,134},{5,133},{7,135},{8... | collective-permute-start | bytes 294920 | tf_op jit(solution)/shard_map/ppermute | solution.py:258
  216.1 5.9 %collective-permute-start.16 = (bf16[96,512]{1,0:T(8,128)(2,1)S(1)}, bf16[96,512]{1,0:T(8,128)(2,1)S(1)}, u32[]{:S(2)}, u32[]{:S(2)}) collective-permute-start(bf16[96,512]{1,0:T(8,128)(2,1)S(1)} %get-tuple-element.31), channel_id=1, source_target_pairs={{130,128},{128,130},{131,129},{129,131},{134,132},{132,134},{135,1... | collective-permute-start | bytes 294920 | tf_op jit(solution)/shard_map/ppermute | solution.py:257
  216.7 7.4 %collective-permute-start.15 = (bf16[96,512]{1,0:T(8,128)(2,1)S(1)}, bf16[96,512]{1,0:T(8,128)(2,1)S(1)}, u32[]{:S(2)}, u32[]{:S(2)}) collective-permute-start(bf16[96,512]{1,0:T(8,128)(2,1)S(1)} %get-tuple-element.31), channel_id=1, source_target_pairs={{2,128},{0,130},{3,129},{1,131},{6,132},{4,134},{7,133},{5,135},{1... | collective-permute-start | bytes 294920 | tf_op jit(solution)/shard_map/ppermute | solution.py:259
  228.3 39.0 %all-to-all-start.2 = ((bf16[16,128,512]{2,1,0:T(8,128)(2,1)}), bf16[16,128,512]{2,1,0:T(8,128)(2,1)S(1)}, u32[]{:S(2)}, u32[]{:S(2)}) async-start(bf16[16,128,512]{2,1,0:T(8,128)(2,1)} %get-tuple-element.10), calls=%async_computation.2 | async-start | bytes 4194304 | tf_op jit(solution)/shard_map/all_to_all | solution.py:30
  267.8 4.7 %copy-start.9 = (bf16[1024,256]{1,0:T(8,128)(2,1)S(1)}, bf16[1024,256]{1,0:T(8,128)(2,1)}, u32[]{:S(2)}) copy-start(bf16[1024,256]{1,0:T(8,128)(2,1)} %convolution_convert_fusion.1) | copy-start | bytes 1572868
  300.0 25.3 %copy-start.6 = (bf16[1792,256]{1,0:T(8,128)(2,1)S(1)}, bf16[1792,256]{1,0:T(8,128)(2,1)}, u32[]{:S(2)}) copy-start(bf16[1792,256]{1,0:T(8,128)(2,1)} %param.13) | copy-start | bytes 2752516
  300.0 25.3 %copy-start.8 = (bf16[1024,256]{1,0:T(8,128)(2,1)S(1)}, bf16[1024,256]{1,0:T(8,128)(2,1)}, u32[]{:S(2)}) copy-start(bf16[1024,256]{1,0:T(8,128)(2,1)} %param.14) | copy-start | bytes 1572868
  301.0 24.2 %all-to-all-start.6 = ((bf16[16,48,256]{2,1,0:T(8,128)(2,1)}), bf16[16,48,256]{2,1,0:T(8,128)(2,1)S(1)}, u32[]{:S(2)}, u32[]{:S(2)}) async-start(bf16[16,48,256]{2,1,0:T(8,128)(2,1)} %pad_maximum_fusion.3), calls=%async_computation.6 | async-start | bytes 786432 | tf_op jit(solution)/shard_map/all_to_all | solution.py:30
  325.6 1.1 collective-permute-start.17
  326.9 5.1 %collective-permute-start.18 = (f32[47]{0:T(128)S(1)}, f32[47]{0:T(128)S(1)}, u32[]{:S(2)}, u32[]{:S(2)}) collective-permute-start(f32[47]{0:T(128)S(1)} %fusion.64), channel_id=1, source_target_pairs={{0,2},{2,0},{1,3},{3,1},{4,6},{6,4},{5,7},{7,5},{8,10},{10,8},{9,1... | collective-permute-start | bytes 572 | tf_op jit(solution)/shard_map/ppermute | solution.py:26
  349.5 23.6 %all-to-all-start.8 = ((bf16[4,16,48,256]{3,2,1,0:T(8,128)(2,1)}), bf16[4,16,48,256]{3,2,1,0:T(8,128)(2,1)S(1)}, u32[]{:S(2)}, u32[]{:S(2)}) async-start(bf16[4,16,48,256]{3,2,1,0:T(8,128)(2,1)} %broadcast_in_dim.16), calls=%async_computation.8 | async-start | bytes 3145728 | tf_op jit(solution)/shard_map/all_to_all | solution.py:30
  (5 other events, 7.8 us)
Sparse Core Ops, SparseCore 0:
  71.3 13.8 all-gather.5
  87.0 83.1 all-gather.3

commit v2 on v1

v2 whole, which is shorter than its diff:
```python
import jax
import jax.numpy as jnp
from jax import lax
from jax.experimental import pallas as pl
from jax.experimental.pallas import tpu as pltpu
from jax.sharding import Mesh, PartitionSpec as P

EPS = 1e-06
F32 = jnp.float32
BF16 = jnp.bfloat16
Z = 8
TEXT_Z = 4
DP = ("yl", "z", "x")
STEPS = 4


def hidden_rows(features, gain_vec):
    values = features.astype(F32)
    center = jnp.mean(values, axis=1, keepdims=True)
    spread = jnp.mean(values * values, axis=1, keepdims=True) - center * center
    scaled = (values - center) * lax.rsqrt(spread + EPS)
    return (scaled * gain_vec).astype(BF16)


def swap(value, axis):
    return lax.ppermute(value, axis, [(0, 1), (1, 0)])


def exchange(value, axes):
    return lax.all_to_all(value, axes, split_axis=0, concat_axis=0, tiled=True)


def split3(value):
    high = value.astype(BF16)
    rest = value - high.astype(F32)
    middle = rest.astype(BF16)
    return high, middle, (rest - middle.astype(F32)).astype(BF16)


def tile_kernel(
    factors, partner, columns, emb_i, emb_t, out_i, out_t, out_s, acc, sums
):
    step = pl.program_id(0)
    scale, shift = factors[0], factors[1]

    @pl.when(step == 0)
    def _():
        acc[...] = jnp.zeros_like(acc)
        sums[...] = jnp.zeros_like(sums)

    rows = jnp.concatenate(
        [
            jnp.concatenate([emb_i[0], emb_i[1]], axis=1),
            jnp.concatenate([emb_i[2], emb_i[3]], axis=1),
        ],
        axis=0,
    )
    texts = emb_t[...]
    high = emb_i.shape[1]
    half = emb_i.shape[2]
    place = lax.broadcasted_iota(jnp.int32, (2 * high, 1), 0)
    weight = jnp.where(place < high, factors[2], factors[3])
    similar = lax.dot_general(rows, texts, (((1,), (1,)), ((), ())), preferred_element_type=F32)
    logits = scale * similar + shift
    pair = partner[...] == columns[...]
    signed = jnp.where(pair, -logits, logits)
    small = jnp.exp(-jnp.abs(signed))
    total = 1.0 + small
    inverse = 1.0 / total
    sigmoid = jnp.where(signed >= 0, inverse, small * inverse)
    soft = jnp.maximum(signed, 0.0) + jnp.log(total) + (small - (total - 1.0)) * inverse
    grad = jnp.where(pair, -sigmoid, sigmoid) * weight
    sums[0:1] += jnp.sum(soft * weight, axis=0, keepdims=True)
    sums[1:2] += jnp.sum(grad * similar, axis=0, keepdims=True)
    sums[2:3] += jnp.sum(grad, axis=0, keepdims=True)
    rounded = grad.astype(BF16)
    acc[...] += lax.dot_general(rounded, rows, (((0,), (0,)), ((), ())), preferred_element_type=F32)
    grad_rows = jnp.dot(rounded, texts, preferred_element_type=F32)
    wide = rows.astype(F32)
    inner = jnp.sum(wide * grad_rows, axis=1, keepdims=True)
    result = (scale * (grad_rows - wide * inner)).astype(BF16)
    out_i[0] = result[:high, :half]
    out_i[1] = result[:high, half:]
    out_i[2] = result[high:, :half]
    out_i[3] = result[high:, half:]

    @pl.when(step == STEPS - 1)
    def _():
        texts = emb_t[...].astype(F32)
        grads = acc[...]
        inner = jnp.sum(texts * grads, axis=1, keepdims=True)
        out_t[...] = (scale * (grads - texts * inner)).astype(BF16)
        out_s[...] = jnp.broadcast_to(jnp.sum(sums[...], axis=1, keepdims=True), out_s.shape)


def tile_grads(factors, partner, columns, emb_i, emb_t):
    slabs, high, half = emb_i.shape
    block = slabs // STEPS
    count, width = emb_t.shape
    return pl.pallas_call(
        tile_kernel,
        grid=(STEPS,),
        in_specs=[
            pl.BlockSpec(memory_space=pltpu.SMEM),
            pl.BlockSpec((partner.shape[0] // STEPS, 1), lambda i: (i, 0)),
            pl.BlockSpec((1, count), lambda i: (0, 0)),
            pl.BlockSpec((block, high, half), lambda i: (i, 0, 0)),
            pl.BlockSpec((count, width), lambda i: (0, 0)),
        ],
        out_specs=[
            pl.BlockSpec((block, high, half), lambda i: (i, 0, 0)),
            pl.BlockSpec((count, width), lambda i: (0, 0)),
            pl.BlockSpec((8, 128), lambda i: (0, 0)),
        ],
        out_shape=[
            jax.ShapeDtypeStruct(emb_i.shape, BF16),
            jax.ShapeDtypeStruct(emb_t.shape, BF16),
            jax.ShapeDtypeStruct((8, 128), F32),
        ],
        scratch_shapes=[pltpu.VMEM((count, width), F32), pltpu.VMEM((8, count), F32)],
        compiler_params=pltpu.CompilerParams(vmem_limit_bytes=40 * 1024 * 1024),
    )(factors, partner, columns, emb_i, emb_t)


def half_place(half, j):
    return TEXT_Z + j if half else TEXT_Z - 1 - j


def turn(k):
    return [
        (half_place(half, j), half_place(half, (j + k) % TEXT_Z))
        for half in range(2)
        for j in range(TEXT_Z)
    ]


def finish_kernel(places, first, second, third, fourth, out_i, out_t, out_g, rows):
    image_rows = rows.shape[0] // 16
    text_rows = out_t.shape[0] // 64
    padded = first.shape[1] - text_rows
    for k, piece in enumerate((first, second, third, fourth)):
        place = places[k]
        for s in range(16):
            values = piece[s].astype(F32)
            rows[s * image_rows : (s + 1) * image_rows] = values[:image_rows]
            start = pl.multiple_of(place * (16 * text_rows) + s * text_rows, 8)
            out_t[pl.ds(start, text_rows)] = values[padded:]
            tail = values[image_rows:padded]
            out_g[place, s : s + 1] = tail[0:1] + tail[1:2] + tail[2:3]
        start = pl.multiple_of(place * (16 * image_rows), 8)
        out_i[pl.ds(start, 16 * image_rows)] = rows[...]


def finish(places, pieces, image_total, text_total):
    cols = pieces[0].shape[2]
    whole = pl.BlockSpec(memory_space=pltpu.VMEM)
    return pl.pallas_call(
        finish_kernel,
        in_specs=[pl.BlockSpec(memory_space=pltpu.SMEM)] + [whole] * 4,
        out_specs=[whole] * 3,
        out_shape=[
            jax.ShapeDtypeStruct((image_total, cols), F32),
            jax.ShapeDtypeStruct((text_total, cols), F32),
            jax.ShapeDtypeStruct((4, 16, cols), F32),
        ],
        scratch_shapes=[pltpu.VMEM((image_total // 4, cols), F32)],
        compiler_params=pltpu.CompilerParams(vmem_limit_bytes=24 * 1024 * 1024),
    )(places, *pieces)


def ring(k):
    return [(i, (i + k) % 4) for i in range(4)]


def y_move(value, k):
    return lax.ppermute(value, ("yl", "yh"), [(i, i ^ k) for i in range(4)])


def pick(value, index, axis=0):
    return lax.dynamic_index_in_dim(value, index, axis, keepdims=False)


def local(
    img_feats, txt_feats, img_gain, txt_gain, img_weight, txt_weight, log_scale, bias, pair_perm
):
    yl, z, x = lax.axis_index("yl"), lax.axis_index("z"), lax.axis_index("x")
    yh, core = lax.axis_index("yh"), lax.axis_index("co")
    pair_count = pair_perm.shape[0]
    img_count, txt_count = img_feats.shape[0], txt_feats.shape[0]
    img_half, txt_half = img_count // 2, txt_count // 2
    piece = txt_half // 4
    is_text = (yl == 1) & (z >= TEXT_Z)
    near = jnp.where(z >= TEXT_Z, z - TEXT_Z, TEXT_Z - 1 - z)
    sources = [jnp.mod(x - k + 4, 4) for k in range(4)]
    targets = [jnp.mod(x + k, 4) for k in range(4)]

    text_hidden = hidden_rows(txt_feats, txt_gain)
    image_hidden = hidden_rows(img_feats, img_gain)
    text_proj = jnp.dot(text_hidden, txt_weight, preferred_element_type=F32)
    image_proj = jnp.dot(image_hidden, img_weight, preferred_element_type=F32)
    squares = jnp.concatenate(
        [jnp.sum(text_proj * text_proj, axis=1), jnp.sum(image_proj * image_proj, axis=1)]
    )
    squares = squares + swap(squares, "co")
    squares = squares + swap(squares, "yh")
    norms = jnp.sqrt(squares + EPS)[:, None]
    text_norm, image_norm = norms[:txt_count], norms[txt_count:]
    text_emb = (text_proj / text_norm).astype(BF16)
    image_emb = (image_proj / image_norm).astype(BF16)

    def halves(index):
        return jnp.concatenate(
            [
                lax.dynamic_slice_in_dim(image_emb, index * img_half, img_half, 0),
                lax.dynamic_slice_in_dim(text_emb, index * txt_half, txt_half, 0),
            ],
            axis=0,
        )

    kept = halves(core)
    taken = swap(halves(1 - core), "co")
    both = jnp.where(
        core == 0,
        jnp.concatenate([kept, taken], axis=1),
        jnp.concatenate([taken, kept], axis=1),
    )
    width = both.shape[1]
    image_own = both[:img_half]
    text_own = both[img_half:].reshape(4, piece, width)

    got = []
    for k in range(1, 4):
        target = jnp.bitwise_xor(yl * 2 + yh, k)
        got.append(y_move(jnp.concatenate([image_own, pick(text_own, target)], axis=0), k))
    slabs = jnp.stack([image_own] + [g[:img_half] for g in got])
    mine = jnp.where(yl == 1, pick(text_own, yl * 2 + yh), got[1][img_half:])
    other = jnp.where(yl == 1, got[0][img_half:], got[2][img_half:])
    chunk = jnp.concatenate([mine, other], axis=1)
    mirror = [(a, Z - 1 - a) for a in range(TEXT_Z, Z)]
    chunk = jnp.where(z >= TEXT_Z, chunk, lax.ppermute(chunk, "z", mirror))
    image_all = jnp.concatenate([slabs] + [lax.ppermute(slabs, "x", ring(k)) for k in range(1, 4)])
    chunks = jnp.stack([chunk] + [lax.ppermute(chunk, "z", turn(k)) for k in range(1, TEXT_Z)])
    text_tile = jnp.stack([chunks, swap(chunks, "co")])
    text_tile = text_tile.reshape(2 * TEXT_Z * piece, 2 * width)

    quarter = yl * 2 + yh
    order = jnp.arange(TEXT_Z, dtype=jnp.int32)
    group = jnp.mod(near - order + TEXT_Z, TEXT_Z) * 4 + x
    columns = (
        group[None, :, None] * txt_count
        + jnp.mod(core + jnp.arange(2, dtype=jnp.int32), 2)[:, None, None] * txt_half
        + quarter * piece
        + jnp.arange(piece, dtype=jnp.int32)[None, None, :]
    ).reshape(1, -1)
    padded = jnp.concatenate([pair_perm, jnp.full((16 * img_count,), -1, jnp.int32)])
    padded = pick(pick(padded.reshape(2, Z, 4, 2, img_half), z, 1), core, 2)
    padded = jnp.where(yl == 0, padded, padded[::-1])
    partner = jnp.stack([pick(padded, source, 1) for source in sources]).reshape(-1, 1)
    logit_scale = jnp.exp(log_scale[0])
    weights = [
        jnp.where((side == 1) & (z >= TEXT_Z), 0.0, 1.0).astype(F32) for side in (yl, 1 - yl)
    ]
    factors = jnp.stack([logit_scale, bias[0], *weights])

    share_cols = image_hidden.shape[1] // 4
    parts = jnp.stack(
        [image_hidden[:, i * share_cols : (i + 1) * share_cols] for i in range(4)]
    )
    hidden_x = jnp.concatenate(
        [pick(parts, x)]
        + [lax.ppermute(pick(parts, targets[k]), "x", ring(k)) for k in range(1, 4)]
    )

    image_part, text_part, part_sums = tile_grads(factors, partner, columns, image_all, text_tile)

    image_part = image_part.reshape(4, 4, img_half, width)
    image_sum = image_part[0].astype(F32)
    for k in range(1, 4):
        image_sum = image_sum + lax.ppermute(image_part[k], "x", ring(-k)).astype(F32)

    text_part = text_part.reshape(2, TEXT_Z, piece, 2 * width)
    both = text_part[0].astype(F32) + swap(text_part[1], "co").astype(F32)
    rounded = both.astype(BF16)
    text_sum = both[0]
    for k in range(1, TEXT_Z):
        text_sum = text_sum + lax.ppermute(rounded[k], "z", turn(TEXT_Z - k)).astype(F32)
    text_sum = text_sum + lax.ppermute(
        text_sum.astype(BF16), "z", [(b, a) for a, b in mirror]
    ).astype(F32)
    text_sum = text_sum.astype(BF16)
    same, cross = text_sum[:, :width], text_sum[:, width:]
    image_round = image_sum.astype(BF16)
    got = [
        y_move(jnp.concatenate([image_round[k], cross if k & 1 else same], axis=0), k)
        for k in range(1, 4)
    ]
    image_sum = image_sum[0]
    for g in got:
        image_sum = image_sum + g[:img_half].astype(F32)
    across, straight, diagonal = [g[img_half:] for g in got]
    text_rows = jnp.where(
        yh == 0,
        jnp.concatenate([straight, diagonal, same, across], axis=0),
        jnp.concatenate([diagonal, straight, across, same], axis=0),
    )
    image_rows = image_sum / lax.dynamic_slice_in_dim(image_norm, core * img_half, img_half, 0)
    text_rows = text_rows.astype(F32) / lax.dynamic_slice_in_dim(
        text_norm, core * txt_half, txt_half, 0
    )
    text_rows = jnp.where(is_text, text_rows, 0.0)
    both = jnp.concatenate([image_rows.astype(BF16), text_rows.astype(BF16)], axis=0)
    cols = width // 2
    kept = lax.dynamic_slice_in_dim(both, core * cols, cols, 1)
    taken = swap(lax.dynamic_slice_in_dim(both, (1 - core) * cols, cols, 1), "co")
    first = jnp.where(core == 0, kept, taken)
    second = jnp.where(core == 0, taken, kept)
    image_du = jnp.concatenate([first[:img_half], second[:img_half]], axis=0)
    text_du = jnp.concatenate([first[img_half:], second[img_half:]], axis=0)

    transposed = (((0,), (0,)), ((), ()))
    text_weight = lax.dot_general(text_hidden, text_du, transposed, preferred_element_type=F32)
    text_share = text_weight.shape[0] // 4
    text_weight = text_weight.reshape(4, text_share, cols)
    loss_parts = part_sums[:3, 0]

    def small_rows(values, count):
        rows = jnp.stack(split3(values), axis=0)
        return jnp.pad(rows, ((0, count - 3), (0, cols - values.shape[0])))

    def join(rows):
        return rows[0] + rows[1] + rows[2]

    tail = small_rows(loss_parts, 16)
    got = [
        lax.ppermute(
            jnp.concatenate([image_du, pick(text_weight, targets[k]).astype(BF16), tail], axis=0),
            "x",
            ring(k),
        )
        for k in range(1, 4)
    ]
    du_x = jnp.concatenate([image_du] + [g[:img_count] for g in got], axis=0)
    text_weight = pick(text_weight, x)
    for g in got:
        text_weight = text_weight + g[img_count : img_count + text_share].astype(F32)
        loss_parts = loss_parts + join(g[img_count + text_share :].astype(F32))[:3]
    image_weight = lax.dot_general(hidden_x, du_x, transposed, preferred_element_type=F32)

    img_share, txt_share = share_cols // 16, text_share // 16
    slot = 32
    block = jnp.concatenate(
        [
            image_weight.astype(BF16).reshape(16, img_share, cols),
            jnp.broadcast_to(
                small_rows(loss_parts, slot - img_share), (16, slot - img_share, cols)
            ),
            text_weight.astype(BF16).reshape(16, txt_share, cols),
        ],
        axis=1,
    )
    reduced = jnp.sum(exchange(block, ("yl", "z")).astype(F32), axis=0)
    loss_parts = join(reduced[img_share:slot])[:3]
    place = yl * Z + z
    own_image = x * share_cols + place * img_share
    own_text = x * text_share + place * txt_share

    def own(weight, gain, values, start):
        count = values.shape[0]
        used = lax.dynamic_slice_in_dim(weight, start, count, 0).astype(F32)
        return jnp.sum(values * used, axis=1) / lax.dynamic_slice_in_dim(gain, start, count, 0)

    small = jnp.concatenate(
        [
            own(img_weight, img_gain, reduced[:img_share], own_image),
            own(txt_weight, txt_gain, reduced[slot:], own_text),
            loss_parts,
        ]
    )
    small = small + swap(small, "co")
    small = small + swap(small, "yh")
    gains, loss_parts = small[: img_share + txt_share], small[img_share + txt_share :]
    ready = jnp.concatenate(
        [
            reduced[:img_share].astype(BF16),
            small_rows(gains, slot - img_share),
            reduced[slot:].astype(BF16),
        ],
        axis=0,
    )
    gathered = exchange(jnp.broadcast_to(ready, (16, *ready.shape)), ("yl", "z"))
    pieces = [gathered] + [lax.ppermute(gathered, "x", ring(k)) for k in range(1, 4)]
    image_grad, text_grad, gains = finish(
        jnp.stack(sources), pieces, img_weight.shape[0], txt_weight.shape[0]
    )
    return (
        loss_parts[0:1] / pair_count,
        image_grad,
        text_grad,
        gains[:, :, :img_share].reshape(-1),
        gains[:, :, img_share : img_share + txt_share].reshape(-1),
        loss_parts[1:2] * logit_scale,
        loss_parts[2:3],
    )


def solution(mesh):
    inner = Mesh(mesh.devices.reshape(2, Z, 4, 2, 2), ("yl", "z", "x", "yh", "co"))
    tensor = ("yh", "co")
    return jax.shard_map(
        local,
        mesh=inner,
        in_specs=(
            P(DP, None),
            P(DP, None),
            P(),
            P(),
            P(None, tensor),
            P(None, tensor),
            P(),
            P(),
            P(),
        ),
        out_specs=(P(), P(None, tensor), P(None, tensor), P(), P(), P(), P()),
        check_vma=False,
    )
```

time: 397 us -> 250 us (0.63)
  waiting for transfers between devices: 213 us -> 120 us
  blocking collectives: 58.8 us -> 16.5 us
  starting transfers between devices: 54.4 us -> 70.7 us
  local copies, waits for them, and re-layouts: 22.2 us -> 6.22 us
  between operations: 19.6 us -> 6.58 us
    all_gather x2 -> x0, waiting for transfers between devices: 92.1 us -> none  [the longest x1 85 us: local(): lax.all_gather(image_half, ('yl', 'x', 'yh'), axis=0, tiled=False)]
    ppermute x7 -> x22, waiting for transfers between devices: 18.9 us -> 80 us  [the longest x6 20.8 us: y_move(): return lax.ppermute(value, ('yl', 'yh'), [(i, i ^ k) for i in range(4)])]
    all_to_all x3 -> x1, waiting for transfers between devices: 58.9 us -> 11.9 us  [exchange(): return lax.all_to_all(value, axes, split_axis=0, concat_axis=0, tiled=True)]
    all_to_all x2 -> x1, blocking collectives: 42.9 us -> 16.5 us  [exchange(): return lax.all_to_all(value, axes, split_axis=0, concat_axis=0, tiled=True)]
    ppermute x7 -> x22, starting transfers between devices: 13.1 us -> 37.5 us  [the longest x6 9.21 us: y_move(): return lax.ppermute(value, ('yl', 'yh'), [(i, i ^ k) for i in range(4)])]
    all_to_all x4 -> x0, blocking collectives: 15.9 us -> none  [the longest x1 4.05 us: local(): lax.all_to_all(text_emb, 'co', split_axis=0, concat_axis=1, tiled=True)]
    ppermute x3, waiting for transfers between devices: 14.1 us -> 2.93 us  [local(): lax.ppermute(rounded[k], 'z', turn(TEXT_Z - k)).astype(F32)]
    all_to_all x3 -> x1, starting transfers between devices: 22.8 us -> 14.6 us  [exchange(): return lax.all_to_all(value, axes, split_axis=0, concat_axis=0, tiled=True)]
  transfers between devices with their start and end apart: 24 -> 38, of which waited for: 20 -> 26; matrix products, arithmetic and copies ran while one was open for 1% -> 2% of each run, Pallas kernels for 0% -> 0%
where the time goes in v2:
time: 250 us
  waiting for transfers between devices  120 us (48%)
  starting transfers between devices  70.7 us (28%)
  blocking collectives  16.5 us (7%)
  Pallas kernels  15.1 us (6%)
  other arithmetic  12.4 us (5%)
  between operations  6.58 us (3%)
  local copies, waits for them, and re-layouts  6.22 us (2%)
    ppermute x6, waiting for transfers between devices, y_move(): return lax.ppermute(value, ('yl', 'yh'), [(i, i ^ k) for i in range(4)])  20.8 us
    ppermute x3, waiting for transfers between devices, local(): lax.ppermute(image_part[k], 'x', ring(-k)).astype(F32)  20.6 us
    ppermute x3, waiting for transfers between devices, local(): lax.ppermute(jnp.concatenate([image_du, pick(text_weight, targets[k]).ast...  17.6 us
    all_to_all x1, blocking collectives, exchange(): return lax.all_to_all(value, axes, split_axis=0, concat_axis=0, tiled=True)  16.5 us
    all_to_all x1, starting transfers between devices, exchange(): return lax.all_to_all(value, axes, split_axis=0, concat_axis=0, tiled=True)  14.6 us
    ppermute x3, waiting for transfers between devices, local(): lax.ppermute(gathered, 'x', ring(k))  14.4 us
    pallas_call x1, Pallas kernels, tile_grads(): pl.pallas_call(tile_kernel, grid=(STEPS,), in_specs=[pl.BlockSpec(memory_...  12.6 us
    all_to_all x1, waiting for transfers between devices, exchange(): return lax.all_to_all(value, axes, split_axis=0, concat_axis=0, tiled=True)  11.9 us
  transfers between devices with their start and end apart: 38, of which 26 were waited for; matrix products, arithmetic and copies ran while one was open for 2% of the time, Pallas kernels for 0%

profile of v2, /device:TPU:32, one launch (start us, length us, event | category | flops | bytes accessed | tf_op | source)
XLA Modules:
  0.0 249.6 jit_solution(10674175430853595327)
XLA Ops:
  8.9 3.2 %collective-permute-start.4 = (f32[1024]{0:T(1024)S(1)}, f32[1024]{0:T(1024)S(1)}, u32[]{:S(2)}, u32[]{:S(2)}) collective-permute-start(f32[1024]{0:T(1024)S(1)} %fusion.98), channel_id=1, source_target_pairs={{0,2},{2,0},{1,3},{3,1},{4,6},{6,4},{5,7},{7,5},{8,10},{10,8},{9,1... | collective-permute-start | bytes 12296 | tf_op jit(solution)/shard_map/ppermute | solution.py:26
  16.4 3.3 %collective-permute-start.6 = (bf16[224,512]{1,0:T(8,128)(2,1)S(1)}, bf16[224,512]{1,0:T(8,128)(2,1)S(1)}, u32[]{:S(2)}, u32[]{:S(2)}) collective-permute-start(bf16[224,512]{1,0:T(8,128)(2,1)S(1)} %get-tuple-element.72), channel_id=1, source_target_pairs={{0,2},{2,0},{128,130},{130,128},{1,3},{3,1},{129,131},{131,129},{4... | collective-permute-start | bytes 688136 | tf_op jit(solution)/shard_map/ppermute | solution.py:176
  20.8 5.7 %collective-permute-done.6 = bf16[224,512]{1,0:T(8,128)(2,1)S(1)} collective-permute-done((bf16[224,512]{1,0:T(8,128)(2,1)S(1)}, bf16[224,512]{1,0:T(8,128)(2,1)S(1)}, u32[]{:S(2)}, u32[]{:S(2)}) %collective-permute-start.6) | collective-permute-done | bytes 229408 | tf_op jit(solution)/shard_map/ppermute | solution.py:176
  26.5 4.4 %collective-permute-done.8 = bf16[224,512]{1,0:T(8,128)(2,1)S(1)} collective-permute-done((bf16[224,512]{1,0:T(8,128)(2,1)S(1)}, bf16[224,512]{1,0:T(8,128)(2,1)S(1)}, u32[]{:S(2)}, u32[]{:S(2)}) %collective-permute-start.8) | collective-permute-done | bytes 229408 | tf_op jit(solution)/shard_map/ppermute | solution.py:176
  34.3 2.7 %collective-permute-start.10 = (bf16[4,128,512]{2,1,0:T(8,128)(2,1)S(1)}, bf16[4,128,512]{2,1,0:T(8,128)(2,1)S(1)}, u32[]{:S(2)}, u32[]{:S(2)}) collective-permute-start(bf16[4,128,512]{2,1,0:T(8,128)(2,1)S(1)} %pad_maximum_fusion.3), channel_id=1, source_target_pairs={{0,8},{4,12},{8,0},{12,4},{1,9},{5,13},{9,1},{13,5},{2,10},{6,14},... | collective-permute-start | bytes 1572872 | tf_op jit(solution)/shard_map/ppermute | solution.py:241
  37.1 6.3 %collective-permute-done.12 = bf16[96,1024]{1,0:T(8,128)(2,1)S(1)} collective-permute-done((bf16[96,1024]{1,0:T(8,128)(2,1)S(1)}, bf16[96,1024]{1,0:T(8,128)(2,1)S(1)}, u32[]{:S(2)}, u32[]{:S(2)}) %collective-permute-start.12) | collective-permute-done | bytes 196640 | tf_op jit(solution)/shard_map/ppermute | solution.py:240
  43.4 4.3 %collective-permute-start.13 = (bf16[96,1024]{1,0:T(8,128)(2,1)S(1)}, bf16[96,1024]{1,0:T(8,128)(2,1)S(1)}, u32[]{:S(2)}, u32[]{:S(2)}) collective-permute-start(bf16[96,1024]{1,0:T(8,128)(2,1)S(1)} %broadcast_select_fusion.2), channel_id=1, source_target_pairs={{48,32},{32,16},{16,0},{0,48},{64,80},{80,96},{96,112},{112,64},{4... | collective-permute-start | bytes 589832 | tf_op jit(solution)/shard_map/ppermute | solution.py:242
  48.6 2.8 %collective-permute-start.15 = (bf16[96,1024]{1,0:T(8,128)(2,1)S(1)}, bf16[96,1024]{1,0:T(8,128)(2,1)S(1)}, u32[]{:S(2)}, u32[]{:S(2)}) collective-permute-start(bf16[96,1024]{1,0:T(8,128)(2,1)S(1)} %broadcast_select_fusion.2), channel_id=1, source_target_pairs={{48,0},{32,48},{16,32},{0,16},{64,112},{80,64},{96,80},{112,96},{4... | collective-permute-start | bytes 589832 | tf_op jit(solution)/shard_map/ppermute | solution.py:242
  53.4 2.8 %collective-permute-start.11 = (bf16[4,128,512]{2,1,0:T(8,128)(2,1)S(1)}, bf16[4,128,512]{2,1,0:T(8,128)(2,1)S(1)}, u32[]{:S(2)}, u32[]{:S(2)}) collective-permute-start(bf16[4,128,512]{2,1,0:T(8,128)(2,1)S(1)} %pad_maximum_fusion.3), channel_id=1, source_target_pairs={{0,12},{4,0},{8,4},{12,8},{1,13},{5,1},{9,5},{13,9},{2,14},{6,2},{... | collective-permute-start | bytes 1572872 | tf_op jit(solution)/shard_map/ppermute | solution.py:241
  56.1 5.8 %collective-permute-done.14 = bf16[96,1024]{1,0:T(8,128)(2,1)S(1)} collective-permute-done((bf16[96,1024]{1,0:T(8,128)(2,1)S(1)}, bf16[96,1024]{1,0:T(8,128)(2,1)S(1)}, u32[]{:S(2)}, u32[]{:S(2)}) %collective-permute-start.14) | collective-permute-done | bytes 196640 | tf_op jit(solution)/shard_map/ppermute | solution.py:242
  61.9 3.3 %collective-permute-done.15 = bf16[96,1024]{1,0:T(8,128)(2,1)S(1)} collective-permute-done((bf16[96,1024]{1,0:T(8,128)(2,1)S(1)}, bf16[96,1024]{1,0:T(8,128)(2,1)S(1)}, u32[]{:S(2)}, u32[]{:S(2)}) %collective-permute-start.15) | collective-permute-done | bytes 196640 | tf_op jit(solution)/shard_map/ppermute | solution.py:242
  68.0 12.6 %shard_map.144 = (bf16[16,128,512]{2,1,0:T(8,128)(2,1)S(1)}, bf16[768,1024]{1,0:T(8,128)(2,1)S(1)}, f32[8,128]{1,0:T(8,128)S(1)}) custom-call(f32[4]{0:T(128)S(1)} %pad_maximum_fusion.19.factors, s32[1024,1]{1,0:T(8,128)S(1)} %copy.16.partner, s32[1,768]{1,0:T(1,128)S(1)} %add.396.columns, bf16[16,128,512]{2,1,0:T(8,128)(2,1)S(1)} %constant_dynamic-update-slice_fusion.emb_i, ...), custom_call_target="tpu_custom_call" | custom-call | tf_op jit(solution)/shard_map/pallas_call | solution.py:100
  82.6 2.9 %collective-permute-start.17 = (bf16[4,128,512]{2,1,0:T(8,128)(2,1)S(1)}, bf16[4,128,512]{2,1,0:T(8,128)(2,1)S(1)}, u32[]{:S(2)}, u32[]{:S(2)}) collective-permute-start(bf16[4,128,512]{2,1,0:T(8,128)(2,1)S(1)} %get-tuple-element.27), channel_id=1, source_target_pairs={{0,12},{4,0},{8,4},{12,8},{1,13},{5,1},{9,5},{13,9},{2,14},{6,2},{... | collective-permute-start | bytes 1572872 | tf_op jit(solution)/shard_map/ppermute | solution.py:279
  88.6 2.6 %collective-permute-start.21 = (bf16[96,1024]{1,0:T(8,128)(2,1)S(1)}, bf16[96,1024]{1,0:T(8,128)(2,1)S(1)}, u32[]{:S(2)}, u32[]{:S(2)}) collective-permute-start(bf16[96,1024]{1,0:T(8,128)(2,1)S(1)} %get-tuple-element.47), channel_id=1, source_target_pairs={{48,0},{32,48},{16,32},{0,16},{64,112},{80,64},{96,80},{112,96},{4... | collective-permute-start | bytes 589832 | tf_op jit(solution)/shard_map/ppermute | solution.py:286
  91.3 17.1 %collective-permute-done.17 = bf16[4,128,512]{2,1,0:T(8,128)(2,1)S(1)} collective-permute-done((bf16[4,128,512]{2,1,0:T(8,128)(2,1)S(1)}, bf16[4,128,512]{2,1,0:T(8,128)(2,1)S(1)}, u32[]{:S(2)}, u32[]{:S(2)}) %collective-permute-start.17) | collective-permute-done | bytes 524320 | tf_op jit(solution)/shard_map/ppermute | solution.py:279
  108.6 3.5 %collective-permute-done.19 = bf16[4,128,512]{2,1,0:T(8,128)(2,1)S(1)} collective-permute-done((bf16[4,128,512]{2,1,0:T(8,128)(2,1)S(1)}, bf16[4,128,512]{2,1,0:T(8,128)(2,1)S(1)}, u32[]{:S(2)}, u32[]{:S(2)}) %collective-permute-start.19) | collective-permute-done | bytes 524320 | tf_op jit(solution)/shard_map/ppermute | solution.py:279
  112.4 2.9 %collective-permute-done.23 = bf16[96,1024]{1,0:T(8,128)(2,1)S(1)} collective-permute-done((bf16[96,1024]{1,0:T(8,128)(2,1)S(1)}, bf16[96,1024]{1,0:T(8,128)(2,1)S(1)}, u32[]{:S(2)}, u32[]{:S(2)}) %collective-permute-start.23) | collective-permute-done | bytes 196640 | tf_op jit(solution)/shard_map/ppermute | solution.py:286
  117.8 3.1 %collective-permute-done.24 = bf16[96,1024]{1,0:T(8,128)(2,1)S(1)} collective-permute-done((bf16[96,1024]{1,0:T(8,128)(2,1)S(1)}, bf16[96,1024]{1,0:T(8,128)(2,1)S(1)}, u32[]{:S(2)}, u32[]{:S(2)}) %collective-permute-start.24) | collective-permute-done | bytes 196640 | tf_op jit(solution)/shard_map/ppermute | solution.py:287
  122.9 3.0 %collective-permute-start.25 = (bf16[224,512]{1,0:T(8,128)(2,1)S(1)}, bf16[224,512]{1,0:T(8,128)(2,1)S(1)}, u32[]{:S(2)}, u32[]{:S(2)}) collective-permute-start(bf16[224,512]{1,0:T(8,128)(2,1)S(1)} %get-tuple-element.77), channel_id=1, source_target_pairs={{0,2},{2,0},{128,130},{130,128},{1,3},{3,1},{129,131},{131,129},{4... | collective-permute-start | bytes 688136 | tf_op jit(solution)/shard_map/ppermute | solution.py:176
  126.2 3.0 %collective-permute-done.26 = bf16[224,512]{1,0:T(8,128)(2,1)S(1)} collective-permute-done((bf16[224,512]{1,0:T(8,128)(2,1)S(1)}, bf16[224,512]{1,0:T(8,128)(2,1)S(1)}, u32[]{:S(2)}, u32[]{:S(2)}) %collective-permute-start.26) | collective-permute-done | bytes 229408 | tf_op jit(solution)/shard_map/ppermute | solution.py:176
  129.2 7.4 %collective-permute-done.27 = bf16[224,512]{1,0:T(8,128)(2,1)S(1)} collective-permute-done((bf16[224,512]{1,0:T(8,128)(2,1)S(1)}, bf16[224,512]{1,0:T(8,128)(2,1)S(1)}, u32[]{:S(2)}, u32[]{:S(2)}) %collective-permute-start.27) | collective-permute-done | bytes 229408 | tf_op jit(solution)/shard_map/ppermute | solution.py:176
  140.1 5.6 %collective-permute-start.30 = (bf16[528,256]{1,0:T(8,128)(2,1)S(1)}, bf16[528,256]{1,0:T(8,128)(2,1)S(1)}, u32[]{:S(2)}, u32[]{:S(2)}) collective-permute-start(bf16[528,256]{1,0:T(8,128)(2,1)S(1)} %get-tuple-element.69), channel_id=1, source_target_pairs={{0,8},{4,12},{8,0},{12,4},{1,9},{5,13},{9,1},{13,5},{2,10},{6,14},... | collective-permute-start | bytes 811016 | tf_op jit(solution)/shard_map/ppermute | solution.py:335
  146.0 3.1 %collective-permute-start.2 = (bf16[256,448]{1,0:T(8,128)(2,1)S(1)}, bf16[256,448]{1,0:T(8,128)(2,1)S(1)}, u32[]{:S(2)}, u32[]{:S(2)}) collective-permute-start(bf16[256,448]{1,0:T(8,128)(2,1)S(1)} %get-tuple-element.35), channel_id=1, source_target_pairs={{0,12},{4,0},{8,4},{12,8},{1,13},{5,1},{9,5},{13,9},{2,14},{6,2},{... | collective-permute-start | bytes 688136 | tf_op jit(solution)/shard_map/ppermute | solution.py:271
  153.3 5.3 %collective-permute-done.30 = bf16[528,256]{1,0:T(8,128)(2,1)S(1)} collective-permute-done((bf16[528,256]{1,0:T(8,128)(2,1)S(1)}, bf16[528,256]{1,0:T(8,128)(2,1)S(1)}, u32[]{:S(2)}, u32[]{:S(2)}) %collective-permute-start.30) | collective-permute-done | bytes 270368 | tf_op jit(solution)/shard_map/ppermute | solution.py:335
  158.5 10.1 %collective-permute-done.31 = bf16[528,256]{1,0:T(8,128)(2,1)S(1)} collective-permute-done((bf16[528,256]{1,0:T(8,128)(2,1)S(1)}, bf16[528,256]{1,0:T(8,128)(2,1)S(1)}, u32[]{:S(2)}, u32[]{:S(2)}) %collective-permute-start.31) | collective-permute-done | bytes 270368 | tf_op jit(solution)/shard_map/ppermute | solution.py:335
  170.6 14.6 %all-to-all-start = ((bf16[16,48,256]{2,1,0:T(8,128)(2,1)}), bf16[16,48,256]{2,1,0:T(8,128)(2,1)S(1)}, u32[]{:S(2)}, u32[]{:S(2)}) async-start(bf16[16,48,256]{2,1,0:T(8,128)(2,1)} %pad_maximum_fusion.7), calls=%async_computation | async-start | bytes 786432 | tf_op jit(solution)/shard_map/all_to_all | solution.py:30
  185.1 11.9 %all-to-all-done = bf16[16,48,256]{2,1,0:T(8,128)(2,1)S(1)} async-done(((bf16[16,48,256]{2,1,0:T(8,128)(2,1)}), bf16[16,48,256]{2,1,0:T(8,128)(2,1)S(1)}, u32[]{:S(2)}, u32[]{:S(2)}) %all-to-all-start) | async-done | bytes 393248 | tf_op jit(solution)/shard_map/all_to_all | solution.py:30
  202.2 3.9 %collective-permute-done.33 = f32[47]{0:T(128)S(1)} collective-permute-done((f32[47]{0:T(128)S(1)}, f32[47]{0:T(128)S(1)}, u32[]{:S(2)}, u32[]{:S(2)}) %collective-permute-start.33) | collective-permute-done | bytes 220 | tf_op jit(solution)/shard_map/ppermute | solution.py:26
  206.1 16.5 %all_to_all.10.first = bf16[16,48,256]{2,1,0:T(8,128)(2,1)S(1)} all-to-all(bf16[16,48,256]{2,1,0:T(8,128)(2,1)S(1)} %broadcast_in_dim.9), channel_id=1, replica_groups=mesh['yl'=2,'z'=8,'x'=4,'yh'=2,'co'=2] {'yl','z'}, dimensions={0} | all-to-all | bytes 786432 | tf_op jit(solution)/shard_map/all_to_all | solution.py:30
  223.2 3.8 %collective-permute-start.35 = (bf16[16,48,256]{2,1,0:T(8,128)(2,1)S(1)}, bf16[16,48,256]{2,1,0:T(8,128)(2,1)S(1)}, u32[]{:S(2)}, u32[]{:S(2)}) collective-permute-start(bf16[16,48,256]{2,1,0:T(8,128)(2,1)S(1)} %all_to_all.10.first), channel_id=1, source_target_pairs={{0,8},{4,12},{8,0},{12,4},{1,9},{5,13},{9,1},{13,5},{2,10},{6,14},... | collective-permute-start | bytes 1179656 | tf_op jit(solution)/shard_map/ppermute | solution.py:391
  229.0 5.7 %collective-permute-done.34.second = bf16[16,48,256]{2,1,0:T(8,128)(2,1)S(1)} collective-permute-done((bf16[16,48,256]{2,1,0:T(8,128)(2,1)S(1)}, bf16[16,48,256]{2,1,0:T(8,128)(2,1)S(1)}, u32[]{:S(2)}, u32[]{:S(2)}) %collective-permute-start.34) | collective-permute-done | bytes 393248 | tf_op jit(solution)/shard_map/ppermute | solution.py:391
  234.7 8.7 %collective-permute-done.35.third = bf16[16,48,256]{2,1,0:T(8,128)(2,1)S(1)} collective-permute-done((bf16[16,48,256]{2,1,0:T(8,128)(2,1)S(1)}, bf16[16,48,256]{2,1,0:T(8,128)(2,1)S(1)}, u32[]{:S(2)}, u32[]{:S(2)}) %collective-permute-start.35) | collective-permute-done | bytes 393248 | tf_op jit(solution)/shard_map/ppermute | solution.py:391
  (196 shorter events, 51.5 us)
Async XLA Ops:
  8.9 5.1 %collective-permute-start.4 = (f32[1024]{0:T(1024)S(1)}, f32[1024]{0:T(1024)S(1)}, u32[]{:S(2)}, u32[]{:S(2)}) collective-permute-start(f32[1024]{0:T(1024)S(1)} %fusion.98), channel_id=1, source_target_pairs={{0,2},{2,0},{1,3},{3,1},{4,6},{6,4},{5,7},{7,5},{8,10},{10,8},{9,1... | collective-permute-start | bytes 12296 | tf_op jit(solution)/shard_map/ppermute | solution.py:26
  16.4 10.0 %collective-permute-start.6 = (bf16[224,512]{1,0:T(8,128)(2,1)S(1)}, bf16[224,512]{1,0:T(8,128)(2,1)S(1)}, u32[]{:S(2)}, u32[]{:S(2)}) collective-permute-start(bf16[224,512]{1,0:T(8,128)(2,1)S(1)} %get-tuple-element.72), channel_id=1, source_target_pairs={{0,2},{2,0},{128,130},{130,128},{1,3},{3,1},{129,131},{131,129},{4... | collective-permute-start | bytes 688136 | tf_op jit(solution)/shard_map/ppermute | solution.py:176
  19.7 11.2 %collective-permute-start.8 = (bf16[224,512]{1,0:T(8,128)(2,1)S(1)}, bf16[224,512]{1,0:T(8,128)(2,1)S(1)}, u32[]{:S(2)}, u32[]{:S(2)}) collective-permute-start(bf16[224,512]{1,0:T(8,128)(2,1)S(1)} %get-tuple-element.71), channel_id=1, source_target_pairs={{0,130},{2,128},{128,2},{130,0},{1,131},{3,129},{129,3},{131,1},{4... | collective-permute-start | bytes 688136 | tf_op jit(solution)/shard_map/ppermute | solution.py:176
  20.8 10.5 %collective-permute-start.7 = (bf16[224,512]{1,0:T(8,128)(2,1)S(1)}, bf16[224,512]{1,0:T(8,128)(2,1)S(1)}, u32[]{:S(2)}, u32[]{:S(2)}) collective-permute-start(bf16[224,512]{1,0:T(8,128)(2,1)S(1)} %get-tuple-element.73), channel_id=1, source_target_pairs={{0,128},{2,130},{128,0},{130,2},{1,129},{3,131},{129,1},{131,3},{4... | collective-permute-start | bytes 688136 | tf_op jit(solution)/shard_map/ppermute | solution.py:176
  31.3 12.0 %collective-permute-start.12 = (bf16[96,1024]{1,0:T(8,128)(2,1)S(1)}, bf16[96,1024]{1,0:T(8,128)(2,1)S(1)}, u32[]{:S(2)}, u32[]{:S(2)}) collective-permute-start(bf16[96,1024]{1,0:T(8,128)(2,1)S(1)} %pad_maximum_fusion.16), channel_id=1, source_target_pairs={{64,48},{80,32},{96,16},{112,0},{65,49},{81,33},{97,17},{113,1},{6... | collective-permute-start | bytes 589832 | tf_op jit(solution)/shard_map/ppermute | solution.py:240
  32.7 32.9 %collective-permute-start.9 = (bf16[4,128,512]{2,1,0:T(8,128)(2,1)S(1)}, bf16[4,128,512]{2,1,0:T(8,128)(2,1)S(1)}, u32[]{:S(2)}, u32[]{:S(2)}) collective-permute-start(bf16[4,128,512]{2,1,0:T(8,128)(2,1)S(1)} %pad_maximum_fusion.3), channel_id=1, source_target_pairs={{0,4},{4,8},{8,12},{12,0},{1,5},{5,9},{9,13},{13,1},{2,6},{6,10},{... | collective-permute-start | bytes 1572872 | tf_op jit(solution)/shard_map/ppermute | solution.py:241
  34.3 31.3 %collective-permute-start.10 = (bf16[4,128,512]{2,1,0:T(8,128)(2,1)S(1)}, bf16[4,128,512]{2,1,0:T(8,128)(2,1)S(1)}, u32[]{:S(2)}, u32[]{:S(2)}) collective-permute-start(bf16[4,128,512]{2,1,0:T(8,128)(2,1)S(1)} %pad_maximum_fusion.3), channel_id=1, source_target_pairs={{0,8},{4,12},{8,0},{12,4},{1,9},{5,13},{9,1},{13,5},{2,10},{6,14},... | collective-permute-start | bytes 1572872 | tf_op jit(solution)/shard_map/ppermute | solution.py:241
  43.4 10.0 %collective-permute-start.13 = (bf16[96,1024]{1,0:T(8,128)(2,1)S(1)}, bf16[96,1024]{1,0:T(8,128)(2,1)S(1)}, u32[]{:S(2)}, u32[]{:S(2)}) collective-permute-start(bf16[96,1024]{1,0:T(8,128)(2,1)S(1)} %broadcast_select_fusion.2), channel_id=1, source_target_pairs={{48,32},{32,16},{16,0},{0,48},{64,80},{80,96},{96,112},{112,64},{4... | collective-permute-start | bytes 589832 | tf_op jit(solution)/shard_map/ppermute | solution.py:242
  47.7 14.2 %collective-permute-start.14 = (bf16[96,1024]{1,0:T(8,128)(2,1)S(1)}, bf16[96,1024]{1,0:T(8,128)(2,1)S(1)}, u32[]{:S(2)}, u32[]{:S(2)}) collective-permute-start(bf16[96,1024]{1,0:T(8,128)(2,1)S(1)} %broadcast_select_fusion.2), channel_id=1, source_target_pairs={{48,16},{32,0},{16,48},{0,32},{64,96},{80,112},{96,64},{112,80},{4... | collective-permute-start | bytes 589832 | tf_op jit(solution)/shard_map/ppermute | solution.py:242
  48.6 16.5 %collective-permute-start.15 = (bf16[96,1024]{1,0:T(8,128)(2,1)S(1)}, bf16[96,1024]{1,0:T(8,128)(2,1)S(1)}, u32[]{:S(2)}, u32[]{:S(2)}) collective-permute-start(bf16[96,1024]{1,0:T(8,128)(2,1)S(1)} %broadcast_select_fusion.2), channel_id=1, source_target_pairs={{48,0},{32,48},{16,32},{0,16},{64,112},{80,64},{96,80},{112,96},{4... | collective-permute-start | bytes 589832 | tf_op jit(solution)/shard_map/ppermute | solution.py:242
  53.4 12.4 %collective-permute-start.11 = (bf16[4,128,512]{2,1,0:T(8,128)(2,1)S(1)}, bf16[4,128,512]{2,1,0:T(8,128)(2,1)S(1)}, u32[]{:S(2)}, u32[]{:S(2)}) collective-permute-start(bf16[4,128,512]{2,1,0:T(8,128)(2,1)S(1)} %pad_maximum_fusion.3), channel_id=1, source_target_pairs={{0,12},{4,0},{8,4},{12,8},{1,13},{5,1},{9,5},{13,9},{2,14},{6,2},{... | collective-permute-start | bytes 1572872 | tf_op jit(solution)/shard_map/ppermute | solution.py:241
  81.9 5.2 %collective-permute-start.20 = (bf16[4,96,1024]{2,1,0:T(8,128)(2,1)}, bf16[4,96,1024]{2,1,0:T(8,128)(2,1)}, u32[]{:S(2)}, u32[]{:S(2)}) collective-permute-start(bf16[4,96,1024]{2,1,0:T(8,128)(2,1)} %bitcast.36), channel_id=1, source_target_pairs={{0,1},{1,0},{2,3},{3,2},{4,5},{5,4},{6,7},{7,6},{8,9},{9,8},{10,11... | collective-permute-start | bytes 2359304 | tf_op jit(solution)/shard_map/ppermute | solution.py:26
  82.6 25.8 %collective-permute-start.17 = (bf16[4,128,512]{2,1,0:T(8,128)(2,1)S(1)}, bf16[4,128,512]{2,1,0:T(8,128)(2,1)S(1)}, u32[]{:S(2)}, u32[]{:S(2)}) collective-permute-start(bf16[4,128,512]{2,1,0:T(8,128)(2,1)S(1)} %get-tuple-element.27), channel_id=1, source_target_pairs={{0,12},{4,0},{8,4},{12,8},{1,13},{5,1},{9,5},{13,9},{2,14},{6,2},{... | collective-permute-start | bytes 1572872 | tf_op jit(solution)/shard_map/ppermute | solution.py:279
  85.4 23.2 %collective-permute-start.18 = (bf16[4,128,512]{2,1,0:T(8,128)(2,1)S(1)}, bf16[4,128,512]{2,1,0:T(8,128)(2,1)S(1)}, u32[]{:S(2)}, u32[]{:S(2)}) collective-permute-start(bf16[4,128,512]{2,1,0:T(8,128)(2,1)S(1)} %get-tuple-element.29), channel_id=1, source_target_pairs={{0,8},{4,12},{8,0},{12,4},{1,9},{5,13},{9,1},{13,5},{2,10},{6,14},... | collective-permute-start | bytes 1572872 | tf_op jit(solution)/shard_map/ppermute | solution.py:279
  86.2 25.8 %collective-permute-start.19 = (bf16[4,128,512]{2,1,0:T(8,128)(2,1)S(1)}, bf16[4,128,512]{2,1,0:T(8,128)(2,1)S(1)}, u32[]{:S(2)}, u32[]{:S(2)}) collective-permute-start(bf16[4,128,512]{2,1,0:T(8,128)(2,1)S(1)} %get-tuple-element.28), channel_id=1, source_target_pairs={{0,4},{4,8},{8,12},{12,0},{1,5},{5,9},{9,13},{13,1},{2,6},{6,10},{... | collective-permute-start | bytes 1572872 | tf_op jit(solution)/shard_map/ppermute | solution.py:279
  88.6 23.8 %collective-permute-start.21 = (bf16[96,1024]{1,0:T(8,128)(2,1)S(1)}, bf16[96,1024]{1,0:T(8,128)(2,1)S(1)}, u32[]{:S(2)}, u32[]{:S(2)}) collective-permute-start(bf16[96,1024]{1,0:T(8,128)(2,1)S(1)} %get-tuple-element.47), channel_id=1, source_target_pairs={{48,0},{32,48},{16,32},{0,16},{64,112},{80,64},{96,80},{112,96},{4... | collective-permute-start | bytes 589832 | tf_op jit(solution)/shard_map/ppermute | solution.py:286
  91.2 21.2 %collective-permute-start.22 = (bf16[96,1024]{1,0:T(8,128)(2,1)S(1)}, bf16[96,1024]{1,0:T(8,128)(2,1)S(1)}, u32[]{:S(2)}, u32[]{:S(2)}) collective-permute-start(bf16[96,1024]{1,0:T(8,128)(2,1)S(1)} %get-tuple-element.49), channel_id=1, source_target_pairs={{48,16},{32,0},{16,48},{0,32},{64,96},{80,112},{96,64},{112,80},{4... | collective-permute-start | bytes 589832 | tf_op jit(solution)/shard_map/ppermute | solution.py:286
  108.4 6.9 %collective-permute-start.23 = (bf16[96,1024]{1,0:T(8,128)(2,1)S(1)}, bf16[96,1024]{1,0:T(8,128)(2,1)S(1)}, u32[]{:S(2)}, u32[]{:S(2)}) collective-permute-start(bf16[96,1024]{1,0:T(8,128)(2,1)S(1)} %get-tuple-element.48), channel_id=1, source_target_pairs={{48,32},{32,16},{16,0},{0,48},{64,80},{80,96},{96,112},{112,64},{4... | collective-permute-start | bytes 589832 | tf_op jit(solution)/shard_map/ppermute | solution.py:286
  115.4 5.5 %collective-permute-start.24 = (bf16[96,1024]{1,0:T(8,128)(2,1)S(1)}, bf16[96,1024]{1,0:T(8,128)(2,1)S(1)}, u32[]{:S(2)}, u32[]{:S(2)}) collective-permute-start(bf16[96,1024]{1,0:T(8,128)(2,1)S(1)} %fusion.44), channel_id=1, source_target_pairs={{48,64},{32,80},{16,96},{0,112},{49,65},{33,81},{17,97},{1,113},{5... | collective-permute-start | bytes 589832 | tf_op jit(solution)/shard_map/ppermute | solution.py:287
  121.2 8.0 %collective-permute-start.26 = (bf16[224,512]{1,0:T(8,128)(2,1)S(1)}, bf16[224,512]{1,0:T(8,128)(2,1)S(1)}, u32[]{:S(2)}, u32[]{:S(2)}) collective-permute-start(bf16[224,512]{1,0:T(8,128)(2,1)S(1)} %pad_maximum_fusion.15), channel_id=1, source_target_pairs={{0,128},{2,130},{128,0},{130,2},{1,129},{3,131},{129,1},{131,3},{4... | collective-permute-start | bytes 688136 | tf_op jit(solution)/shard_map/ppermute | solution.py:176
  122.9 13.7 %collective-permute-start.25 = (bf16[224,512]{1,0:T(8,128)(2,1)S(1)}, bf16[224,512]{1,0:T(8,128)(2,1)S(1)}, u32[]{:S(2)}, u32[]{:S(2)}) collective-permute-start(bf16[224,512]{1,0:T(8,128)(2,1)S(1)} %get-tuple-element.77), channel_id=1, source_target_pairs={{0,2},{2,0},{128,130},{130,128},{1,3},{3,1},{129,131},{131,129},{4... | collective-permute-start | bytes 688136 | tf_op jit(solution)/shard_map/ppermute | solution.py:176
  125.9 10.7 %collective-permute-start.27 = (bf16[224,512]{1,0:T(8,128)(2,1)S(1)}, bf16[224,512]{1,0:T(8,128)(2,1)S(1)}, u32[]{:S(2)}, u32[]{:S(2)}) collective-permute-start(bf16[224,512]{1,0:T(8,128)(2,1)S(1)} %get-tuple-element.76), channel_id=1, source_target_pairs={{0,130},{2,128},{128,2},{130,0},{1,131},{3,129},{129,3},{131,1},{4... | collective-permute-start | bytes 688136 | tf_op jit(solution)/shard_map/ppermute | solution.py:176
  139.8 11.5 %collective-permute-start.29 = (bf16[528,256]{1,0:T(8,128)(2,1)S(1)}, bf16[528,256]{1,0:T(8,128)(2,1)S(1)}, u32[]{:S(2)}, u32[]{:S(2)}) collective-permute-start(bf16[528,256]{1,0:T(8,128)(2,1)S(1)} %get-tuple-element.68), channel_id=1, source_target_pairs={{0,4},{4,8},{8,12},{12,0},{1,5},{5,9},{9,13},{13,1},{2,6},{6,10},{... | collective-permute-start | bytes 811016 | tf_op jit(solution)/shard_map/ppermute | solution.py:335
  140.1 18.4 %collective-permute-start.30 = (bf16[528,256]{1,0:T(8,128)(2,1)S(1)}, bf16[528,256]{1,0:T(8,128)(2,1)S(1)}, u32[]{:S(2)}, u32[]{:S(2)}) collective-permute-start(bf16[528,256]{1,0:T(8,128)(2,1)S(1)} %get-tuple-element.69), channel_id=1, source_target_pairs={{0,8},{4,12},{8,0},{12,4},{1,9},{5,13},{9,1},{13,5},{2,10},{6,14},... | collective-permute-start | bytes 811016 | tf_op jit(solution)/shard_map/ppermute | solution.py:335
  145.8 22.9 %collective-permute-start = (bf16[256,448]{1,0:T(8,128)(2,1)S(1)}, bf16[256,448]{1,0:T(8,128)(2,1)S(1)}, u32[]{:S(2)}, u32[]{:S(2)}) collective-permute-start(bf16[256,448]{1,0:T(8,128)(2,1)S(1)} %get-tuple-element.37), channel_id=1, source_target_pairs={{0,4},{4,8},{8,12},{12,0},{1,5},{5,9},{9,13},{13,1},{2,6},{6,10},{... | collective-permute-start | bytes 688136 | tf_op jit(solution)/shard_map/ppermute | solution.py:271
  145.8 23.1 %collective-permute-start.1 = (bf16[256,448]{1,0:T(8,128)(2,1)S(1)}, bf16[256,448]{1,0:T(8,128)(2,1)S(1)}, u32[]{:S(2)}, u32[]{:S(2)}) collective-permute-start(bf16[256,448]{1,0:T(8,128)(2,1)S(1)} %get-tuple-element.36), channel_id=1, source_target_pairs={{0,8},{4,12},{8,0},{12,4},{1,9},{5,13},{9,1},{13,5},{2,10},{6,14},... | collective-permute-start | bytes 688136 | tf_op jit(solution)/shard_map/ppermute | solution.py:271
  146.0 23.0 %collective-permute-start.2 = (bf16[256,448]{1,0:T(8,128)(2,1)S(1)}, bf16[256,448]{1,0:T(8,128)(2,1)S(1)}, u32[]{:S(2)}, u32[]{:S(2)}) collective-permute-start(bf16[256,448]{1,0:T(8,128)(2,1)S(1)} %get-tuple-element.35), channel_id=1, source_target_pairs={{0,12},{4,0},{8,4},{12,8},{1,13},{5,1},{9,5},{13,9},{2,14},{6,2},{... | collective-permute-start | bytes 688136 | tf_op jit(solution)/shard_map/ppermute | solution.py:271
  151.3 17.3 %collective-permute-start.31 = (bf16[528,256]{1,0:T(8,128)(2,1)S(1)}, bf16[528,256]{1,0:T(8,128)(2,1)S(1)}, u32[]{:S(2)}, u32[]{:S(2)}) collective-permute-start(bf16[528,256]{1,0:T(8,128)(2,1)S(1)} %get-tuple-element.70), channel_id=1, source_target_pairs={{0,12},{4,0},{8,4},{12,8},{1,13},{5,1},{9,5},{13,9},{2,14},{6,2},{... | collective-permute-start | bytes 811016 | tf_op jit(solution)/shard_map/ppermute | solution.py:335
  170.6 26.5 %all-to-all-start = ((bf16[16,48,256]{2,1,0:T(8,128)(2,1)}), bf16[16,48,256]{2,1,0:T(8,128)(2,1)S(1)}, u32[]{:S(2)}, u32[]{:S(2)}) async-start(bf16[16,48,256]{2,1,0:T(8,128)(2,1)} %pad_maximum_fusion.7), calls=%async_computation | async-start | bytes 786432 | tf_op jit(solution)/shard_map/all_to_all | solution.py:30
  222.6 12.2 %collective-permute-start.34 = (bf16[16,48,256]{2,1,0:T(8,128)(2,1)S(1)}, bf16[16,48,256]{2,1,0:T(8,128)(2,1)S(1)}, u32[]{:S(2)}, u32[]{:S(2)}) collective-permute-start(bf16[16,48,256]{2,1,0:T(8,128)(2,1)S(1)} %all_to_all.10.first), channel_id=1, source_target_pairs={{0,4},{4,8},{8,12},{12,0},{1,5},{5,9},{9,13},{13,1},{2,6},{6,10},{... | collective-permute-start | bytes 1179656 | tf_op jit(solution)/shard_map/ppermute | solution.py:391
  223.2 20.2 %collective-permute-start.35 = (bf16[16,48,256]{2,1,0:T(8,128)(2,1)S(1)}, bf16[16,48,256]{2,1,0:T(8,128)(2,1)S(1)}, u32[]{:S(2)}, u32[]{:S(2)}) collective-permute-start(bf16[16,48,256]{2,1,0:T(8,128)(2,1)S(1)} %all_to_all.10.first), channel_id=1, source_target_pairs={{0,8},{4,12},{8,0},{12,4},{1,9},{5,13},{9,1},{13,5},{2,10},{6,14},... | collective-permute-start | bytes 1179656 | tf_op jit(solution)/shard_map/ppermute | solution.py:391
  227.1 16.4 %collective-permute-start.36 = (bf16[16,48,256]{2,1,0:T(8,128)(2,1)S(1)}, bf16[16,48,256]{2,1,0:T(8,128)(2,1)S(1)}, u32[]{:S(2)}, u32[]{:S(2)}) collective-permute-start(bf16[16,48,256]{2,1,0:T(8,128)(2,1)S(1)} %all_to_all.10.first), channel_id=1, source_target_pairs={{0,12},{4,0},{8,4},{12,8},{1,13},{5,1},{9,5},{13,9},{2,14},{6,2},{... | collective-permute-start | bytes 1179656 | tf_op jit(solution)/shard_map/ppermute | solution.py:391
  (18 other events, 42.6 us)

commit v3 on v2

--- a/solution.py
+++ b/solution.py
@@ -134,7 +134,7 @@
     ]
 
 
-def finish_kernel(places, first, second, third, fourth, out_i, out_t, out_g, rows):
+def finish_kernel(places, first, second, third, fourth, out_i, out_t, rows):
     image_rows = rows.shape[0] // 16
     text_rows = out_t.shape[0] // 64
     padded = first.shape[1] - text_rows
@@ -145,8 +145,6 @@
             rows[s * image_rows : (s + 1) * image_rows] = values[:image_rows]
             start = pl.multiple_of(place * (16 * text_rows) + s * text_rows, 8)
             out_t[pl.ds(start, text_rows)] = values[padded:]
-            tail = values[image_rows:padded]
-            out_g[place, s : s + 1] = tail[0:1] + tail[1:2] + tail[2:3]
         start = pl.multiple_of(place * (16 * image_rows), 8)
         out_i[pl.ds(start, 16 * image_rows)] = rows[...]
 
@@ -157,11 +155,10 @@
     return pl.pallas_call(
         finish_kernel,
         in_specs=[pl.BlockSpec(memory_space=pltpu.SMEM)] + [whole] * 4,
-        out_specs=[whole] * 3,
+        out_specs=[whole] * 2,
         out_shape=[
             jax.ShapeDtypeStruct((image_total, cols), F32),
             jax.ShapeDtypeStruct((text_total, cols), F32),
-            jax.ShapeDtypeStruct((4, 16, cols), F32),
         ],
         scratch_shapes=[pltpu.VMEM((image_total // 4, cols), F32)],
         compiler_params=pltpu.CompilerParams(vmem_limit_bytes=24 * 1024 * 1024),
@@ -196,6 +193,13 @@
 
     text_hidden = hidden_rows(txt_feats, txt_gain)
     image_hidden = hidden_rows(img_feats, img_gain)
+    share_cols = image_hidden.shape[1] // 4
+    parts = jnp.stack(
+        [image_hidden[:, i * share_cols : (i + 1) * share_cols] for i in range(4)]
+    )
+    hidden_x = [pick(parts, x)]
+    hidden_x += [lax.ppermute(pick(parts, targets[k]), "x", ring(k)) for k in range(1, 4)]
+
     text_proj = jnp.dot(text_hidden, txt_weight, preferred_element_type=F32)
     image_proj = jnp.dot(image_hidden, img_weight, preferred_element_type=F32)
     squares = jnp.concatenate(
@@ -203,6 +207,7 @@
     )
     squares = squares + swap(squares, "co")
     squares = squares + swap(squares, "yh")
+    squares, hidden_x[1] = lax.optimization_barrier((squares, hidden_x[1]))
     norms = jnp.sqrt(squares + EPS)[:, None]
     text_norm, image_norm = norms[:txt_count], norms[txt_count:]
     text_emb = (text_proj / text_norm).astype(BF16)
@@ -232,6 +237,7 @@
     for k in range(1, 4):
         target = jnp.bitwise_xor(yl * 2 + yh, k)
         got.append(y_move(jnp.concatenate([image_own, pick(text_own, target)], axis=0), k))
+    got, hidden_x = lax.optimization_barrier((got, hidden_x))
     slabs = jnp.stack([image_own] + [g[:img_half] for g in got])
     mine = jnp.where(yl == 1, pick(text_own, yl * 2 + yh), got[1][img_half:])
     other = jnp.where(yl == 1, got[0][img_half:], got[2][img_half:])
@@ -262,65 +268,69 @@
     ]
     factors = jnp.stack([logit_scale, bias[0], *weights])
 
-    share_cols = image_hidden.shape[1] // 4
-    parts = jnp.stack(
-        [image_hidden[:, i * share_cols : (i + 1) * share_cols] for i in range(4)]
-    )
-    hidden_x = jnp.concatenate(
-        [pick(parts, x)]
-        + [lax.ppermute(pick(parts, targets[k]), "x", ring(k)) for k in range(1, 4)]
-    )
-
     image_part, text_part, part_sums = tile_grads(factors, partner, columns, image_all, text_tile)
-
-    image_part = image_part.reshape(4, 4, img_half, width)
-    image_sum = image_part[0].astype(F32)
-    for k in range(1, 4):
-        image_sum = image_sum + lax.ppermute(image_part[k], "x", ring(-k)).astype(F32)
 
     text_part = text_part.reshape(2, TEXT_Z, piece, 2 * width)
     both = text_part[0].astype(F32) + swap(text_part[1], "co").astype(F32)
     rounded = both.astype(BF16)
+    image_part = image_part.reshape(4, 4, img_half, width)
+    text_got = [lax.ppermute(rounded[k], "z", turn(TEXT_Z - k)) for k in range(1, TEXT_Z)]
+    image_near = [lax.ppermute(image_part[k], "x", ring(-k)) for k in (1, 3)]
+    text_got[0], image_far = lax.optimization_barrier((text_got[0], image_part[2]))
+    image_far = lax.ppermute(image_far, "x", ring(-2))
+    text_got, image_near, image_far = lax.optimization_barrier((text_got, image_near, image_far))
     text_sum = both[0]
-    for k in range(1, TEXT_Z):
-        text_sum = text_sum + lax.ppermute(rounded[k], "z", turn(TEXT_Z - k)).astype(F32)
-    text_sum = text_sum + lax.ppermute(
-        text_sum.astype(BF16), "z", [(b, a) for a, b in mirror]
-    ).astype(F32)
-    text_sum = text_sum.astype(BF16)
+    for g in text_got:
+        text_sum = text_sum + g.astype(F32)
+    text_round = text_sum.astype(BF16)
+    text_mirror = lax.ppermute(text_round, "z", [(b, a) for a, b in mirror])
+    image_sum = image_part[0].astype(F32)
+    for g in (*image_near, image_far):
+        image_sum = image_sum + g.astype(F32)
+
+    image_round = image_sum.astype(BF16)
+    image_sum = image_sum[0]
+    for k in range(1, 4):
+        image_sum = image_sum + y_move(image_round[k], k).astype(F32)
+    text_sum, text_mirror, image_sum = lax.optimization_barrier(
+        (text_sum, text_mirror, image_sum)
+    )
+    text_sum = (text_sum + text_mirror.astype(F32)).astype(BF16)
     same, cross = text_sum[:, :width], text_sum[:, width:]
-    image_round = image_sum.astype(BF16)
-    got = [
-        y_move(jnp.concatenate([image_round[k], cross if k & 1 else same], axis=0), k)
-        for k in range(1, 4)
-    ]
-    image_sum = image_sum[0]
-    for g in got:
-        image_sum = image_sum + g[:img_half].astype(F32)
-    across, straight, diagonal = [g[img_half:] for g in got]
+    across, straight, diagonal = [y_move(cross if k & 1 else same, k) for k in range(1, 4)]
+    cols = width // 2
+
+    def join_cores(rows):
+        kept = lax.dynamic_slice_in_dim(rows, core * cols, cols, 1)
+        taken = swap(lax.dynamic_slice_in_dim(rows, (1 - core) * cols, cols, 1), "co")
+        return jnp.where(
+            core == 0,
+            jnp.concatenate([kept, taken], axis=0),
+            jnp.concatenate([taken, kept], axis=0),
+        )
+
+    image_rows = image_sum / lax.dynamic_slice_in_dim(image_norm, core * img_half, img_half, 0)
+    image_du = join_cores(image_rows.astype(BF16))
+    du_x = [image_du] + [lax.ppermute(image_du, "x", ring(k)) for k in (1, 3)]
+    across, straight, diagonal, du_x = lax.optimization_barrier(
+        (across, straight, diagonal, du_x)
+    )
+    du_x.insert(2, lax.ppermute(image_du, "x", ring(2)))
+    transposed = (((0,), (0,)), ((), ()))
+
     text_rows = jnp.where(
         yh == 0,
         jnp.concatenate([straight, diagonal, same, across], axis=0),
         jnp.concatenate([diagonal, straight, across, same], axis=0),
     )
-    image_rows = image_sum / lax.dynamic_slice_in_dim(image_norm, core * img_half, img_half, 0)
     text_rows = text_rows.astype(F32) / lax.dynamic_slice_in_dim(
         text_norm, core * txt_half, txt_half, 0
     )
-    text_rows = jnp.where(is_text, text_rows, 0.0)
-    both = jnp.concatenate([image_rows.astype(BF16), text_rows.astype(BF16)], axis=0)
-    cols = width // 2
-    kept = lax.dynamic_slice_in_dim(both, core * cols, cols, 1)
-    taken = swap(lax.dynamic_slice_in_dim(both, (1 - core) * cols, cols, 1), "co")
-    first = jnp.where(core == 0, kept, taken)
-    second = jnp.where(core == 0, taken, kept)
-    image_du = jnp.concatenate([first[:img_half], second[:img_half]], axis=0)
-    text_du = jnp.concatenate([first[img_half:], second[img_half:]], axis=0)
-
-    transposed = (((0,), (0,)), ((), ()))
+    text_du = join_cores(jnp.where(is_text, text_rows, 0.0).astype(BF16))
     text_weight = lax.dot_general(text_hidden, text_du, transposed, preferred_element_type=F32)
     text_share = text_weight.shape[0] // 4
     text_weight = text_weight.reshape(4, text_share, cols)
+    text_weight, du_x = lax.optimization_barrier((text_weight, du_x))
     loss_parts = part_sums[:3, 0]
 
     def small_rows(values, count):
@@ -333,18 +343,19 @@
     tail = small_rows(loss_parts, 16)
     got = [
         lax.ppermute(
-            jnp.concatenate([image_du, pick(text_weight, targets[k]).astype(BF16), tail], axis=0),
+            jnp.concatenate([pick(text_weight, targets[k]).astype(BF16), tail], axis=0),
             "x",
             ring(k),
         )
         for k in range(1, 4)
     ]
-    du_x = jnp.concatenate([image_du] + [g[:img_count] for g in got], axis=0)
+    image_weight = lax.dot_general(
+        jnp.concatenate(hidden_x), jnp.concatenate(du_x), transposed, preferred_element_type=F32
+    )
     text_weight = pick(text_weight, x)
     for g in got:
-        text_weight = text_weight + g[img_count : img_count + text_share].astype(F32)
-        loss_parts = loss_parts + join(g[img_count + text_share :].astype(F32))[:3]
-    image_weight = lax.dot_general(hidden_x, du_x, transposed, preferred_element_type=F32)
+        text_weight = text_weight + g[:text_share].astype(F32)
+        loss_parts = loss_parts + join(g[text_share:].astype(F32))[:3]
 
     img_share, txt_share = share_cols // 16, text_share // 16
     slot = 32
@@ -369,16 +380,12 @@
         used = lax.dynamic_slice_in_dim(weight, start, count, 0).astype(F32)
         return jnp.sum(values * used, axis=1) / lax.dynamic_slice_in_dim(gain, start, count, 0)
 
-    small = jnp.concatenate(
+    gains = jnp.concatenate(
         [
             own(img_weight, img_gain, reduced[:img_share], own_image),
             own(txt_weight, txt_gain, reduced[slot:], own_text),
-            loss_parts,
         ]
     )
-    small = small + swap(small, "co")
-    small = small + swap(small, "yh")
-    gains, loss_parts = small[: img_share + txt_share], small[img_share + txt_share :]
     ready = jnp.concatenate(
         [
             reduced[:img_share].astype(BF16),
@@ -388,16 +395,31 @@
         axis=0,
     )
     gathered = exchange(jnp.broadcast_to(ready, (16, *ready.shape)), ("yl", "z"))
-    pieces = [gathered] + [lax.ppermute(gathered, "x", ring(k)) for k in range(1, 4)]
-    image_grad, text_grad, gains = finish(
-        jnp.stack(sources), pieces, img_weight.shape[0], txt_weight.shape[0]
+    pieces = [lax.ppermute(gathered, "x", ring(k)) for k in (1, 3)]
+
+    count = img_share + txt_share
+    small = jnp.sum(gathered[:, img_share : img_share + 3, :count].astype(F32), axis=1)
+    small = jnp.concatenate([small.reshape(-1), loss_parts])
+    small = small + swap(small, "co")
+    small = small + swap(small, "yh")
+    small, pieces, far = lax.optimization_barrier((small, pieces, gathered))
+    far = lax.ppermute(far, "x", ring(2))
+    gains, loss_parts = small[: 16 * count], small[16 * count :]
+    gains = jnp.stack([gains] + [lax.ppermute(gains, "x", ring(k)) for k in range(1, 4)])
+    gains = jnp.stack([pick(gains, jnp.mod(x - a + 4, 4)) for a in range(4)])
+    gains = gains.reshape(64, count)
+    image_grad, text_grad = finish(
+        jnp.stack(sources),
+        [gathered, pieces[0], far, pieces[1]],
+        img_weight.shape[0],
+        txt_weight.shape[0],
     )
     return (
         loss_parts[0:1] / pair_count,
         image_grad,
         text_grad,
-        gains[:, :, :img_share].reshape(-1),
-        gains[:, :, img_share : img_share + txt_share].reshape(-1),
+        gains[:, :img_share].reshape(-1),
+        gains[:, img_share:].reshape(-1),
         loss_parts[1:2] * logit_scale,
         loss_parts[2:3],
     )

time: 250 us -> 253 us (1.012); the launches traced: 250 us -> 249 us
  starting transfers between devices: 70.7 us -> 90.7 us
  blocking collectives: 16.5 us -> 0 us
  waiting for transfers between devices: 120 us -> 110 us
    ppermute x13 -> x19, waiting for transfers between devices: 58.6 us -> 40 us  [the longest x2 18.3 us: local(): image_near = [lax.ppermute(image_part[k], 'x', ring(-k)) for k in (1, 3)]]
    all_to_all x1 -> x0, blocking collectives: 16.5 us -> none  [exchange(): return lax.all_to_all(value, axes, split_axis=0, concat_axis=0, tiled=True)]
    ppermute x6 -> x9, starting transfers between devices: 9.21 us -> 21.9 us  [y_move(): return lax.ppermute(value, ('yl', 'yh'), [(i, i ^ k) for i in range(4)])]
    all_to_all x1 -> x2, waiting for transfers between devices: 11.9 us -> 23.3 us  [exchange(): return lax.all_to_all(value, axes, split_axis=0, concat_axis=0, tiled=True)]
    ppermute x13 -> x19, starting transfers between devices: 21.9 us -> 31.1 us  [the longest x3 6.43 us: local(): lax.ppermute(rounded[k], 'z', turn(TEXT_Z - k))]
    ppermute x6 -> x9, waiting for transfers between devices: 20.8 us -> 14.3 us  [y_move(): return lax.ppermute(value, ('yl', 'yh'), [(i, i ^ k) for i in range(4)])]
    ppermute x3, starting transfers between devices: 7.05 us -> 1.59 us  [local(): lax.ppermute(slabs, 'x', ring(k))]
    ppermute x3, waiting for transfers between devices: 10.9 us -> 13.7 us  [local(): lax.ppermute(chunk, 'z', turn(k))]
  transfers between devices with their start and end apart: 38 -> 49, of which waited for: 26 -> 30; matrix products, arithmetic and copies ran while one was open for 2% -> 5% of each run, Pallas kernels for 0% -> 0%
where the time goes in v3:
time: 253 us; the launch traced here: 249 us
  waiting for transfers between devices  110 us (43%)
  starting transfers between devices  90.7 us (36%)
  Pallas kernels  15 us (6%)
  other arithmetic  14.2 us (6%)
  local copies, waits for them, and re-layouts  8.57 us (3%)
  between operations  6.68 us (3%)
  matrix products  3.38 us (1%)
    all_to_all x2, waiting for transfers between devices, exchange(): return lax.all_to_all(value, axes, split_axis=0, concat_axis=0, tiled=True)  23.3 us
    ppermute x9, starting transfers between devices, y_move(): return lax.ppermute(value, ('yl', 'yh'), [(i, i ^ k) for i in range(4)])  21.9 us
    ppermute x2, waiting for transfers between devices, local(): image_near = [lax.ppermute(image_part[k], 'x', ring(-k)) for k in (1, 3)]  18.3 us
    all_to_all x2, starting transfers between devices, exchange(): return lax.all_to_all(value, axes, split_axis=0, concat_axis=0, tiled=True)  14.5 us
    ppermute x9, waiting for transfers between devices, y_move(): return lax.ppermute(value, ('yl', 'yh'), [(i, i ^ k) for i in range(4)])  14.3 us
    ppermute x3, waiting for transfers between devices, local(): lax.ppermute(chunk, 'z', turn(k))  13.7 us
    pallas_call x1, Pallas kernels, tile_grads(): pl.pallas_call(tile_kernel, grid=(STEPS,), in_specs=[pl.BlockSpec(memory_...  12.6 us
    ppermute x9, waiting for transfers between devices, swap(): return lax.ppermute(value, axis, [(0, 1), (1, 0)])  9.91 us
  transfers between devices with their start and end apart: 49, of which 30 were waited for; matrix products, arithmetic and copies ran while one was open for 5% of the time, Pallas kernels for 0%

profile of v3, /device:TPU:32, one launch (start us, length us, event | category | flops | bytes accessed | tf_op | source)
XLA Modules:
  0.0 248.7 jit_solution(6549980341920258091)
XLA Ops:
  10.1 2.8 %collective-permute-start.7 = (bf16[256,448]{1,0:T(8,128)(2,1)S(1)}, bf16[256,448]{1,0:T(8,128)(2,1)}, u32[]{:S(2)}, u32[]{:S(2)}) collective-permute-start(bf16[256,448]{1,0:T(8,128)(2,1)S(1)} %get-tuple-element.110), channel_id=1, source_target_pairs={{0,8},{4,12},{8,0},{12,4},{1,9},{5,13},{9,1},{13,5},{2,10},{6,14},... | collective-permute-start | bytes 688136 | tf_op jit(solution)/shard_map/ppermute | solution.py:201
  15.1 3.3 %collective-permute-start.1 = (f32[1024]{0:T(1024)S(1)}, f32[1024]{0:T(1024)S(1)}, u32[]{:S(2)}, u32[]{:S(2)}) collective-permute-start(f32[1024]{0:T(1024)S(1)} %fusion.108), channel_id=1, source_target_pairs={{0,2},{2,0},{1,3},{3,1},{4,6},{6,4},{5,7},{7,5},{8,10},{10,8},{9,1... | collective-permute-start | bytes 12296 | tf_op jit(solution)/shard_map/ppermute | solution.py:26
  22.8 3.3 %collective-permute-start.4 = (bf16[224,512]{1,0:T(8,128)(2,1)S(1)}, bf16[224,512]{1,0:T(8,128)(2,1)S(1)}, u32[]{:S(2)}, u32[]{:S(2)}) collective-permute-start(bf16[224,512]{1,0:T(8,128)(2,1)S(1)} %get-tuple-element.140), channel_id=1, source_target_pairs={{0,2},{2,0},{128,130},{130,128},{1,3},{3,1},{129,131},{131,129},{4... | collective-permute-start | bytes 688136 | tf_op jit(solution)/shard_map/ppermute | solution.py:173
  27.2 5.6 %collective-permute-done.4 = bf16[224,512]{1,0:T(8,128)(2,1)S(1)} collective-permute-done((bf16[224,512]{1,0:T(8,128)(2,1)S(1)}, bf16[224,512]{1,0:T(8,128)(2,1)S(1)}, u32[]{:S(2)}, u32[]{:S(2)}) %collective-permute-start.4) | collective-permute-done | bytes 229408 | tf_op jit(solution)/shard_map/ppermute | solution.py:173
  32.8 4.8 %collective-permute-done.5 = bf16[224,512]{1,0:T(8,128)(2,1)S(1)} collective-permute-done((bf16[224,512]{1,0:T(8,128)(2,1)S(1)}, bf16[224,512]{1,0:T(8,128)(2,1)S(1)}, u32[]{:S(2)}, u32[]{:S(2)}) %collective-permute-start.5) | collective-permute-done | bytes 229408 | tf_op jit(solution)/shard_map/ppermute | solution.py:173
  40.7 9.0 %collective-permute-done.12 = bf16[96,1024]{1,0:T(8,128)(2,1)S(1)} collective-permute-done((bf16[96,1024]{1,0:T(8,128)(2,1)S(1)}, bf16[96,1024]{1,0:T(8,128)(2,1)S(1)}, u32[]{:S(2)}, u32[]{:S(2)}) %collective-permute-start.12) | collective-permute-done | bytes 196640 | tf_op jit(solution)/shard_map/ppermute | solution.py:246
  49.8 4.3 %collective-permute-start.13 = (bf16[96,1024]{1,0:T(8,128)(2,1)S(1)}, bf16[96,1024]{1,0:T(8,128)(2,1)S(1)}, u32[]{:S(2)}, u32[]{:S(2)}) collective-permute-start(bf16[96,1024]{1,0:T(8,128)(2,1)S(1)} %broadcast_select_fusion), channel_id=1, source_target_pairs={{48,32},{32,16},{16,0},{0,48},{64,80},{80,96},{96,112},{112,64},{4... | collective-permute-start | bytes 589832 | tf_op jit(solution)/shard_map/ppermute | solution.py:248
  55.3 2.8 %collective-permute-start.15 = (bf16[96,1024]{1,0:T(8,128)(2,1)S(1)}, bf16[96,1024]{1,0:T(8,128)(2,1)S(1)}, u32[]{:S(2)}, u32[]{:S(2)}) collective-permute-start(bf16[96,1024]{1,0:T(8,128)(2,1)S(1)} %broadcast_select_fusion), channel_id=1, source_target_pairs={{48,0},{32,48},{16,32},{0,16},{64,112},{80,64},{96,80},{112,96},{4... | collective-permute-start | bytes 589832 | tf_op jit(solution)/shard_map/ppermute | solution.py:248
  59.3 9.0 %collective-permute-done.14 = bf16[96,1024]{1,0:T(8,128)(2,1)S(1)} collective-permute-done((bf16[96,1024]{1,0:T(8,128)(2,1)S(1)}, bf16[96,1024]{1,0:T(8,128)(2,1)S(1)}, u32[]{:S(2)}, u32[]{:S(2)}) %collective-permute-start.14) | collective-permute-done | bytes 196640 | tf_op jit(solution)/shard_map/ppermute | solution.py:248
  68.3 3.5 %collective-permute-done.15 = bf16[96,1024]{1,0:T(8,128)(2,1)S(1)} collective-permute-done((bf16[96,1024]{1,0:T(8,128)(2,1)S(1)}, bf16[96,1024]{1,0:T(8,128)(2,1)S(1)}, u32[]{:S(2)}, u32[]{:S(2)}) %collective-permute-start.15) | collective-permute-done | bytes 196640 | tf_op jit(solution)/shard_map/ppermute | solution.py:248
  74.5 12.6 %shard_map.144 = (bf16[16,128,512]{2,1,0:T(8,128)(2,1)S(1)}, bf16[768,1024]{1,0:T(8,128)(2,1)S(1)}, f32[8,128]{1,0:T(8,128)S(1)}) custom-call(f32[4]{0:T(128)S(1)} %pad_maximum_fusion.18.factors, s32[1024,1]{1,0:T(8,128)S(1)} %copy.16.partner, s32[1,768]{1,0:T(1,128)S(1)} %add.424.columns, bf16[16,128,512]{2,1,0:T(8,128)(2,1)S(1)} %constant_dynamic-update-slice_fusion.emb_i, ...), custom_call_target="tpu_custom_call" | custom-call | tf_op jit(solution)/shard_map/pallas_call | solution.py:100
  91.9 2.5 collective-permute-start.18
  99.4 2.2 collective-permute-start.19
  103.7 6.9 %collective-permute-done.21 = bf16[4,128,512]{2,1,0:T(8,128)(2,1)S(1)} collective-permute-done((bf16[4,128,512]{2,1,0:T(8,128)(2,1)}, bf16[4,128,512]{2,1,0:T(8,128)(2,1)S(1)}, u32[]{:S(2)}, u32[]{:S(2)}) %collective-permute-start.21) | collective-permute-done | bytes 524320 | tf_op jit(solution)/shard_map/ppermute | solution.py:278
  110.6 11.4 %collective-permute-done.22 = bf16[4,128,512]{2,1,0:T(8,128)(2,1)} collective-permute-done((bf16[4,128,512]{2,1,0:T(8,128)(2,1)}, bf16[4,128,512]{2,1,0:T(8,128)(2,1)}, u32[]{:S(2)}, u32[]{:S(2)}) %collective-permute-start.22) | collective-permute-done | bytes 524320 | tf_op jit(solution)/shard_map/ppermute | solution.py:278
  123.6 12.3 %collective-permute-start.25 = (bf16[128,512]{1,0:T(8,128)(2,1)S(1)}, bf16[128,512]{1,0:T(8,128)(2,1)S(1)}, u32[]{:S(2)}, u32[]{:S(2)}) collective-permute-start(bf16[128,512]{1,0:T(8,128)(2,1)S(1)} %get-tuple-element.122), channel_id=1, source_target_pairs={{0,2},{2,0},{128,130},{130,128},{1,3},{3,1},{129,131},{131,129},{4... | collective-permute-start | bytes 393224 | tf_op jit(solution)/shard_map/ppermute | solution.py:173
  138.2 2.4 collective-permute-start.24
  144.1 3.2 %collective-permute-start.28 = (bf16[96,512]{1,0:T(8,128)(2,1)S(1)}, bf16[96,512]{1,0:T(8,128)(2,1)S(1)}, u32[]{:S(2)}, u32[]{:S(2)}) collective-permute-start(bf16[96,512]{1,0:T(8,128)(2,1)S(1)} %get-tuple-element.135), channel_id=1, source_target_pairs={{0,2},{2,0},{128,130},{130,128},{1,3},{3,1},{129,131},{131,129},{4... | collective-permute-start | bytes 294920 | tf_op jit(solution)/shard_map/ppermute | solution.py:173
  148.4 3.2 %collective-permute-start.33 = (bf16[256,256]{1,0:T(8,128)(2,1)S(1)}, bf16[256,256]{1,0:T(8,128)(2,1)S(1)}, u32[]{:S(2)}, u32[]{:S(2)}) collective-permute-start(bf16[256,256]{1,0:T(8,128)(2,1)S(1)} %maximum_select_fusion.4), channel_id=1, source_target_pairs={{0,12},{4,0},{8,4},{12,8},{1,13},{5,1},{9,5},{13,9},{2,14},{6,2},{... | collective-permute-start | bytes 393224 | tf_op jit(solution)/shard_map/ppermute | solution.py:314
  157.6 5.3 %collective-permute-done.35 = bf16[256,256]{1,0:T(8,128)(2,1)S(1)} collective-permute-done((bf16[256,256]{1,0:T(8,128)(2,1)S(1)}, bf16[256,256]{1,0:T(8,128)(2,1)S(1)}, u32[]{:S(2)}, u32[]{:S(2)}) %collective-permute-start.35) | collective-permute-done | bytes 131104 | tf_op jit(solution)/shard_map/ppermute | solution.py:318
  165.3 3.9 %collective-permute-start.37 = (bf16[272,256]{1,0:T(8,128)(2,1)S(1)}, bf16[272,256]{1,0:T(8,128)(2,1)S(1)}, u32[]{:S(2)}, u32[]{:S(2)}) collective-permute-start(bf16[272,256]{1,0:T(8,128)(2,1)S(1)} %get-tuple-element.160), channel_id=1, source_target_pairs={{0,8},{4,12},{8,0},{12,4},{1,9},{5,13},{9,1},{13,5},{2,10},{6,14},... | collective-permute-start | bytes 417800 | tf_op jit(solution)/shard_map/ppermute | solution.py:345
  169.6 4.1 %collective-permute-done.37 = bf16[272,256]{1,0:T(8,128)(2,1)S(1)} collective-permute-done((bf16[272,256]{1,0:T(8,128)(2,1)S(1)}, bf16[272,256]{1,0:T(8,128)(2,1)S(1)}, u32[]{:S(2)}, u32[]{:S(2)}) %collective-permute-start.37) | collective-permute-done | bytes 139296 | tf_op jit(solution)/shard_map/ppermute | solution.py:345
  175.8 9.5 %all-to-all-start = ((bf16[16,48,256]{2,1,0:T(8,128)(2,1)}), bf16[16,48,256]{2,1,0:T(8,128)(2,1)S(1)}, u32[]{:S(2)}, u32[]{:S(2)}) async-start(bf16[16,48,256]{2,1,0:T(8,128)(2,1)} %pad_maximum_fusion.4), calls=%async_computation | async-start | bytes 786432 | tf_op jit(solution)/shard_map/all_to_all | solution.py:30
  185.4 11.7 %all-to-all-done = bf16[16,48,256]{2,1,0:T(8,128)(2,1)S(1)} async-done(((bf16[16,48,256]{2,1,0:T(8,128)(2,1)}), bf16[16,48,256]{2,1,0:T(8,128)(2,1)S(1)}, u32[]{:S(2)}, u32[]{:S(2)}) %all-to-all-start) | async-done | bytes 393248 | tf_op jit(solution)/shard_map/all_to_all | solution.py:30
  199.9 5.0 %all-to-all-start.1 = ((bf16[16,48,256]{2,1,0:T(8,128)(2,1)}), bf16[16,48,256]{2,1,0:T(8,128)(2,1)S(1)}, u32[]{:S(2)}, u32[]{:S(2)}) async-start(bf16[16,48,256]{2,1,0:T(8,128)(2,1)} %broadcast_in_dim.9), calls=%async_computation.1 | async-start | bytes 786432 | tf_op jit(solution)/shard_map/all_to_all | solution.py:30
  204.9 11.6 %all-to-all-done.1.first = bf16[16,48,256]{2,1,0:T(8,128)(2,1)S(1)} async-done(((bf16[16,48,256]{2,1,0:T(8,128)(2,1)}), bf16[16,48,256]{2,1,0:T(8,128)(2,1)S(1)}, u32[]{:S(2)}, u32[]{:S(2)}) %all-to-all-start.1) | async-done | bytes 393248 | tf_op jit(solution)/shard_map/all_to_all | solution.py:30
  216.6 2.4 collective-permute-start.41
  222.1 2.2 collective-permute-start.40
  224.4 2.9 %collective-permute-done.40 = f32[707]{0:T(1024)S(1)} collective-permute-done((f32[707]{0:T(1024)S(1)}, f32[707]{0:T(1024)S(1)}, u32[]{:S(2)}, u32[]{:S(2)}) %collective-permute-start.40) | collective-permute-done | bytes 2860 | tf_op jit(solution)/shard_map/ppermute | solution.py:26
  230.0 3.4 %collective-permute-start.45 = (f32[704]{0:T(1024)S(1)}, f32[704]{0:T(1024)S(1)}, u32[]{:S(2)}, u32[]{:S(2)}) collective-permute-start(f32[704]{0:T(1024)S(1)} %bitcast.179), channel_id=1, source_target_pairs={{0,8},{4,12},{8,0},{12,4},{1,9},{5,13},{9,1},{13,5},{2,10},{6,14},... | collective-permute-start | bytes 8456 | tf_op jit(solution)/shard_map/ppermute | solution.py:408
  238.7 5.1 %collective-permute-done.43.third = bf16[16,48,256]{2,1,0:T(8,128)(2,1)S(1)} collective-permute-done((bf16[16,48,256]{2,1,0:T(8,128)(2,1)S(1)}, bf16[16,48,256]{2,1,0:T(8,128)(2,1)S(1)}, u32[]{:S(2)}, u32[]{:S(2)}) %collective-permute-start.43) | collective-permute-done | bytes 393248 | tf_op jit(solution)/shard_map/ppermute | solution.py:406
  243.8 2.4 shard_map.145
  (217 shorter events, 67.5 us)
Async XLA Ops:
  5.1 15.2 %collective-permute-start.2 = (bf16[256,448]{1,0:T(8,128)(2,1)S(1)}, bf16[256,448]{1,0:T(8,128)(2,1)}, u32[]{:S(2)}, u32[]{:S(2)}) collective-permute-start(bf16[256,448]{1,0:T(8,128)(2,1)S(1)} %get-tuple-element.112), channel_id=1, source_target_pairs={{0,4},{4,8},{8,12},{12,0},{1,5},{5,9},{9,13},{13,1},{2,6},{6,10},{... | collective-permute-start | bytes 688136 | tf_op jit(solution)/shard_map/ppermute | solution.py:201
  10.1 17.1 %collective-permute-start.7 = (bf16[256,448]{1,0:T(8,128)(2,1)S(1)}, bf16[256,448]{1,0:T(8,128)(2,1)}, u32[]{:S(2)}, u32[]{:S(2)}) collective-permute-start(bf16[256,448]{1,0:T(8,128)(2,1)S(1)} %get-tuple-element.110), channel_id=1, source_target_pairs={{0,8},{4,12},{8,0},{12,4},{1,9},{5,13},{9,1},{13,5},{2,10},{6,14},... | collective-permute-start | bytes 688136 | tf_op jit(solution)/shard_map/ppermute | solution.py:201
  12.9 14.3 %collective-permute-start.8 = (bf16[256,448]{1,0:T(8,128)(2,1)S(1)}, bf16[256,448]{1,0:T(8,128)(2,1)}, u32[]{:S(2)}, u32[]{:S(2)}) collective-permute-start(bf16[256,448]{1,0:T(8,128)(2,1)S(1)} %get-tuple-element.109), channel_id=1, source_target_pairs={{0,12},{4,0},{8,4},{12,8},{1,13},{5,1},{9,5},{13,9},{2,14},{6,2},{... | collective-permute-start | bytes 688136 | tf_op jit(solution)/shard_map/ppermute | solution.py:201
  22.8 10.0 %collective-permute-start.4 = (bf16[224,512]{1,0:T(8,128)(2,1)S(1)}, bf16[224,512]{1,0:T(8,128)(2,1)S(1)}, u32[]{:S(2)}, u32[]{:S(2)}) collective-permute-start(bf16[224,512]{1,0:T(8,128)(2,1)S(1)} %get-tuple-element.140), channel_id=1, source_target_pairs={{0,2},{2,0},{128,130},{130,128},{1,3},{3,1},{129,131},{131,129},{4... | collective-permute-start | bytes 688136 | tf_op jit(solution)/shard_map/ppermute | solution.py:173
  26.1 11.6 %collective-permute-start.5 = (bf16[224,512]{1,0:T(8,128)(2,1)S(1)}, bf16[224,512]{1,0:T(8,128)(2,1)S(1)}, u32[]{:S(2)}, u32[]{:S(2)}) collective-permute-start(bf16[224,512]{1,0:T(8,128)(2,1)S(1)} %get-tuple-element.139), channel_id=1, source_target_pairs={{0,128},{2,130},{128,0},{130,2},{1,129},{3,131},{129,1},{131,3},{4... | collective-permute-start | bytes 688136 | tf_op jit(solution)/shard_map/ppermute | solution.py:173
  26.8 10.9 %collective-permute-start.6 = (bf16[224,512]{1,0:T(8,128)(2,1)S(1)}, bf16[224,512]{1,0:T(8,128)(2,1)S(1)}, u32[]{:S(2)}, u32[]{:S(2)}) collective-permute-start(bf16[224,512]{1,0:T(8,128)(2,1)S(1)} %get-tuple-element.138), channel_id=1, source_target_pairs={{0,130},{2,128},{128,2},{130,0},{1,131},{3,129},{129,3},{131,1},{4... | collective-permute-start | bytes 688136 | tf_op jit(solution)/shard_map/ppermute | solution.py:173
  37.8 11.9 %collective-permute-start.12 = (bf16[96,1024]{1,0:T(8,128)(2,1)S(1)}, bf16[96,1024]{1,0:T(8,128)(2,1)S(1)}, u32[]{:S(2)}, u32[]{:S(2)}) collective-permute-start(bf16[96,1024]{1,0:T(8,128)(2,1)S(1)} %pad_maximum_fusion.12), channel_id=1, source_target_pairs={{64,48},{80,32},{96,16},{112,0},{65,49},{81,33},{97,17},{113,1},{6... | collective-permute-start | bytes 589832 | tf_op jit(solution)/shard_map/ppermute | solution.py:246
  39.2 32.9 %collective-permute-start.9 = (bf16[4,128,512]{2,1,0:T(8,128)(2,1)S(1)}, bf16[4,128,512]{2,1,0:T(8,128)(2,1)S(1)}, u32[]{:S(2)}, u32[]{:S(2)}) collective-permute-start(bf16[4,128,512]{2,1,0:T(8,128)(2,1)S(1)} %pad_maximum_fusion.3), channel_id=1, source_target_pairs={{0,4},{4,8},{8,12},{12,0},{1,5},{5,9},{9,13},{13,1},{2,6},{6,10},{... | collective-permute-start | bytes 1572872 | tf_op jit(solution)/shard_map/ppermute | solution.py:247
  39.8 32.3 %collective-permute-start.10 = (bf16[4,128,512]{2,1,0:T(8,128)(2,1)S(1)}, bf16[4,128,512]{2,1,0:T(8,128)(2,1)S(1)}, u32[]{:S(2)}, u32[]{:S(2)}) collective-permute-start(bf16[4,128,512]{2,1,0:T(8,128)(2,1)S(1)} %pad_maximum_fusion.3), channel_id=1, source_target_pairs={{0,8},{4,12},{8,0},{12,4},{1,9},{5,13},{9,1},{13,5},{2,10},{6,14},... | collective-permute-start | bytes 1572872 | tf_op jit(solution)/shard_map/ppermute | solution.py:247
  49.8 9.5 %collective-permute-start.13 = (bf16[96,1024]{1,0:T(8,128)(2,1)S(1)}, bf16[96,1024]{1,0:T(8,128)(2,1)S(1)}, u32[]{:S(2)}, u32[]{:S(2)}) collective-permute-start(bf16[96,1024]{1,0:T(8,128)(2,1)S(1)} %broadcast_select_fusion), channel_id=1, source_target_pairs={{48,32},{32,16},{16,0},{0,48},{64,80},{80,96},{96,112},{112,64},{4... | collective-permute-start | bytes 589832 | tf_op jit(solution)/shard_map/ppermute | solution.py:248
  54.1 14.2 %collective-permute-start.14 = (bf16[96,1024]{1,0:T(8,128)(2,1)S(1)}, bf16[96,1024]{1,0:T(8,128)(2,1)S(1)}, u32[]{:S(2)}, u32[]{:S(2)}) collective-permute-start(bf16[96,1024]{1,0:T(8,128)(2,1)S(1)} %broadcast_select_fusion), channel_id=1, source_target_pairs={{48,16},{32,0},{16,48},{0,32},{64,96},{80,112},{96,64},{112,80},{4... | collective-permute-start | bytes 589832 | tf_op jit(solution)/shard_map/ppermute | solution.py:248
  55.3 16.5 %collective-permute-start.15 = (bf16[96,1024]{1,0:T(8,128)(2,1)S(1)}, bf16[96,1024]{1,0:T(8,128)(2,1)S(1)}, u32[]{:S(2)}, u32[]{:S(2)}) collective-permute-start(bf16[96,1024]{1,0:T(8,128)(2,1)S(1)} %broadcast_select_fusion), channel_id=1, source_target_pairs={{48,0},{32,48},{16,32},{0,16},{64,112},{80,64},{96,80},{112,96},{4... | collective-permute-start | bytes 589832 | tf_op jit(solution)/shard_map/ppermute | solution.py:248
  59.3 12.9 %collective-permute-start.11 = (bf16[4,128,512]{2,1,0:T(8,128)(2,1)S(1)}, bf16[4,128,512]{2,1,0:T(8,128)(2,1)S(1)}, u32[]{:S(2)}, u32[]{:S(2)}) collective-permute-start(bf16[4,128,512]{2,1,0:T(8,128)(2,1)S(1)} %pad_maximum_fusion.3), channel_id=1, source_target_pairs={{0,12},{4,0},{8,4},{12,8},{1,13},{5,1},{9,5},{13,9},{2,14},{6,2},{... | collective-permute-start | bytes 1572872 | tf_op jit(solution)/shard_map/ppermute | solution.py:247
  91.9 7.1 %collective-permute-start.18 = (bf16[96,1024]{1,0:T(8,128)(2,1)S(1)}, bf16[96,1024]{1,0:T(8,128)(2,1)}, u32[]{:S(2)}, u32[]{:S(2)}) collective-permute-start(bf16[96,1024]{1,0:T(8,128)(2,1)S(1)} %get-tuple-element.119), channel_id=1, source_target_pairs={{48,0},{32,48},{16,32},{0,16},{64,112},{80,64},{96,80},{112,96},{4... | collective-permute-start | bytes 589832 | tf_op jit(solution)/shard_map/ppermute | solution.py:277
  95.5 15.0 %collective-permute-start.21 = (bf16[4,128,512]{2,1,0:T(8,128)(2,1)}, bf16[4,128,512]{2,1,0:T(8,128)(2,1)S(1)}, u32[]{:S(2)}, u32[]{:S(2)}) collective-permute-start(bf16[4,128,512]{2,1,0:T(8,128)(2,1)} %get-tuple-element.100), channel_id=1, source_target_pairs={{0,12},{4,0},{8,4},{12,8},{1,13},{5,1},{9,5},{13,9},{2,14},{6,2},{... | collective-permute-start | bytes 1572872 | tf_op jit(solution)/shard_map/ppermute | solution.py:278
  95.6 26.4 %collective-permute-start.22 = (bf16[4,128,512]{2,1,0:T(8,128)(2,1)}, bf16[4,128,512]{2,1,0:T(8,128)(2,1)}, u32[]{:S(2)}, u32[]{:S(2)}) collective-permute-start(bf16[4,128,512]{2,1,0:T(8,128)(2,1)} %get-tuple-element.99), channel_id=1, source_target_pairs={{0,4},{4,8},{8,12},{12,0},{1,5},{5,9},{9,13},{13,1},{2,6},{6,10},{... | collective-permute-start | bytes 1572872 | tf_op jit(solution)/shard_map/ppermute | solution.py:278
  98.9 23.1 %collective-permute-start.23 = (bf16[4,128,512]{2,1,0:T(8,128)(2,1)}, bf16[4,128,512]{2,1,0:T(8,128)(2,1)}, u32[]{:S(2)}, u32[]{:S(2)}) collective-permute-start(bf16[4,128,512]{2,1,0:T(8,128)(2,1)} %get-tuple-element.59), channel_id=1, source_target_pairs={{0,8},{4,12},{8,0},{12,4},{1,9},{5,13},{9,1},{13,5},{2,10},{6,14},... | collective-permute-start | bytes 1572872 | tf_op jit(solution)/shard_map/ppermute | solution.py:280
  99.4 22.5 %collective-permute-start.19 = (bf16[96,1024]{1,0:T(8,128)(2,1)}, bf16[96,1024]{1,0:T(8,128)(2,1)}, u32[]{:S(2)}, u32[]{:S(2)}) collective-permute-start(bf16[96,1024]{1,0:T(8,128)(2,1)} %get-tuple-element.118), channel_id=1, source_target_pairs={{48,16},{32,0},{16,48},{0,32},{64,96},{80,112},{96,64},{112,80},{4... | collective-permute-start | bytes 589832 | tf_op jit(solution)/shard_map/ppermute | solution.py:277
  101.6 20.3 %collective-permute-start.20 = (bf16[96,1024]{1,0:T(8,128)(2,1)}, bf16[96,1024]{1,0:T(8,128)(2,1)}, u32[]{:S(2)}, u32[]{:S(2)}) collective-permute-start(bf16[96,1024]{1,0:T(8,128)(2,1)} %get-tuple-element.117), channel_id=1, source_target_pairs={{48,32},{32,16},{16,0},{0,48},{64,80},{80,96},{96,112},{112,64},{4... | collective-permute-start | bytes 589832 | tf_op jit(solution)/shard_map/ppermute | solution.py:277
  123.6 17.1 %collective-permute-start.25 = (bf16[128,512]{1,0:T(8,128)(2,1)S(1)}, bf16[128,512]{1,0:T(8,128)(2,1)S(1)}, u32[]{:S(2)}, u32[]{:S(2)}) collective-permute-start(bf16[128,512]{1,0:T(8,128)(2,1)S(1)} %get-tuple-element.122), channel_id=1, source_target_pairs={{0,2},{2,0},{128,130},{130,128},{1,3},{3,1},{129,131},{131,129},{4... | collective-permute-start | bytes 393224 | tf_op jit(solution)/shard_map/ppermute | solution.py:173
  144.1 7.6 %collective-permute-start.28 = (bf16[96,512]{1,0:T(8,128)(2,1)S(1)}, bf16[96,512]{1,0:T(8,128)(2,1)S(1)}, u32[]{:S(2)}, u32[]{:S(2)}) collective-permute-start(bf16[96,512]{1,0:T(8,128)(2,1)S(1)} %get-tuple-element.135), channel_id=1, source_target_pairs={{0,2},{2,0},{128,130},{130,128},{1,3},{3,1},{129,131},{131,129},{4... | collective-permute-start | bytes 294920 | tf_op jit(solution)/shard_map/ppermute | solution.py:173
  148.3 6.6 %collective-permute-start.32 = (bf16[256,256]{1,0:T(8,128)(2,1)S(1)}, bf16[256,256]{1,0:T(8,128)(2,1)S(1)}, u32[]{:S(2)}, u32[]{:S(2)}) collective-permute-start(bf16[256,256]{1,0:T(8,128)(2,1)S(1)} %maximum_select_fusion.4), channel_id=1, source_target_pairs={{0,4},{4,8},{8,12},{12,0},{1,5},{5,9},{9,13},{13,1},{2,6},{6,10},{... | collective-permute-start | bytes 393224 | tf_op jit(solution)/shard_map/ppermute | solution.py:314
  155.4 7.5 %collective-permute-start.35 = (bf16[256,256]{1,0:T(8,128)(2,1)S(1)}, bf16[256,256]{1,0:T(8,128)(2,1)S(1)}, u32[]{:S(2)}, u32[]{:S(2)}) collective-permute-start(bf16[256,256]{1,0:T(8,128)(2,1)S(1)} %maximum_select_fusion.4), channel_id=1, source_target_pairs={{0,8},{4,12},{8,0},{12,4},{1,9},{5,13},{9,1},{13,5},{2,10},{6,14},... | collective-permute-start | bytes 393224 | tf_op jit(solution)/shard_map/ppermute | solution.py:318
  162.9 6.6 %collective-permute-start.36 = (bf16[272,256]{1,0:T(8,128)(2,1)S(1)}, bf16[272,256]{1,0:T(8,128)(2,1)S(1)}, u32[]{:S(2)}, u32[]{:S(2)}) collective-permute-start(bf16[272,256]{1,0:T(8,128)(2,1)S(1)} %get-tuple-element.159), channel_id=1, source_target_pairs={{0,4},{4,8},{8,12},{12,0},{1,5},{5,9},{9,13},{13,1},{2,6},{6,10},{... | collective-permute-start | bytes 417800 | tf_op jit(solution)/shard_map/ppermute | solution.py:345
  165.3 8.4 %collective-permute-start.37 = (bf16[272,256]{1,0:T(8,128)(2,1)S(1)}, bf16[272,256]{1,0:T(8,128)(2,1)S(1)}, u32[]{:S(2)}, u32[]{:S(2)}) collective-permute-start(bf16[272,256]{1,0:T(8,128)(2,1)S(1)} %get-tuple-element.160), channel_id=1, source_target_pairs={{0,8},{4,12},{8,0},{12,4},{1,9},{5,13},{9,1},{13,5},{2,10},{6,14},... | collective-permute-start | bytes 417800 | tf_op jit(solution)/shard_map/ppermute | solution.py:345
  175.8 21.3 %all-to-all-start = ((bf16[16,48,256]{2,1,0:T(8,128)(2,1)}), bf16[16,48,256]{2,1,0:T(8,128)(2,1)S(1)}, u32[]{:S(2)}, u32[]{:S(2)}) async-start(bf16[16,48,256]{2,1,0:T(8,128)(2,1)} %pad_maximum_fusion.4), calls=%async_computation | async-start | bytes 786432 | tf_op jit(solution)/shard_map/all_to_all | solution.py:30
  199.9 16.6 %all-to-all-start.1 = ((bf16[16,48,256]{2,1,0:T(8,128)(2,1)}), bf16[16,48,256]{2,1,0:T(8,128)(2,1)S(1)}, u32[]{:S(2)}, u32[]{:S(2)}) async-start(bf16[16,48,256]{2,1,0:T(8,128)(2,1)} %broadcast_in_dim.9), calls=%async_computation.1 | async-start | bytes 786432 | tf_op jit(solution)/shard_map/all_to_all | solution.py:30
  216.6 12.0 %collective-permute-start.41 = (bf16[16,48,256]{2,1,0:T(8,128)(2,1)S(1)}, bf16[16,48,256]{2,1,0:T(8,128)(2,1)S(1)}, u32[]{:S(2)}, u32[]{:S(2)}) collective-permute-start(bf16[16,48,256]{2,1,0:T(8,128)(2,1)S(1)} %all-to-all-done.1.first), channel_id=1, source_target_pairs={{0,4},{4,8},{8,12},{12,0},{1,5},{5,9},{9,13},{13,1},{2,6},{6,10},{... | collective-permute-start | bytes 1179656 | tf_op jit(solution)/shard_map/ppermute | solution.py:398
  219.0 9.9 %collective-permute-start.42 = (bf16[16,48,256]{2,1,0:T(8,128)(2,1)S(1)}, bf16[16,48,256]{2,1,0:T(8,128)(2,1)S(1)}, u32[]{:S(2)}, u32[]{:S(2)}) collective-permute-start(bf16[16,48,256]{2,1,0:T(8,128)(2,1)S(1)} %all-to-all-done.1.first), channel_id=1, source_target_pairs={{0,12},{4,0},{8,4},{12,8},{1,13},{5,1},{9,5},{13,9},{2,14},{6,2},{... | collective-permute-start | bytes 1179656 | tf_op jit(solution)/shard_map/ppermute | solution.py:398
  228.8 8.1 %collective-permute-start.44 = (f32[704]{0:T(1024)S(1)}, f32[704]{0:T(1024)S(1)}, u32[]{:S(2)}, u32[]{:S(2)}) collective-permute-start(f32[704]{0:T(1024)S(1)} %bitcast.178), channel_id=1, source_target_pairs={{0,4},{4,8},{8,12},{12,0},{1,5},{5,9},{9,13},{13,1},{2,6},{6,10},{... | collective-permute-start | bytes 8456 | tf_op jit(solution)/shard_map/ppermute | solution.py:408
  230.0 6.9 %collective-permute-start.45 = (f32[704]{0:T(1024)S(1)}, f32[704]{0:T(1024)S(1)}, u32[]{:S(2)}, u32[]{:S(2)}) collective-permute-start(f32[704]{0:T(1024)S(1)} %bitcast.179), channel_id=1, source_target_pairs={{0,8},{4,12},{8,0},{12,4},{1,9},{5,13},{9,1},{13,5},{2,10},{6,14},... | collective-permute-start | bytes 8456 | tf_op jit(solution)/shard_map/ppermute | solution.py:408
  234.4 9.4 %collective-permute-start.43 = (bf16[16,48,256]{2,1,0:T(8,128)(2,1)S(1)}, bf16[16,48,256]{2,1,0:T(8,128)(2,1)S(1)}, u32[]{:S(2)}, u32[]{:S(2)}) collective-permute-start(bf16[16,48,256]{2,1,0:T(8,128)(2,1)S(1)} %all-to-all-done.1.first), channel_id=1, source_target_pairs={{0,8},{4,12},{8,0},{12,4},{1,9},{5,13},{9,1},{13,5},{2,10},{6,14},... | collective-permute-start | bytes 1179656 | tf_op jit(solution)/shard_map/ppermute | solution.py:406
  (30 other events, 188.8 us)

commit v4 on v3

--- a/solution.py
+++ b/solution.py
@@ -197,9 +197,6 @@
     parts = jnp.stack(
         [image_hidden[:, i * share_cols : (i + 1) * share_cols] for i in range(4)]
     )
-    hidden_x = [pick(parts, x)]
-    hidden_x += [lax.ppermute(pick(parts, targets[k]), "x", ring(k)) for k in range(1, 4)]
-
     text_proj = jnp.dot(text_hidden, txt_weight, preferred_element_type=F32)
     image_proj = jnp.dot(image_hidden, img_weight, preferred_element_type=F32)
     squares = jnp.concatenate(
@@ -207,7 +204,6 @@
     )
     squares = squares + swap(squares, "co")
     squares = squares + swap(squares, "yh")
-    squares, hidden_x[1] = lax.optimization_barrier((squares, hidden_x[1]))
     norms = jnp.sqrt(squares + EPS)[:, None]
     text_norm, image_norm = norms[:txt_count], norms[txt_count:]
     text_emb = (text_proj / text_norm).astype(BF16)
@@ -229,6 +225,9 @@
         jnp.concatenate([kept, taken], axis=1),
         jnp.concatenate([taken, kept], axis=1),
     )
+    parts, both = lax.optimization_barrier((parts, both))
+    hidden_x = [pick(parts, x)]
+    hidden_x += [lax.ppermute(pick(parts, targets[k]), "x", ring(k)) for k in range(1, 4)]
     width = both.shape[1]
     image_own = both[:img_half]
     text_own = both[img_half:].reshape(4, piece, width)
@@ -237,7 +236,7 @@
     for k in range(1, 4):
         target = jnp.bitwise_xor(yl * 2 + yh, k)
         got.append(y_move(jnp.concatenate([image_own, pick(text_own, target)], axis=0), k))
-    got, hidden_x = lax.optimization_barrier((got, hidden_x))
+    got, hidden_x[1], hidden_x[3] = lax.optimization_barrier((got, hidden_x[1], hidden_x[3]))
     slabs = jnp.stack([image_own] + [g[:img_half] for g in got])
     mine = jnp.where(yl == 1, pick(text_own, yl * 2 + yh), got[1][img_half:])
     other = jnp.where(yl == 1, got[0][img_half:], got[2][img_half:])
@@ -246,6 +245,7 @@
     chunk = jnp.where(z >= TEXT_Z, chunk, lax.ppermute(chunk, "z", mirror))
     image_all = jnp.concatenate([slabs] + [lax.ppermute(slabs, "x", ring(k)) for k in range(1, 4)])
     chunks = jnp.stack([chunk] + [lax.ppermute(chunk, "z", turn(k)) for k in range(1, TEXT_Z)])
+    chunks, hidden_x[2] = lax.optimization_barrier((chunks, hidden_x[2]))
     text_tile = jnp.stack([chunks, swap(chunks, "co")])
     text_tile = text_tile.reshape(2 * TEXT_Z * piece, 2 * width)
 
@@ -330,7 +330,6 @@
     text_weight = lax.dot_general(text_hidden, text_du, transposed, preferred_element_type=F32)
     text_share = text_weight.shape[0] // 4
     text_weight = text_weight.reshape(4, text_share, cols)
-    text_weight, du_x = lax.optimization_barrier((text_weight, du_x))
     loss_parts = part_sums[:3, 0]
 
     def small_rows(values, count):
@@ -395,22 +394,21 @@
         axis=0,
     )
     gathered = exchange(jnp.broadcast_to(ready, (16, *ready.shape)), ("yl", "z"))
-    pieces = [lax.ppermute(gathered, "x", ring(k)) for k in (1, 3)]
+    pieces = [lax.ppermute(gathered, "x", ring(k)) for k in range(1, 4)]
 
     count = img_share + txt_share
     small = jnp.sum(gathered[:, img_share : img_share + 3, :count].astype(F32), axis=1)
     small = jnp.concatenate([small.reshape(-1), loss_parts])
     small = small + swap(small, "co")
     small = small + swap(small, "yh")
-    small, pieces, far = lax.optimization_barrier((small, pieces, gathered))
-    far = lax.ppermute(far, "x", ring(2))
+    small, pieces[0], pieces[2] = lax.optimization_barrier((small, pieces[0], pieces[2]))
     gains, loss_parts = small[: 16 * count], small[16 * count :]
     gains = jnp.stack([gains] + [lax.ppermute(gains, "x", ring(k)) for k in range(1, 4)])
     gains = jnp.stack([pick(gains, jnp.mod(x - a + 4, 4)) for a in range(4)])
     gains = gains.reshape(64, count)
     image_grad, text_grad = finish(
         jnp.stack(sources),
-        [gathered, pieces[0], far, pieces[1]],
+        [gathered, *pieces],
         img_weight.shape[0],
         txt_weight.shape[0],
     )

time: 253 us -> 263 us (1.040)
  the two profiles are of different devices: /device:TPU:32 before, /device:TPU:34 now
where the time goes in v4:
time: 263 us; the launch traced here: 258 us
  starting transfers between devices  105 us (40%)
  waiting for transfers between devices  105 us (40%)
  Pallas kernels  15 us (6%)
  other arithmetic  14 us (5%)
  local copies, waits for them, and re-layouts  9.45 us (4%)
  between operations  6.79 us (3%)
    all_to_all x2, waiting for transfers between devices, exchange(): return lax.all_to_all(value, axes, split_axis=0, concat_axis=0, tiled=True)  23.8 us
    ppermute x9, starting transfers between devices, y_move(): return lax.ppermute(value, ('yl', 'yh'), [(i, i ^ k) for i in range(4)])  21.1 us
    all_to_all x2, starting transfers between devices, exchange(): return lax.all_to_all(value, axes, split_axis=0, concat_axis=0, tiled=True)  17.3 us
    ppermute x3, waiting for transfers between devices, local(): lax.ppermute(slabs, 'x', ring(k))  13.7 us
    ppermute x3, starting transfers between devices, local(): lax.ppermute(gains, 'x', ring(k))  12.7 us
    pallas_call x1, Pallas kernels, tile_grads(): pl.pallas_call(tile_kernel, grid=(STEPS,), in_specs=[pl.BlockSpec(memory_...  12.6 us
    ppermute x9, waiting for transfers between devices, y_move(): return lax.ppermute(value, ('yl', 'yh'), [(i, i ^ k) for i in range(4)])  9.59 us
    ppermute x3, starting transfers between devices, local(): lax.ppermute(slabs, 'x', ring(k))  9.06 us
  transfers between devices with their start and end apart: 49, of which 34 were waited for; matrix products, arithmetic and copies ran while one was open for 3% of the time, Pallas kernels for 1%

profile of v4, /device:TPU:34, one launch (start us, length us, event | category | flops | bytes accessed | tf_op | source)
XLA Modules:
  0.0 257.9 jit_solution(12888759397826035533)
XLA Ops:
  8.9 3.2 %collective-permute-start.1 = (f32[1024]{0:T(1024)S(1)}, f32[1024]{0:T(1024)S(1)}, u32[]{:S(2)}, u32[]{:S(2)}) collective-permute-start(f32[1024]{0:T(1024)S(1)} %fusion.107), channel_id=1, source_target_pairs={{0,2},{2,0},{1,3},{3,1},{4,6},{6,4},{5,7},{7,5},{8,10},{10,8},{9,1... | collective-permute-start | bytes 12296 | tf_op jit(solution)/shard_map/ppermute | solution.py:26
  16.8 3.3 %collective-permute-start.3 = (bf16[224,512]{1,0:T(8,128)(2,1)S(1)}, bf16[224,512]{1,0:T(8,128)(2,1)S(1)}, u32[]{:S(2)}, u32[]{:S(2)}) collective-permute-start(bf16[224,512]{1,0:T(8,128)(2,1)S(1)} %get-tuple-element.126), channel_id=1, source_target_pairs={{0,2},{2,0},{128,130},{130,128},{1,3},{3,1},{129,131},{131,129},{4... | collective-permute-start | bytes 688136 | tf_op jit(solution)/shard_map/ppermute | solution.py:173
  24.0 2.8 %collective-permute-done.3 = bf16[224,512]{1,0:T(8,128)(2,1)S(1)} collective-permute-done((bf16[224,512]{1,0:T(8,128)(2,1)S(1)}, bf16[224,512]{1,0:T(8,128)(2,1)S(1)}, u32[]{:S(2)}, u32[]{:S(2)}) %collective-permute-start.3) | collective-permute-done | bytes 229408 | tf_op jit(solution)/shard_map/ppermute | solution.py:173
  28.9 2.7 %collective-permute-done.4 = bf16[224,512]{1,0:T(8,128)(2,1)S(1)} collective-permute-done((bf16[224,512]{1,0:T(8,128)(2,1)S(1)}, bf16[224,512]{1,0:T(8,128)(2,1)S(1)}, u32[]{:S(2)}, u32[]{:S(2)}) %collective-permute-start.4) | collective-permute-done | bytes 229408 | tf_op jit(solution)/shard_map/ppermute | solution.py:173
  36.0 9.0 %collective-permute-done.8 = bf16[96,1024]{1,0:T(8,128)(2,1)S(1)} collective-permute-done((bf16[96,1024]{1,0:T(8,128)(2,1)S(1)}, bf16[96,1024]{1,0:T(8,128)(2,1)S(1)}, u32[]{:S(2)}, u32[]{:S(2)}) %collective-permute-start.8) | collective-permute-done | bytes 196640 | tf_op jit(solution)/shard_map/ppermute | solution.py:245
  45.0 4.3 %collective-permute-start.9 = (bf16[96,1024]{1,0:T(8,128)(2,1)S(1)}, bf16[96,1024]{1,0:T(8,128)(2,1)S(1)}, u32[]{:S(2)}, u32[]{:S(2)}) collective-permute-start(bf16[96,1024]{1,0:T(8,128)(2,1)S(1)} %broadcast_select_fusion), channel_id=1, source_target_pairs={{48,32},{32,16},{16,0},{0,48},{64,80},{80,96},{96,112},{112,64},{4... | collective-permute-start | bytes 589832 | tf_op jit(solution)/shard_map/ppermute | solution.py:247
  50.3 3.1 %collective-permute-start.11 = (bf16[96,1024]{1,0:T(8,128)(2,1)S(1)}, bf16[96,1024]{1,0:T(8,128)(2,1)S(1)}, u32[]{:S(2)}, u32[]{:S(2)}) collective-permute-start(bf16[96,1024]{1,0:T(8,128)(2,1)S(1)} %broadcast_select_fusion), channel_id=1, source_target_pairs={{48,0},{32,48},{16,32},{0,16},{64,112},{80,64},{96,80},{112,96},{4... | collective-permute-start | bytes 589832 | tf_op jit(solution)/shard_map/ppermute | solution.py:247
  55.0 7.5 %collective-permute-start.14 = (bf16[4,128,512]{2,1,0:T(8,128)(2,1)S(1)}, bf16[4,128,512]{2,1,0:T(8,128)(2,1)S(1)}, u32[]{:S(2)}, u32[]{:S(2)}) collective-permute-start(bf16[4,128,512]{2,1,0:T(8,128)(2,1)S(1)} %pad_maximum_fusion.3), channel_id=1, source_target_pairs={{0,8},{4,12},{8,0},{12,4},{1,9},{5,13},{9,1},{13,5},{2,10},{6,14},... | collective-permute-start | bytes 1572872 | tf_op jit(solution)/shard_map/ppermute | solution.py:246
  63.6 3.3 %collective-permute-done.11 = bf16[96,1024]{1,0:T(8,128)(2,1)S(1)} collective-permute-done((bf16[96,1024]{1,0:T(8,128)(2,1)S(1)}, bf16[96,1024]{1,0:T(8,128)(2,1)S(1)}, u32[]{:S(2)}, u32[]{:S(2)}) %collective-permute-start.11) | collective-permute-done | bytes 196640 | tf_op jit(solution)/shard_map/ppermute | solution.py:247
  67.2 6.9 %collective-permute-done.14 = bf16[4,128,512]{2,1,0:T(8,128)(2,1)S(1)} collective-permute-done((bf16[4,128,512]{2,1,0:T(8,128)(2,1)S(1)}, bf16[4,128,512]{2,1,0:T(8,128)(2,1)S(1)}, u32[]{:S(2)}, u32[]{:S(2)}) %collective-permute-start.14) | collective-permute-done | bytes 524320 | tf_op jit(solution)/shard_map/ppermute | solution.py:246
  74.1 6.9 %collective-permute-done.15 = bf16[4,128,512]{2,1,0:T(8,128)(2,1)S(1)} collective-permute-done((bf16[4,128,512]{2,1,0:T(8,128)(2,1)S(1)}, bf16[4,128,512]{2,1,0:T(8,128)(2,1)S(1)}, u32[]{:S(2)}, u32[]{:S(2)}) %collective-permute-start.15) | collective-permute-done | bytes 524320 | tf_op jit(solution)/shard_map/ppermute | solution.py:246
  81.1 12.6 %shard_map.144 = (bf16[16,128,512]{2,1,0:T(8,128)(2,1)S(1)}, bf16[768,1024]{1,0:T(8,128)(2,1)S(1)}, f32[8,128]{1,0:T(8,128)S(1)}) custom-call(f32[4]{0:T(128)S(1)} %pad_maximum_fusion.18.factors, s32[1024,1]{1,0:T(8,128)S(1)} %copy.16.partner, s32[1,768]{1,0:T(1,128)S(1)} %add.425.columns, bf16[16,128,512]{2,1,0:T(8,128)(2,1)S(1)} %constant_dynamic-update-slice_fusion.emb_i, ...), custom_call_target="tpu_custom_call" | custom-call | tf_op jit(solution)/shard_map/pallas_call | solution.py:100
  105.6 3.0 %collective-permute-start.19 = (bf16[96,1024]{1,0:T(8,128)(2,1)}, bf16[96,1024]{1,0:T(8,128)(2,1)}, u32[]{:S(2)}, u32[]{:S(2)}) collective-permute-start(bf16[96,1024]{1,0:T(8,128)(2,1)} %get-tuple-element.106), channel_id=1, source_target_pairs={{48,16},{32,0},{16,48},{0,32},{64,96},{80,112},{96,64},{112,80},{4... | collective-permute-start | bytes 589832 | tf_op jit(solution)/shard_map/ppermute | solution.py:277
  109.3 7.4 %collective-permute-done.21 = bf16[4,128,512]{2,1,0:T(8,128)(2,1)S(1)} collective-permute-done((bf16[4,128,512]{2,1,0:T(8,128)(2,1)}, bf16[4,128,512]{2,1,0:T(8,128)(2,1)S(1)}, u32[]{:S(2)}, u32[]{:S(2)}) %collective-permute-start.21) | collective-permute-done | bytes 524320 | tf_op jit(solution)/shard_map/ppermute | solution.py:278
  117.7 2.9 %collective-permute-done.19 = bf16[96,1024]{1,0:T(8,128)(2,1)} collective-permute-done((bf16[96,1024]{1,0:T(8,128)(2,1)}, bf16[96,1024]{1,0:T(8,128)(2,1)}, u32[]{:S(2)}, u32[]{:S(2)}) %collective-permute-start.19) | collective-permute-done | bytes 196640 | tf_op jit(solution)/shard_map/ppermute | solution.py:277
  121.4 5.6 %collective-permute-done.23 = bf16[4,128,512]{2,1,0:T(8,128)(2,1)} collective-permute-done((bf16[4,128,512]{2,1,0:T(8,128)(2,1)}, bf16[4,128,512]{2,1,0:T(8,128)(2,1)}, u32[]{:S(2)}, u32[]{:S(2)}) %collective-permute-start.23) | collective-permute-done | bytes 524320 | tf_op jit(solution)/shard_map/ppermute | solution.py:280
  128.5 10.3 %collective-permute-start.25 = (bf16[128,512]{1,0:T(8,128)(2,1)S(1)}, bf16[128,512]{1,0:T(8,128)(2,1)S(1)}, u32[]{:S(2)}, u32[]{:S(2)}) collective-permute-start(bf16[128,512]{1,0:T(8,128)(2,1)S(1)} %get-tuple-element.108), channel_id=1, source_target_pairs={{0,2},{2,0},{128,130},{130,128},{1,3},{3,1},{129,131},{131,129},{4... | collective-permute-start | bytes 393224 | tf_op jit(solution)/shard_map/ppermute | solution.py:173
  151.4 2.9 %collective-permute-start.32 = (bf16[256,256]{1,0:T(8,128)(2,1)S(1)}, bf16[256,256]{1,0:T(8,128)(2,1)S(1)}, u32[]{:S(2)}, u32[]{:S(2)}) collective-permute-start(bf16[256,256]{1,0:T(8,128)(2,1)S(1)} %maximum_select_fusion.4), channel_id=1, source_target_pairs={{0,4},{4,8},{8,12},{12,0},{1,5},{5,9},{9,13},{13,1},{2,6},{6,10},{... | collective-permute-start | bytes 393224 | tf_op jit(solution)/shard_map/ppermute | solution.py:314
  159.8 3.5 %collective-permute-start.34 = (bf16[256,256]{1,0:T(8,128)(2,1)S(1)}, bf16[256,256]{1,0:T(8,128)(2,1)S(1)}, u32[]{:S(2)}, u32[]{:S(2)}) collective-permute-start(bf16[256,256]{1,0:T(8,128)(2,1)S(1)} %maximum_select_fusion.4), channel_id=1, source_target_pairs={{0,8},{4,12},{8,0},{12,4},{1,9},{5,13},{9,1},{13,5},{2,10},{6,14},... | collective-permute-start | bytes 393224 | tf_op jit(solution)/shard_map/ppermute | solution.py:318
  164.1 3.3 %collective-permute-done.34 = bf16[256,256]{1,0:T(8,128)(2,1)S(1)} collective-permute-done((bf16[256,256]{1,0:T(8,128)(2,1)S(1)}, bf16[256,256]{1,0:T(8,128)(2,1)S(1)}, u32[]{:S(2)}, u32[]{:S(2)}) %collective-permute-start.34) | collective-permute-done | bytes 131104 | tf_op jit(solution)/shard_map/ppermute | solution.py:318
  168.0 3.3 %collective-permute-start.37 = (bf16[272,256]{1,0:T(8,128)(2,1)S(1)}, bf16[272,256]{1,0:T(8,128)(2,1)S(1)}, u32[]{:S(2)}, u32[]{:S(2)}) collective-permute-start(bf16[272,256]{1,0:T(8,128)(2,1)S(1)} %get-tuple-element.146), channel_id=1, source_target_pairs={{0,8},{4,12},{8,0},{12,4},{1,9},{5,13},{9,1},{13,5},{2,10},{6,14},... | collective-permute-start | bytes 417800 | tf_op jit(solution)/shard_map/ppermute | solution.py:344
  171.3 4.8 %collective-permute-done.37 = bf16[272,256]{1,0:T(8,128)(2,1)S(1)} collective-permute-done((bf16[272,256]{1,0:T(8,128)(2,1)S(1)}, bf16[272,256]{1,0:T(8,128)(2,1)S(1)}, u32[]{:S(2)}, u32[]{:S(2)}) %collective-permute-start.37) | collective-permute-done | bytes 139296 | tf_op jit(solution)/shard_map/ppermute | solution.py:344
  178.9 12.3 %all-to-all-start = ((bf16[16,48,256]{2,1,0:T(8,128)(2,1)}), bf16[16,48,256]{2,1,0:T(8,128)(2,1)S(1)}, u32[]{:S(2)}, u32[]{:S(2)}) async-start(bf16[16,48,256]{2,1,0:T(8,128)(2,1)} %pad_maximum_fusion.4), calls=%async_computation | async-start | bytes 786432 | tf_op jit(solution)/shard_map/all_to_all | solution.py:30
  191.2 12.2 %all-to-all-done = bf16[16,48,256]{2,1,0:T(8,128)(2,1)S(1)} async-done(((bf16[16,48,256]{2,1,0:T(8,128)(2,1)}), bf16[16,48,256]{2,1,0:T(8,128)(2,1)S(1)}, u32[]{:S(2)}, u32[]{:S(2)}) %all-to-all-start) | async-done | bytes 393248 | tf_op jit(solution)/shard_map/all_to_all | solution.py:30
  206.2 5.0 %all-to-all-start.1 = ((bf16[16,48,256]{2,1,0:T(8,128)(2,1)}), bf16[16,48,256]{2,1,0:T(8,128)(2,1)S(1)}, u32[]{:S(2)}, u32[]{:S(2)}) async-start(bf16[16,48,256]{2,1,0:T(8,128)(2,1)} %broadcast_in_dim.9), calls=%async_computation.1 | async-start | bytes 786432 | tf_op jit(solution)/shard_map/all_to_all | solution.py:30
  211.2 11.6 %all-to-all-done.1.first = bf16[16,48,256]{2,1,0:T(8,128)(2,1)S(1)} async-done(((bf16[16,48,256]{2,1,0:T(8,128)(2,1)}), bf16[16,48,256]{2,1,0:T(8,128)(2,1)S(1)}, u32[]{:S(2)}, u32[]{:S(2)}) %all-to-all-start.1) | async-done | bytes 393248 | tf_op jit(solution)/shard_map/all_to_all | solution.py:30
  225.3 3.9 %collective-permute-start.43 = (bf16[16,48,256]{2,1,0:T(8,128)(2,1)S(1)}, bf16[16,48,256]{2,1,0:T(8,128)(2,1)S(1)}, u32[]{:S(2)}, u32[]{:S(2)}) collective-permute-start(bf16[16,48,256]{2,1,0:T(8,128)(2,1)S(1)} %all-to-all-done.1.first), channel_id=1, source_target_pairs={{0,8},{4,12},{8,0},{12,4},{1,9},{5,13},{9,1},{13,5},{2,10},{6,14},... | collective-permute-start | bytes 1179656 | tf_op jit(solution)/shard_map/ppermute | solution.py:397
  231.6 2.8 %collective-permute-done.40 = f32[707]{0:T(1024)S(1)} collective-permute-done((f32[707]{0:T(1024)S(1)}, f32[707]{0:T(1024)S(1)}, u32[]{:S(2)}, u32[]{:S(2)}) %collective-permute-start.40) | collective-permute-done | bytes 2860 | tf_op jit(solution)/shard_map/ppermute | solution.py:26
  236.7 2.9 %collective-permute-start.44 = (f32[704]{0:T(1024)S(1)}, f32[704]{0:T(1024)S(1)}, u32[]{:S(2)}, u32[]{:S(2)}) collective-permute-start(f32[704]{0:T(1024)S(1)} %bitcast.178), channel_id=1, source_target_pairs={{0,4},{4,8},{8,12},{12,0},{1,5},{5,9},{9,13},{13,1},{2,6},{6,10},{... | collective-permute-start | bytes 8456 | tf_op jit(solution)/shard_map/ppermute | solution.py:406
  239.6 7.1 %collective-permute-start.45 = (f32[704]{0:T(1024)S(1)}, f32[704]{0:T(1024)S(1)}, u32[]{:S(2)}, u32[]{:S(2)}) collective-permute-start(f32[704]{0:T(1024)S(1)} %bitcast.179), channel_id=1, source_target_pairs={{0,8},{4,12},{8,0},{12,4},{1,9},{5,13},{9,1},{13,5},{2,10},{6,14},... | collective-permute-start | bytes 8456 | tf_op jit(solution)/shard_map/ppermute | solution.py:406
  246.8 2.6 %collective-permute-start.46 = (f32[704]{0:T(1024)S(1)}, f32[704]{0:T(1024)S(1)}, u32[]{:S(2)}, u32[]{:S(2)}) collective-permute-start(f32[704]{0:T(1024)S(1)} %bitcast.180), channel_id=1, source_target_pairs={{0,12},{4,0},{8,4},{12,8},{1,13},{5,1},{9,5},{13,9},{2,14},{6,2},{... | collective-permute-start | bytes 8456 | tf_op jit(solution)/shard_map/ppermute | solution.py:406
  251.3 2.4 shard_map.145
  (230 shorter events, 75.9 us)
Async XLA Ops:
  16.8 10.0 %collective-permute-start.3 = (bf16[224,512]{1,0:T(8,128)(2,1)S(1)}, bf16[224,512]{1,0:T(8,128)(2,1)S(1)}, u32[]{:S(2)}, u32[]{:S(2)}) collective-permute-start(bf16[224,512]{1,0:T(8,128)(2,1)S(1)} %get-tuple-element.126), channel_id=1, source_target_pairs={{0,2},{2,0},{128,130},{130,128},{1,3},{3,1},{129,131},{131,129},{4... | collective-permute-start | bytes 688136 | tf_op jit(solution)/shard_map/ppermute | solution.py:173
  20.1 11.6 %collective-permute-start.4 = (bf16[224,512]{1,0:T(8,128)(2,1)S(1)}, bf16[224,512]{1,0:T(8,128)(2,1)S(1)}, u32[]{:S(2)}, u32[]{:S(2)}) collective-permute-start(bf16[224,512]{1,0:T(8,128)(2,1)S(1)} %get-tuple-element.125), channel_id=1, source_target_pairs={{0,128},{2,130},{128,0},{130,2},{1,129},{3,131},{129,1},{131,3},{4... | collective-permute-start | bytes 688136 | tf_op jit(solution)/shard_map/ppermute | solution.py:173
  20.7 10.9 %collective-permute-start.5 = (bf16[224,512]{1,0:T(8,128)(2,1)S(1)}, bf16[224,512]{1,0:T(8,128)(2,1)S(1)}, u32[]{:S(2)}, u32[]{:S(2)}) collective-permute-start(bf16[224,512]{1,0:T(8,128)(2,1)S(1)} %get-tuple-element.124), channel_id=1, source_target_pairs={{0,130},{2,128},{128,2},{130,0},{1,131},{3,129},{129,3},{131,1},{4... | collective-permute-start | bytes 688136 | tf_op jit(solution)/shard_map/ppermute | solution.py:173
  21.9 9.7 %collective-permute-start.6 = (bf16[256,448]{1,0:T(8,128)(2,1)S(1)}, bf16[256,448]{1,0:T(8,128)(2,1)S(1)}, u32[]{:S(2)}, u32[]{:S(2)}) collective-permute-start(bf16[256,448]{1,0:T(8,128)(2,1)S(1)} %get-tuple-element.97), channel_id=1, source_target_pairs={{0,4},{4,8},{8,12},{12,0},{1,5},{5,9},{9,13},{13,1},{2,6},{6,10},{... | collective-permute-start | bytes 688136 | tf_op jit(solution)/shard_map/ppermute | solution.py:230
  23.4 8.6 %collective-permute-start.7 = (bf16[256,448]{1,0:T(8,128)(2,1)S(1)}, bf16[256,448]{1,0:T(8,128)(2,1)S(1)}, u32[]{:S(2)}, u32[]{:S(2)}) collective-permute-start(bf16[256,448]{1,0:T(8,128)(2,1)S(1)} %get-tuple-element.96), channel_id=1, source_target_pairs={{0,12},{4,0},{8,4},{12,8},{1,13},{5,1},{9,5},{13,9},{2,14},{6,2},{... | collective-permute-start | bytes 688136 | tf_op jit(solution)/shard_map/ppermute | solution.py:230
  26.8 40.2 %collective-permute-start.12 = (bf16[256,448]{1,0:T(8,128)(2,1)S(1)}, bf16[256,448]{1,0:T(8,128)(2,1)S(1)}, u32[]{:S(2)}, u32[]{:S(2)}) collective-permute-start(bf16[256,448]{1,0:T(8,128)(2,1)S(1)} %get-tuple-element.95), channel_id=1, source_target_pairs={{0,8},{4,12},{8,0},{12,4},{1,9},{5,13},{9,1},{13,5},{2,10},{6,14},... | collective-permute-start | bytes 688136 | tf_op jit(solution)/shard_map/ppermute | solution.py:230
  33.1 11.9 %collective-permute-start.8 = (bf16[96,1024]{1,0:T(8,128)(2,1)S(1)}, bf16[96,1024]{1,0:T(8,128)(2,1)S(1)}, u32[]{:S(2)}, u32[]{:S(2)}) collective-permute-start(bf16[96,1024]{1,0:T(8,128)(2,1)S(1)} %pad_maximum_fusion.12), channel_id=1, source_target_pairs={{64,48},{80,32},{96,16},{112,0},{65,49},{81,33},{97,17},{113,1},{6... | collective-permute-start | bytes 589832 | tf_op jit(solution)/shard_map/ppermute | solution.py:245
  34.4 32.7 %collective-permute-start.13 = (bf16[4,128,512]{2,1,0:T(8,128)(2,1)S(1)}, bf16[4,128,512]{2,1,0:T(8,128)(2,1)S(1)}, u32[]{:S(2)}, u32[]{:S(2)}) collective-permute-start(bf16[4,128,512]{2,1,0:T(8,128)(2,1)S(1)} %pad_maximum_fusion.3), channel_id=1, source_target_pairs={{0,4},{4,8},{8,12},{12,0},{1,5},{5,9},{9,13},{13,1},{2,6},{6,10},{... | collective-permute-start | bytes 1572872 | tf_op jit(solution)/shard_map/ppermute | solution.py:246
  45.0 10.0 %collective-permute-start.9 = (bf16[96,1024]{1,0:T(8,128)(2,1)S(1)}, bf16[96,1024]{1,0:T(8,128)(2,1)S(1)}, u32[]{:S(2)}, u32[]{:S(2)}) collective-permute-start(bf16[96,1024]{1,0:T(8,128)(2,1)S(1)} %broadcast_select_fusion), channel_id=1, source_target_pairs={{48,32},{32,16},{16,0},{0,48},{64,80},{80,96},{96,112},{112,64},{4... | collective-permute-start | bytes 589832 | tf_op jit(solution)/shard_map/ppermute | solution.py:247
  49.3 14.2 %collective-permute-start.10 = (bf16[96,1024]{1,0:T(8,128)(2,1)S(1)}, bf16[96,1024]{1,0:T(8,128)(2,1)S(1)}, u32[]{:S(2)}, u32[]{:S(2)}) collective-permute-start(bf16[96,1024]{1,0:T(8,128)(2,1)S(1)} %broadcast_select_fusion), channel_id=1, source_target_pairs={{48,16},{32,0},{16,48},{0,32},{64,96},{80,112},{96,64},{112,80},{4... | collective-permute-start | bytes 589832 | tf_op jit(solution)/shard_map/ppermute | solution.py:247
  50.3 16.5 %collective-permute-start.11 = (bf16[96,1024]{1,0:T(8,128)(2,1)S(1)}, bf16[96,1024]{1,0:T(8,128)(2,1)S(1)}, u32[]{:S(2)}, u32[]{:S(2)}) collective-permute-start(bf16[96,1024]{1,0:T(8,128)(2,1)S(1)} %broadcast_select_fusion), channel_id=1, source_target_pairs={{48,0},{32,48},{16,32},{0,16},{64,112},{80,64},{96,80},{112,96},{4... | collective-permute-start | bytes 589832 | tf_op jit(solution)/shard_map/ppermute | solution.py:247
  55.0 19.0 %collective-permute-start.14 = (bf16[4,128,512]{2,1,0:T(8,128)(2,1)S(1)}, bf16[4,128,512]{2,1,0:T(8,128)(2,1)S(1)}, u32[]{:S(2)}, u32[]{:S(2)}) collective-permute-start(bf16[4,128,512]{2,1,0:T(8,128)(2,1)S(1)} %pad_maximum_fusion.3), channel_id=1, source_target_pairs={{0,8},{4,12},{8,0},{12,4},{1,9},{5,13},{9,1},{13,5},{2,10},{6,14},... | collective-permute-start | bytes 1572872 | tf_op jit(solution)/shard_map/ppermute | solution.py:246
  63.6 17.3 %collective-permute-start.15 = (bf16[4,128,512]{2,1,0:T(8,128)(2,1)S(1)}, bf16[4,128,512]{2,1,0:T(8,128)(2,1)S(1)}, u32[]{:S(2)}, u32[]{:S(2)}) collective-permute-start(bf16[4,128,512]{2,1,0:T(8,128)(2,1)S(1)} %pad_maximum_fusion.3), channel_id=1, source_target_pairs={{0,12},{4,0},{8,4},{12,8},{1,13},{5,1},{9,5},{13,9},{2,14},{6,2},{... | collective-permute-start | bytes 1572872 | tf_op jit(solution)/shard_map/ppermute | solution.py:246
  67.0 14.0 %collective-permute-start.16 = (bf16[4,96,1024]{2,1,0:T(8,128)(2,1)S(1)}, bf16[4,96,1024]{2,1,0:T(8,128)(2,1)S(1)}, u32[]{:S(2)}, u32[]{:S(2)}) collective-permute-start(bf16[4,96,1024]{2,1,0:T(8,128)(2,1)S(1)} %pad_maximum_fusion.2), channel_id=1, source_target_pairs={{0,1},{1,0},{2,3},{3,2},{4,5},{5,4},{6,7},{7,6},{8,9},{9,8},{10,11... | collective-permute-start | bytes 2359304 | tf_op jit(solution)/shard_map/ppermute | solution.py:26
  98.5 7.0 %collective-permute-start.18 = (bf16[96,1024]{1,0:T(8,128)(2,1)S(1)}, bf16[96,1024]{1,0:T(8,128)(2,1)}, u32[]{:S(2)}, u32[]{:S(2)}) collective-permute-start(bf16[96,1024]{1,0:T(8,128)(2,1)S(1)} %get-tuple-element.107), channel_id=1, source_target_pairs={{48,0},{32,48},{16,32},{0,16},{64,112},{80,64},{96,80},{112,96},{4... | collective-permute-start | bytes 589832 | tf_op jit(solution)/shard_map/ppermute | solution.py:277
  101.7 15.0 %collective-permute-start.21 = (bf16[4,128,512]{2,1,0:T(8,128)(2,1)}, bf16[4,128,512]{2,1,0:T(8,128)(2,1)S(1)}, u32[]{:S(2)}, u32[]{:S(2)}) collective-permute-start(bf16[4,128,512]{2,1,0:T(8,128)(2,1)} %get-tuple-element.88), channel_id=1, source_target_pairs={{0,12},{4,0},{8,4},{12,8},{1,13},{5,1},{9,5},{13,9},{2,14},{6,2},{... | collective-permute-start | bytes 1572872 | tf_op jit(solution)/shard_map/ppermute | solution.py:278
  102.5 15.2 %collective-permute-start.22 = (bf16[4,128,512]{2,1,0:T(8,128)(2,1)}, bf16[4,128,512]{2,1,0:T(8,128)(2,1)}, u32[]{:S(2)}, u32[]{:S(2)}) collective-permute-start(bf16[4,128,512]{2,1,0:T(8,128)(2,1)} %get-tuple-element.87), channel_id=1, source_target_pairs={{0,4},{4,8},{8,12},{12,0},{1,5},{5,9},{9,13},{13,1},{2,6},{6,10},{... | collective-permute-start | bytes 1572872 | tf_op jit(solution)/shard_map/ppermute | solution.py:278
  105.6 21.4 %collective-permute-start.23 = (bf16[4,128,512]{2,1,0:T(8,128)(2,1)}, bf16[4,128,512]{2,1,0:T(8,128)(2,1)}, u32[]{:S(2)}, u32[]{:S(2)}) collective-permute-start(bf16[4,128,512]{2,1,0:T(8,128)(2,1)} %get-tuple-element.53), channel_id=1, source_target_pairs={{0,8},{4,12},{8,0},{12,4},{1,9},{5,13},{9,1},{13,5},{2,10},{6,14},... | collective-permute-start | bytes 1572872 | tf_op jit(solution)/shard_map/ppermute | solution.py:280
  105.6 15.1 %collective-permute-start.19 = (bf16[96,1024]{1,0:T(8,128)(2,1)}, bf16[96,1024]{1,0:T(8,128)(2,1)}, u32[]{:S(2)}, u32[]{:S(2)}) collective-permute-start(bf16[96,1024]{1,0:T(8,128)(2,1)} %get-tuple-element.106), channel_id=1, source_target_pairs={{48,16},{32,0},{16,48},{0,32},{64,96},{80,112},{96,64},{112,80},{4... | collective-permute-start | bytes 589832 | tf_op jit(solution)/shard_map/ppermute | solution.py:277
  108.5 12.9 %collective-permute-start.20 = (bf16[96,1024]{1,0:T(8,128)(2,1)}, bf16[96,1024]{1,0:T(8,128)(2,1)}, u32[]{:S(2)}, u32[]{:S(2)}) collective-permute-start(bf16[96,1024]{1,0:T(8,128)(2,1)} %get-tuple-element.105), channel_id=1, source_target_pairs={{48,32},{32,16},{16,0},{0,48},{64,80},{80,96},{96,112},{112,64},{4... | collective-permute-start | bytes 589832 | tf_op jit(solution)/shard_map/ppermute | solution.py:277
  128.5 16.4 %collective-permute-start.25 = (bf16[128,512]{1,0:T(8,128)(2,1)S(1)}, bf16[128,512]{1,0:T(8,128)(2,1)S(1)}, u32[]{:S(2)}, u32[]{:S(2)}) collective-permute-start(bf16[128,512]{1,0:T(8,128)(2,1)S(1)} %get-tuple-element.108), channel_id=1, source_target_pairs={{0,2},{2,0},{128,130},{130,128},{1,3},{3,1},{129,131},{131,129},{4... | collective-permute-start | bytes 393224 | tf_op jit(solution)/shard_map/ppermute | solution.py:173
  159.8 7.6 %collective-permute-start.34 = (bf16[256,256]{1,0:T(8,128)(2,1)S(1)}, bf16[256,256]{1,0:T(8,128)(2,1)S(1)}, u32[]{:S(2)}, u32[]{:S(2)}) collective-permute-start(bf16[256,256]{1,0:T(8,128)(2,1)S(1)} %maximum_select_fusion.4), channel_id=1, source_target_pairs={{0,8},{4,12},{8,0},{12,4},{1,9},{5,13},{9,1},{13,5},{2,10},{6,14},... | collective-permute-start | bytes 393224 | tf_op jit(solution)/shard_map/ppermute | solution.py:318
  164.0 7.3 %collective-permute-start.36 = (bf16[272,256]{1,0:T(8,128)(2,1)S(1)}, bf16[272,256]{1,0:T(8,128)(2,1)S(1)}, u32[]{:S(2)}, u32[]{:S(2)}) collective-permute-start(bf16[272,256]{1,0:T(8,128)(2,1)S(1)} %get-tuple-element.145), channel_id=1, source_target_pairs={{0,4},{4,8},{8,12},{12,0},{1,5},{5,9},{9,13},{13,1},{2,6},{6,10},{... | collective-permute-start | bytes 417800 | tf_op jit(solution)/shard_map/ppermute | solution.py:344
  168.0 8.2 %collective-permute-start.37 = (bf16[272,256]{1,0:T(8,128)(2,1)S(1)}, bf16[272,256]{1,0:T(8,128)(2,1)S(1)}, u32[]{:S(2)}, u32[]{:S(2)}) collective-permute-start(bf16[272,256]{1,0:T(8,128)(2,1)S(1)} %get-tuple-element.146), channel_id=1, source_target_pairs={{0,8},{4,12},{8,0},{12,4},{1,9},{5,13},{9,1},{13,5},{2,10},{6,14},... | collective-permute-start | bytes 417800 | tf_op jit(solution)/shard_map/ppermute | solution.py:344
  178.9 24.5 %all-to-all-start = ((bf16[16,48,256]{2,1,0:T(8,128)(2,1)}), bf16[16,48,256]{2,1,0:T(8,128)(2,1)S(1)}, u32[]{:S(2)}, u32[]{:S(2)}) async-start(bf16[16,48,256]{2,1,0:T(8,128)(2,1)} %pad_maximum_fusion.4), calls=%async_computation | async-start | bytes 786432 | tf_op jit(solution)/shard_map/all_to_all | solution.py:30
  206.2 16.6 %all-to-all-start.1 = ((bf16[16,48,256]{2,1,0:T(8,128)(2,1)}), bf16[16,48,256]{2,1,0:T(8,128)(2,1)S(1)}, u32[]{:S(2)}, u32[]{:S(2)}) async-start(bf16[16,48,256]{2,1,0:T(8,128)(2,1)} %broadcast_in_dim.9), calls=%async_computation.1 | async-start | bytes 786432 | tf_op jit(solution)/shard_map/all_to_all | solution.py:30
  222.9 12.1 %collective-permute-start.41 = (bf16[16,48,256]{2,1,0:T(8,128)(2,1)S(1)}, bf16[16,48,256]{2,1,0:T(8,128)(2,1)S(1)}, u32[]{:S(2)}, u32[]{:S(2)}) collective-permute-start(bf16[16,48,256]{2,1,0:T(8,128)(2,1)S(1)} %all-to-all-done.1.first), channel_id=1, source_target_pairs={{0,4},{4,8},{8,12},{12,0},{1,5},{5,9},{9,13},{13,1},{2,6},{6,10},{... | collective-permute-start | bytes 1179656 | tf_op jit(solution)/shard_map/ppermute | solution.py:397
  223.0 13.7 %collective-permute-start.42 = (bf16[16,48,256]{2,1,0:T(8,128)(2,1)S(1)}, bf16[16,48,256]{2,1,0:T(8,128)(2,1)S(1)}, u32[]{:S(2)}, u32[]{:S(2)}) collective-permute-start(bf16[16,48,256]{2,1,0:T(8,128)(2,1)S(1)} %all-to-all-done.1.first), channel_id=1, source_target_pairs={{0,12},{4,0},{8,4},{12,8},{1,13},{5,1},{9,5},{13,9},{2,14},{6,2},{... | collective-permute-start | bytes 1179656 | tf_op jit(solution)/shard_map/ppermute | solution.py:397
  225.3 26.0 %collective-permute-start.43 = (bf16[16,48,256]{2,1,0:T(8,128)(2,1)S(1)}, bf16[16,48,256]{2,1,0:T(8,128)(2,1)S(1)}, u32[]{:S(2)}, u32[]{:S(2)}) collective-permute-start(bf16[16,48,256]{2,1,0:T(8,128)(2,1)S(1)} %all-to-all-done.1.first), channel_id=1, source_target_pairs={{0,8},{4,12},{8,0},{12,4},{1,9},{5,13},{9,1},{13,5},{2,10},{6,14},... | collective-permute-start | bytes 1179656 | tf_op jit(solution)/shard_map/ppermute | solution.py:397
  236.7 17.0 %collective-permute-start.44 = (f32[704]{0:T(1024)S(1)}, f32[704]{0:T(1024)S(1)}, u32[]{:S(2)}, u32[]{:S(2)}) collective-permute-start(f32[704]{0:T(1024)S(1)} %bitcast.178), channel_id=1, source_target_pairs={{0,4},{4,8},{8,12},{12,0},{1,5},{5,9},{9,13},{13,1},{2,6},{6,10},{... | collective-permute-start | bytes 8456 | tf_op jit(solution)/shard_map/ppermute | solution.py:406
  239.6 14.1 %collective-permute-start.45 = (f32[704]{0:T(1024)S(1)}, f32[704]{0:T(1024)S(1)}, u32[]{:S(2)}, u32[]{:S(2)}) collective-permute-start(f32[704]{0:T(1024)S(1)} %bitcast.179), channel_id=1, source_target_pairs={{0,8},{4,12},{8,0},{12,4},{1,9},{5,13},{9,1},{13,5},{2,10},{6,14},... | collective-permute-start | bytes 8456 | tf_op jit(solution)/shard_map/ppermute | solution.py:406
  246.8 7.0 %collective-permute-start.46 = (f32[704]{0:T(1024)S(1)}, f32[704]{0:T(1024)S(1)}, u32[]{:S(2)}, u32[]{:S(2)}) collective-permute-start(f32[704]{0:T(1024)S(1)} %bitcast.180), channel_id=1, source_target_pairs={{0,12},{4,0},{8,4},{12,8},{1,13},{5,1},{9,5},{13,9},{2,14},{6,2},{... | collective-permute-start | bytes 8456 | tf_op jit(solution)/shard_map/ppermute | solution.py:406
  (37 other events, 221.4 us)

commit v5 on v3

--- a/solution.py
+++ b/solution.py
@@ -276,22 +276,22 @@
     image_part = image_part.reshape(4, 4, img_half, width)
     text_got = [lax.ppermute(rounded[k], "z", turn(TEXT_Z - k)) for k in range(1, TEXT_Z)]
     image_near = [lax.ppermute(image_part[k], "x", ring(-k)) for k in (1, 3)]
-    text_got[0], image_far = lax.optimization_barrier((text_got[0], image_part[2]))
+    text_got[:2], image_far = lax.optimization_barrier((text_got[:2], image_part[2]))
     image_far = lax.ppermute(image_far, "x", ring(-2))
     text_got, image_near, image_far = lax.optimization_barrier((text_got, image_near, image_far))
     text_sum = both[0]
     for g in text_got:
         text_sum = text_sum + g.astype(F32)
     text_round = text_sum.astype(BF16)
-    text_mirror = lax.ppermute(text_round, "z", [(b, a) for a, b in mirror])
     image_sum = image_part[0].astype(F32)
     for g in (*image_near, image_far):
         image_sum = image_sum + g.astype(F32)
 
-    image_round = image_sum.astype(BF16)
+    text_round, image_round = lax.optimization_barrier((text_round, image_sum.astype(BF16)))
     image_sum = image_sum[0]
     for k in range(1, 4):
         image_sum = image_sum + y_move(image_round[k], k).astype(F32)
+    text_mirror = lax.ppermute(text_round, "z", [(b, a) for a, b in mirror])
     text_sum, text_mirror, image_sum = lax.optimization_barrier(
         (text_sum, text_mirror, image_sum)
     )
@@ -311,11 +311,8 @@
 
     image_rows = image_sum / lax.dynamic_slice_in_dim(image_norm, core * img_half, img_half, 0)
     image_du = join_cores(image_rows.astype(BF16))
-    du_x = [image_du] + [lax.ppermute(image_du, "x", ring(k)) for k in (1, 3)]
-    across, straight, diagonal, du_x = lax.optimization_barrier(
-        (across, straight, diagonal, du_x)
-    )
-    du_x.insert(2, lax.ppermute(image_du, "x", ring(2)))
+    straight, image_du = lax.optimization_barrier((straight, image_du))
+    du_x = [image_du] + [lax.ppermute(image_du, "x", ring(k)) for k in range(1, 4)]
     transposed = (((0,), (0,)), ((), ()))
 
     text_rows = jnp.where(
@@ -328,98 +325,86 @@
     )
     text_du = join_cores(jnp.where(is_text, text_rows, 0.0).astype(BF16))
     text_weight = lax.dot_general(text_hidden, text_du, transposed, preferred_element_type=F32)
-    text_share = text_weight.shape[0] // 4
-    text_weight = text_weight.reshape(4, text_share, cols)
-    text_weight, du_x = lax.optimization_barrier((text_weight, du_x))
-    loss_parts = part_sums[:3, 0]
-
-    def small_rows(values, count):
-        rows = jnp.stack(split3(values), axis=0)
-        return jnp.pad(rows, ((0, count - 3), (0, cols - values.shape[0])))
-
-    def join(rows):
-        return rows[0] + rows[1] + rows[2]
-
-    tail = small_rows(loss_parts, 16)
-    got = [
-        lax.ppermute(
-            jnp.concatenate([pick(text_weight, targets[k]).astype(BF16), tail], axis=0),
-            "x",
-            ring(k),
-        )
-        for k in range(1, 4)
-    ]
     image_weight = lax.dot_general(
         jnp.concatenate(hidden_x), jnp.concatenate(du_x), transposed, preferred_element_type=F32
     )
+    text_share = text_weight.shape[0] // 4
+    img_share, txt_share = share_cols // 16, text_share // 16
+    own_weight = lax.dynamic_slice_in_dim(img_weight, x * share_cols, share_cols, 0)
+    own_gain = lax.dynamic_slice_in_dim(img_gain, x * share_cols, share_cols, 0)
+    small = jnp.concatenate(
+        [
+            jnp.sum(image_weight * own_weight.astype(F32), axis=1) / own_gain,
+            jnp.sum(text_weight * txt_weight.astype(F32), axis=1) / txt_gain,
+            part_sums[:3, 0],
+        ]
+    )
+    small = small + swap(small, "co")
+    small = small + swap(small, "yh")
+
+    text_weight = text_weight.reshape(4, text_share, cols)
+    got = [
+        lax.ppermute(pick(text_weight, targets[k]).astype(BF16), "x", ring(k)) for k in range(1, 4)
+    ]
     text_weight = pick(text_weight, x)
     for g in got:
-        text_weight = text_weight + g[:text_share].astype(F32)
-        loss_parts = loss_parts + join(g[text_share:].astype(F32))[:3]
-
-    img_share, txt_share = share_cols // 16, text_share // 16
+        text_weight = text_weight + g.astype(F32)
+
     slot = 32
+    spare = slot - img_share
+    used = img_share + 4 * txt_share
+
+    def spare_rows(values):
+        rows = jnp.stack(split3(values), axis=1)
+        return jnp.pad(rows, ((0, 0), (0, spare - 3), (0, cols - values.shape[1])))
+
+    def joined(blocks):
+        rows = blocks[..., img_share:slot, :].astype(F32)
+        return rows[..., 0, :] + rows[..., 1, :] + rows[..., 2, :]
+
+    sums = jnp.broadcast_to(small[None, share_cols + 4 * text_share :], (16, 3))
+    vector = jnp.concatenate(
+        [
+            small[:share_cols].reshape(16, img_share),
+            small[share_cols : share_cols + 4 * text_share].reshape(16, 4 * txt_share),
+            sums,
+        ],
+        axis=1,
+    )
     block = jnp.concatenate(
         [
             image_weight.astype(BF16).reshape(16, img_share, cols),
-            jnp.broadcast_to(
-                small_rows(loss_parts, slot - img_share), (16, slot - img_share, cols)
-            ),
+            spare_rows(vector),
             text_weight.astype(BF16).reshape(16, txt_share, cols),
         ],
         axis=1,
     )
-    reduced = jnp.sum(exchange(block, ("yl", "z")).astype(F32), axis=0)
-    loss_parts = join(reduced[img_share:slot])[:3]
-    place = yl * Z + z
-    own_image = x * share_cols + place * img_share
-    own_text = x * text_share + place * txt_share
-
-    def own(weight, gain, values, start):
-        count = values.shape[0]
-        used = lax.dynamic_slice_in_dim(weight, start, count, 0).astype(F32)
-        return jnp.sum(values * used, axis=1) / lax.dynamic_slice_in_dim(gain, start, count, 0)
-
-    gains = jnp.concatenate(
-        [
-            own(img_weight, img_gain, reduced[:img_share], own_image),
-            own(txt_weight, txt_gain, reduced[slot:], own_text),
-        ]
-    )
+    reduced = exchange(block, ("yl", "z"))
+    vector = jnp.sum(joined(reduced), axis=0)
+    reduced = jnp.sum(reduced.astype(F32), axis=0)
     ready = jnp.concatenate(
         [
             reduced[:img_share].astype(BF16),
-            small_rows(gains, slot - img_share),
+            spare_rows(vector[None, : used + 3])[0],
             reduced[slot:].astype(BF16),
         ],
         axis=0,
     )
     gathered = exchange(jnp.broadcast_to(ready, (16, *ready.shape)), ("yl", "z"))
-    pieces = [lax.ppermute(gathered, "x", ring(k)) for k in (1, 3)]
-
-    count = img_share + txt_share
-    small = jnp.sum(gathered[:, img_share : img_share + 3, :count].astype(F32), axis=1)
-    small = jnp.concatenate([small.reshape(-1), loss_parts])
-    small = small + swap(small, "co")
-    small = small + swap(small, "yh")
-    small, pieces, far = lax.optimization_barrier((small, pieces, gathered))
-    far = lax.ppermute(far, "x", ring(2))
-    gains, loss_parts = small[: 16 * count], small[16 * count :]
-    gains = jnp.stack([gains] + [lax.ppermute(gains, "x", ring(k)) for k in range(1, 4)])
-    gains = jnp.stack([pick(gains, jnp.mod(x - a + 4, 4)) for a in range(4)])
-    gains = gains.reshape(64, count)
+    pieces = [gathered] + [lax.ppermute(gathered, "x", ring(k)) for k in range(1, 4)]
     image_grad, text_grad = finish(
-        jnp.stack(sources),
-        [gathered, pieces[0], far, pieces[1]],
-        img_weight.shape[0],
-        txt_weight.shape[0],
-    )
+        jnp.stack(sources), pieces, img_weight.shape[0], txt_weight.shape[0]
+    )
+    vectors = jnp.stack([joined(piece) for piece in pieces])
+    total = jnp.sum(vectors[:, :, img_share : used + 3], axis=0)
+    gains = jnp.stack([pick(vectors, jnp.mod(x - a + 4, 4)) for a in range(4)])
+    loss_parts = total[0, 4 * txt_share :]
     return (
         loss_parts[0:1] / pair_count,
         image_grad,
         text_grad,
-        gains[:, :img_share].reshape(-1),
-        gains[:, img_share:].reshape(-1),
+        gains[:, :, :img_share].reshape(-1),
+        total[:, : 4 * txt_share].reshape(-1),
         loss_parts[1:2] * logit_scale,
         loss_parts[2:3],
     )

time: 253 us -> 253 us (level)
  blocking collectives: 0 us -> 22.8 us
  starting transfers between devices: 90.7 us -> 71.3 us
  other arithmetic: 14.2 us -> 9.52 us
    all_to_all x0 -> x1, blocking collectives: none -> 22.8 us  [exchange(): return lax.all_to_all(value, axes, split_axis=0, concat_axis=0, tiled=True)]
    ppermute x2, waiting for transfers between devices: 18.3 us -> 0.01 us  [local(): image_near = [lax.ppermute(image_part[k], 'x', ring(-k)) for k in (1, 3)]]
    ppermute x3, waiting for transfers between devices: 1.36 us -> 14.7 us  [local(): lax.ppermute(rounded[k], 'z', turn(TEXT_Z - k))]
    all_to_all x2 -> x1, waiting for transfers between devices: 23.3 us -> 11.5 us  [exchange(): return lax.all_to_all(value, axes, split_axis=0, concat_axis=0, tiled=True)]
    ppermute x12 -> x9, waiting for transfers between devices: 19.3 us -> 29.2 us  [the longest x3 18.1 us: local(): lax.ppermute(gathered, 'x', ring(k))]
    all_to_all x2 -> x1, starting transfers between devices: 14.5 us -> 5.01 us  [exchange(): return lax.all_to_all(value, axes, split_axis=0, concat_axis=0, tiled=True)]
    ppermute x1, waiting for transfers between devices: 0.01 us -> 7.99 us  [local(): image_far = lax.ppermute(image_far, 'x', ring(-2))]
    ppermute x12 -> x9, starting transfers between devices: 19.8 us -> 12.6 us  [the longest x3 5.3 us: local(): lax.ppermute(gathered, 'x', ring(k))]
  transfers between devices with their start and end apart: 49 -> 45, of which waited for: 30 -> 25; matrix products, arithmetic and copies ran while one was open for 5% -> 4% of each run, Pallas kernels for 0% -> 0%
where the time goes in v5:
time: 253 us; the launch traced here: 248 us
  waiting for transfers between devices  112 us (44%)
  starting transfers between devices  71.3 us (28%)
  blocking collectives  22.8 us (9%)
  Pallas kernels  14.8 us (6%)
  other arithmetic  9.52 us (4%)
  local copies, waits for them, and re-layouts  7.02 us (3%)
  between operations  6.65 us (3%)
  matrix products  3.66 us (1%)
    all_to_all x1, blocking collectives, exchange(): return lax.all_to_all(value, axes, split_axis=0, concat_axis=0, tiled=True)  22.8 us
    ppermute x9, starting transfers between devices, y_move(): return lax.ppermute(value, ('yl', 'yh'), [(i, i ^ k) for i in range(4)])  21.4 us
    ppermute x9, waiting for transfers between devices, y_move(): return lax.ppermute(value, ('yl', 'yh'), [(i, i ^ k) for i in range(4)])  19.1 us
    ppermute x3, waiting for transfers between devices, local(): lax.ppermute(gathered, 'x', ring(k))  18.1 us
    ppermute x3, waiting for transfers between devices, local(): lax.ppermute(rounded[k], 'z', turn(TEXT_Z - k))  14.7 us
    ppermute x3, waiting for transfers between devices, local(): lax.ppermute(chunk, 'z', turn(k))  13.7 us
    pallas_call x1, Pallas kernels, tile_grads(): pl.pallas_call(tile_kernel, grid=(STEPS,), in_specs=[pl.BlockSpec(memory_...  12.3 us
    all_to_all x1, waiting for transfers between devices, exchange(): return lax.all_to_all(value, axes, split_axis=0, concat_axis=0, tiled=True)  11.5 us
  transfers between devices with their start and end apart: 45, of which 25 were waited for; matrix products, arithmetic and copies ran while one was open for 4% of the time, Pallas kernels for 0%

profile of v5, /device:TPU:32, one launch (start us, length us, event | category | flops | bytes accessed | tf_op | source)
XLA Modules:
  0.0 247.9 jit_solution(3816997868734152718)
XLA Ops:
  9.5 2.8 %collective-permute-start.7 = (bf16[256,448]{1,0:T(8,128)(2,1)}, bf16[256,448]{1,0:T(8,128)(2,1)}, u32[]{:S(2)}, u32[]{:S(2)}) collective-permute-start(bf16[256,448]{1,0:T(8,128)(2,1)} %get-tuple-element.88), channel_id=1, source_target_pairs={{0,8},{4,12},{8,0},{12,4},{1,9},{5,13},{9,1},{13,5},{2,10},{6,14},... | collective-permute-start | bytes 688136 | tf_op jit(solution)/shard_map/ppermute | solution.py:201
  14.0 3.3 %collective-permute-start.1 = (f32[1024]{0:T(1024)S(1)}, f32[1024]{0:T(1024)S(1)}, u32[]{:S(2)}, u32[]{:S(2)}) collective-permute-start(f32[1024]{0:T(1024)S(1)} %fusion.91), channel_id=1, source_target_pairs={{0,2},{2,0},{1,3},{3,1},{4,6},{6,4},{5,7},{7,5},{8,10},{10,8},{9,1... | collective-permute-start | bytes 12296 | tf_op jit(solution)/shard_map/ppermute | solution.py:26
  21.6 3.3 %collective-permute-start.4 = (bf16[224,512]{1,0:T(8,128)(2,1)S(1)}, bf16[224,512]{1,0:T(8,128)(2,1)S(1)}, u32[]{:S(2)}, u32[]{:S(2)}) collective-permute-start(bf16[224,512]{1,0:T(8,128)(2,1)S(1)} %get-tuple-element.120), channel_id=1, source_target_pairs={{0,2},{2,0},{128,130},{130,128},{1,3},{3,1},{129,131},{131,129},{4... | collective-permute-start | bytes 688136 | tf_op jit(solution)/shard_map/ppermute | solution.py:173
  26.0 5.6 %collective-permute-done.4 = bf16[224,512]{1,0:T(8,128)(2,1)S(1)} collective-permute-done((bf16[224,512]{1,0:T(8,128)(2,1)S(1)}, bf16[224,512]{1,0:T(8,128)(2,1)S(1)}, u32[]{:S(2)}, u32[]{:S(2)}) %collective-permute-start.4) | collective-permute-done | bytes 229408 | tf_op jit(solution)/shard_map/ppermute | solution.py:173
  31.6 4.9 %collective-permute-done.5 = bf16[224,512]{1,0:T(8,128)(2,1)S(1)} collective-permute-done((bf16[224,512]{1,0:T(8,128)(2,1)S(1)}, bf16[224,512]{1,0:T(8,128)(2,1)S(1)}, u32[]{:S(2)}, u32[]{:S(2)}) %collective-permute-start.5) | collective-permute-done | bytes 229408 | tf_op jit(solution)/shard_map/ppermute | solution.py:173
  39.6 9.0 %collective-permute-done.12 = bf16[96,1024]{1,0:T(8,128)(2,1)S(1)} collective-permute-done((bf16[96,1024]{1,0:T(8,128)(2,1)S(1)}, bf16[96,1024]{1,0:T(8,128)(2,1)S(1)}, u32[]{:S(2)}, u32[]{:S(2)}) %collective-permute-start.12) | collective-permute-done | bytes 196640 | tf_op jit(solution)/shard_map/ppermute | solution.py:246
  48.7 4.3 %collective-permute-start.13 = (bf16[96,1024]{1,0:T(8,128)(2,1)S(1)}, bf16[96,1024]{1,0:T(8,128)(2,1)S(1)}, u32[]{:S(2)}, u32[]{:S(2)}) collective-permute-start(bf16[96,1024]{1,0:T(8,128)(2,1)S(1)} %broadcast_select_fusion), channel_id=1, source_target_pairs={{48,32},{32,16},{16,0},{0,48},{64,80},{80,96},{96,112},{112,64},{4... | collective-permute-start | bytes 589832 | tf_op jit(solution)/shard_map/ppermute | solution.py:248
  54.2 2.8 %collective-permute-start.15 = (bf16[96,1024]{1,0:T(8,128)(2,1)S(1)}, bf16[96,1024]{1,0:T(8,128)(2,1)S(1)}, u32[]{:S(2)}, u32[]{:S(2)}) collective-permute-start(bf16[96,1024]{1,0:T(8,128)(2,1)S(1)} %broadcast_select_fusion), channel_id=1, source_target_pairs={{48,0},{32,48},{16,32},{0,16},{64,112},{80,64},{96,80},{112,96},{4... | collective-permute-start | bytes 589832 | tf_op jit(solution)/shard_map/ppermute | solution.py:248
  58.3 9.0 %collective-permute-done.14 = bf16[96,1024]{1,0:T(8,128)(2,1)S(1)} collective-permute-done((bf16[96,1024]{1,0:T(8,128)(2,1)S(1)}, bf16[96,1024]{1,0:T(8,128)(2,1)S(1)}, u32[]{:S(2)}, u32[]{:S(2)}) %collective-permute-start.14) | collective-permute-done | bytes 196640 | tf_op jit(solution)/shard_map/ppermute | solution.py:248
  67.2 3.5 %collective-permute-done.15 = bf16[96,1024]{1,0:T(8,128)(2,1)S(1)} collective-permute-done((bf16[96,1024]{1,0:T(8,128)(2,1)S(1)}, bf16[96,1024]{1,0:T(8,128)(2,1)S(1)}, u32[]{:S(2)}, u32[]{:S(2)}) %collective-permute-start.15) | collective-permute-done | bytes 196640 | tf_op jit(solution)/shard_map/ppermute | solution.py:248
  71.2 2.1 collective-permute-done.16
  73.4 12.3 %shard_map.144 = (bf16[16,128,512]{2,1,0:T(8,128)(2,1)S(1)}, bf16[768,1024]{1,0:T(8,128)(2,1)S(1)}, f32[8,128]{1,0:T(8,128)S(1)}) custom-call(f32[4]{0:T(128)S(1)} %pad_maximum_fusion.16.factors, s32[1024,1]{1,0:T(8,128)S(1)} %copy.16.partner, s32[1,768]{1,0:T(1,128)S(1)} %add.472.columns, bf16[16,128,512]{2,1,0:T(8,128)(2,1)S(1)} %constant_dynamic-update-slice_fusion.emb_i, ...), custom_call_target="tpu_custom_call" | custom-call | tf_op jit(solution)/shard_map/pallas_call | solution.py:100
  86.1 2.2 collective-permute-done.17
  88.6 2.6 %collective-permute-start.18 = (bf16[96,1024]{1,0:T(8,128)(2,1)S(1)}, bf16[96,1024]{1,0:T(8,128)(2,1)S(1)}, u32[]{:S(2)}, u32[]{:S(2)}) collective-permute-start(bf16[96,1024]{1,0:T(8,128)(2,1)S(1)} %get-tuple-element.97), channel_id=1, source_target_pairs={{48,0},{32,48},{16,32},{0,16},{64,112},{80,64},{96,80},{112,96},{4... | collective-permute-start | bytes 589832 | tf_op jit(solution)/shard_map/ppermute | solution.py:277
  93.5 7.2 %collective-permute-done.18 = bf16[96,1024]{1,0:T(8,128)(2,1)S(1)} collective-permute-done((bf16[96,1024]{1,0:T(8,128)(2,1)S(1)}, bf16[96,1024]{1,0:T(8,128)(2,1)S(1)}, u32[]{:S(2)}, u32[]{:S(2)}) %collective-permute-start.18) | collective-permute-done | bytes 196640 | tf_op jit(solution)/shard_map/ppermute | solution.py:277
  100.7 3.4 %collective-permute-done.19 = bf16[96,1024]{1,0:T(8,128)(2,1)S(1)} collective-permute-done((bf16[96,1024]{1,0:T(8,128)(2,1)S(1)}, bf16[96,1024]{1,0:T(8,128)(2,1)S(1)}, u32[]{:S(2)}, u32[]{:S(2)}) %collective-permute-start.19) | collective-permute-done | bytes 196640 | tf_op jit(solution)/shard_map/ppermute | solution.py:277
  106.7 4.1 %collective-permute-done.20 = bf16[96,1024]{1,0:T(8,128)(2,1)S(1)} collective-permute-done((bf16[96,1024]{1,0:T(8,128)(2,1)S(1)}, bf16[96,1024]{1,0:T(8,128)(2,1)S(1)}, u32[]{:S(2)}, u32[]{:S(2)}) %collective-permute-start.20) | collective-permute-done | bytes 196640 | tf_op jit(solution)/shard_map/ppermute | solution.py:277
  110.7 8.0 %collective-permute-done.23 = bf16[4,128,512]{2,1,0:T(8,128)(2,1)S(1)} collective-permute-done((bf16[4,128,512]{2,1,0:T(8,128)(2,1)S(1)}, bf16[4,128,512]{2,1,0:T(8,128)(2,1)S(1)}, u32[]{:S(2)}, u32[]{:S(2)}) %collective-permute-start.23) | collective-permute-done | bytes 524320 | tf_op jit(solution)/shard_map/ppermute | solution.py:280
  119.9 11.8 %collective-permute-start.25 = (bf16[128,512]{1,0:T(8,128)(2,1)}, bf16[128,512]{1,0:T(8,128)(2,1)}, u32[]{:S(2)}, u32[]{:S(2)}) collective-permute-start(bf16[128,512]{1,0:T(8,128)(2,1)} %get-tuple-element.100), channel_id=1, source_target_pairs={{0,2},{2,0},{128,130},{130,128},{1,3},{3,1},{129,131},{131,129},{4... | collective-permute-start | bytes 393224 | tf_op jit(solution)/shard_map/ppermute | solution.py:173
  133.1 2.4 collective-permute-start.24
  144.6 5.0 %collective-permute-done.28 = bf16[96,512]{1,0:T(8,128)(2,1)S(1)} collective-permute-done((bf16[96,512]{1,0:T(8,128)(2,1)S(1)}, bf16[96,512]{1,0:T(8,128)(2,1)S(1)}, u32[]{:S(2)}, u32[]{:S(2)}) %collective-permute-start.28) | collective-permute-done | bytes 98336 | tf_op jit(solution)/shard_map/ppermute | solution.py:173
  153.5 5.0 %collective-permute-done.30 = bf16[256,256]{1,0:T(8,128)(2,1)S(1)} collective-permute-done((bf16[256,256]{1,0:T(8,128)(2,1)S(1)}, bf16[256,256]{1,0:T(8,128)(2,1)S(1)}, u32[]{:S(2)}, u32[]{:S(2)}) %collective-permute-start.30) | collective-permute-done | bytes 131104 | tf_op jit(solution)/shard_map/ppermute | solution.py:315
  165.6 3.5 %collective-permute-start.39 = (bf16[256,256]{1,0:T(8,128)(2,1)S(1)}, bf16[256,256]{1,0:T(8,128)(2,1)S(1)}, u32[]{:S(2)}, u32[]{:S(2)}) collective-permute-start(bf16[256,256]{1,0:T(8,128)(2,1)S(1)} %get-tuple-element.86), channel_id=1, source_target_pairs={{0,8},{4,12},{8,0},{12,4},{1,9},{5,13},{9,1},{13,5},{2,10},{6,14},... | collective-permute-start | bytes 393224 | tf_op jit(solution)/shard_map/ppermute | solution.py:347
  169.7 2.6 %collective-permute-done.38 = bf16[256,256]{1,0:T(8,128)(2,1)S(1)} collective-permute-done((bf16[256,256]{1,0:T(8,128)(2,1)S(1)}, bf16[256,256]{1,0:T(8,128)(2,1)S(1)}, u32[]{:S(2)}, u32[]{:S(2)}) %collective-permute-start.38) | collective-permute-done | bytes 131104 | tf_op jit(solution)/shard_map/ppermute | solution.py:347
  172.4 2.9 %collective-permute-done.39 = bf16[256,256]{1,0:T(8,128)(2,1)S(1)} collective-permute-done((bf16[256,256]{1,0:T(8,128)(2,1)S(1)}, bf16[256,256]{1,0:T(8,128)(2,1)S(1)}, u32[]{:S(2)}, u32[]{:S(2)}) %collective-permute-start.39) | collective-permute-done | bytes 131104 | tf_op jit(solution)/shard_map/ppermute | solution.py:347
  175.4 22.8 %all_to_all.10 = bf16[16,48,256]{2,1,0:T(8,128)(2,1)S(1)} all-to-all(bf16[16,48,256]{2,1,0:T(8,128)(2,1)S(1)} %pad_maximum_fusion.4), channel_id=1, replica_groups=mesh['yl'=2,'z'=8,'x'=4,'yh'=2,'co'=2] {'yl','z'}, dimensions={0} | all-to-all | bytes 786432 | tf_op jit(solution)/shard_map/all_to_all | solution.py:30
  199.2 5.0 %all-to-all-start.1 = ((bf16[16,48,256]{2,1,0:T(8,128)(2,1)}), bf16[16,48,256]{2,1,0:T(8,128)(2,1)S(1)}, u32[]{:S(2)}, u32[]{:S(2)}) async-start(bf16[16,48,256]{2,1,0:T(8,128)(2,1)} %broadcast_in_dim.9), calls=%async_computation.1 | async-start | bytes 786432 | tf_op jit(solution)/shard_map/all_to_all | solution.py:30
  204.2 11.5 %all-to-all-done.1.first = bf16[16,48,256]{2,1,0:T(8,128)(2,1)S(1)} async-done(((bf16[16,48,256]{2,1,0:T(8,128)(2,1)}), bf16[16,48,256]{2,1,0:T(8,128)(2,1)S(1)}, u32[]{:S(2)}, u32[]{:S(2)}) %all-to-all-start.1) | async-done | bytes 393248 | tf_op jit(solution)/shard_map/all_to_all | solution.py:30
  215.8 4.3 %collective-permute-start.43 = (bf16[16,48,256]{2,1,0:T(8,128)(2,1)S(1)}, bf16[16,48,256]{2,1,0:T(8,128)(2,1)S(1)}, u32[]{:S(2)}, u32[]{:S(2)}) collective-permute-start(bf16[16,48,256]{2,1,0:T(8,128)(2,1)S(1)} %all-to-all-done.1.first), channel_id=1, source_target_pairs={{0,12},{4,0},{8,4},{12,8},{1,13},{5,1},{9,5},{13,9},{2,14},{6,2},{... | collective-permute-start | bytes 1179656 | tf_op jit(solution)/shard_map/ppermute | solution.py:394
  221.1 14.8 %collective-permute-done.43.fourth = bf16[16,48,256]{2,1,0:T(8,128)(2,1)S(1)} collective-permute-done((bf16[16,48,256]{2,1,0:T(8,128)(2,1)S(1)}, bf16[16,48,256]{2,1,0:T(8,128)(2,1)S(1)}, u32[]{:S(2)}, u32[]{:S(2)}) %collective-permute-start.43) | collective-permute-done | bytes 393248 | tf_op jit(solution)/shard_map/ppermute | solution.py:394
  236.1 3.3 %collective-permute-done.41.second = bf16[16,48,256]{2,1,0:T(8,128)(2,1)S(1)} collective-permute-done((bf16[16,48,256]{2,1,0:T(8,128)(2,1)S(1)}, bf16[16,48,256]{2,1,0:T(8,128)(2,1)S(1)}, u32[]{:S(2)}, u32[]{:S(2)}) %collective-permute-start.41) | collective-permute-done | bytes 393248 | tf_op jit(solution)/shard_map/ppermute | solution.py:394
  243.0 2.4 shard_map.145
  (191 shorter events, 53.5 us)
Async XLA Ops:
  5.2 14.0 %collective-permute-start.2 = (bf16[256,448]{1,0:T(8,128)(2,1)}, bf16[256,448]{1,0:T(8,128)(2,1)}, u32[]{:S(2)}, u32[]{:S(2)}) collective-permute-start(bf16[256,448]{1,0:T(8,128)(2,1)} %get-tuple-element.90), channel_id=1, source_target_pairs={{0,4},{4,8},{8,12},{12,0},{1,5},{5,9},{9,13},{13,1},{2,6},{6,10},{... | collective-permute-start | bytes 688136 | tf_op jit(solution)/shard_map/ppermute | solution.py:201
  9.5 16.4 %collective-permute-start.7 = (bf16[256,448]{1,0:T(8,128)(2,1)}, bf16[256,448]{1,0:T(8,128)(2,1)}, u32[]{:S(2)}, u32[]{:S(2)}) collective-permute-start(bf16[256,448]{1,0:T(8,128)(2,1)} %get-tuple-element.88), channel_id=1, source_target_pairs={{0,8},{4,12},{8,0},{12,4},{1,9},{5,13},{9,1},{13,5},{2,10},{6,14},... | collective-permute-start | bytes 688136 | tf_op jit(solution)/shard_map/ppermute | solution.py:201
  12.4 13.6 %collective-permute-start.8 = (bf16[256,448]{1,0:T(8,128)(2,1)}, bf16[256,448]{1,0:T(8,128)(2,1)}, u32[]{:S(2)}, u32[]{:S(2)}) collective-permute-start(bf16[256,448]{1,0:T(8,128)(2,1)} %get-tuple-element.87), channel_id=1, source_target_pairs={{0,12},{4,0},{8,4},{12,8},{1,13},{5,1},{9,5},{13,9},{2,14},{6,2},{... | collective-permute-start | bytes 688136 | tf_op jit(solution)/shard_map/ppermute | solution.py:201
  21.6 10.0 %collective-permute-start.4 = (bf16[224,512]{1,0:T(8,128)(2,1)S(1)}, bf16[224,512]{1,0:T(8,128)(2,1)S(1)}, u32[]{:S(2)}, u32[]{:S(2)}) collective-permute-start(bf16[224,512]{1,0:T(8,128)(2,1)S(1)} %get-tuple-element.120), channel_id=1, source_target_pairs={{0,2},{2,0},{128,130},{130,128},{1,3},{3,1},{129,131},{131,129},{4... | collective-permute-start | bytes 688136 | tf_op jit(solution)/shard_map/ppermute | solution.py:173
  24.9 11.6 %collective-permute-start.5 = (bf16[224,512]{1,0:T(8,128)(2,1)S(1)}, bf16[224,512]{1,0:T(8,128)(2,1)S(1)}, u32[]{:S(2)}, u32[]{:S(2)}) collective-permute-start(bf16[224,512]{1,0:T(8,128)(2,1)S(1)} %get-tuple-element.119), channel_id=1, source_target_pairs={{0,128},{2,130},{128,0},{130,2},{1,129},{3,131},{129,1},{131,3},{4... | collective-permute-start | bytes 688136 | tf_op jit(solution)/shard_map/ppermute | solution.py:173
  25.6 10.9 %collective-permute-start.6 = (bf16[224,512]{1,0:T(8,128)(2,1)S(1)}, bf16[224,512]{1,0:T(8,128)(2,1)S(1)}, u32[]{:S(2)}, u32[]{:S(2)}) collective-permute-start(bf16[224,512]{1,0:T(8,128)(2,1)S(1)} %get-tuple-element.118), channel_id=1, source_target_pairs={{0,130},{2,128},{128,2},{130,0},{1,131},{3,129},{129,3},{131,1},{4... | collective-permute-start | bytes 688136 | tf_op jit(solution)/shard_map/ppermute | solution.py:173
  36.6 12.0 %collective-permute-start.12 = (bf16[96,1024]{1,0:T(8,128)(2,1)S(1)}, bf16[96,1024]{1,0:T(8,128)(2,1)S(1)}, u32[]{:S(2)}, u32[]{:S(2)}) collective-permute-start(bf16[96,1024]{1,0:T(8,128)(2,1)S(1)} %pad_maximum_fusion.9), channel_id=1, source_target_pairs={{64,48},{80,32},{96,16},{112,0},{65,49},{81,33},{97,17},{113,1},{6... | collective-permute-start | bytes 589832 | tf_op jit(solution)/shard_map/ppermute | solution.py:246
  38.0 33.0 %collective-permute-start.9 = (bf16[4,128,512]{2,1,0:T(8,128)(2,1)S(1)}, bf16[4,128,512]{2,1,0:T(8,128)(2,1)S(1)}, u32[]{:S(2)}, u32[]{:S(2)}) collective-permute-start(bf16[4,128,512]{2,1,0:T(8,128)(2,1)S(1)} %pad_maximum_fusion.3), channel_id=1, source_target_pairs={{0,4},{4,8},{8,12},{12,0},{1,5},{5,9},{9,13},{13,1},{2,6},{6,10},{... | collective-permute-start | bytes 1572872 | tf_op jit(solution)/shard_map/ppermute | solution.py:247
  38.7 32.4 %collective-permute-start.10 = (bf16[4,128,512]{2,1,0:T(8,128)(2,1)S(1)}, bf16[4,128,512]{2,1,0:T(8,128)(2,1)S(1)}, u32[]{:S(2)}, u32[]{:S(2)}) collective-permute-start(bf16[4,128,512]{2,1,0:T(8,128)(2,1)S(1)} %pad_maximum_fusion.3), channel_id=1, source_target_pairs={{0,8},{4,12},{8,0},{12,4},{1,9},{5,13},{9,1},{13,5},{2,10},{6,14},... | collective-permute-start | bytes 1572872 | tf_op jit(solution)/shard_map/ppermute | solution.py:247
  48.7 9.6 %collective-permute-start.13 = (bf16[96,1024]{1,0:T(8,128)(2,1)S(1)}, bf16[96,1024]{1,0:T(8,128)(2,1)S(1)}, u32[]{:S(2)}, u32[]{:S(2)}) collective-permute-start(bf16[96,1024]{1,0:T(8,128)(2,1)S(1)} %broadcast_select_fusion), channel_id=1, source_target_pairs={{48,32},{32,16},{16,0},{0,48},{64,80},{80,96},{96,112},{112,64},{4... | collective-permute-start | bytes 589832 | tf_op jit(solution)/shard_map/ppermute | solution.py:248
  53.0 14.3 %collective-permute-start.14 = (bf16[96,1024]{1,0:T(8,128)(2,1)S(1)}, bf16[96,1024]{1,0:T(8,128)(2,1)S(1)}, u32[]{:S(2)}, u32[]{:S(2)}) collective-permute-start(bf16[96,1024]{1,0:T(8,128)(2,1)S(1)} %broadcast_select_fusion), channel_id=1, source_target_pairs={{48,16},{32,0},{16,48},{0,32},{64,96},{80,112},{96,64},{112,80},{4... | collective-permute-start | bytes 589832 | tf_op jit(solution)/shard_map/ppermute | solution.py:248
  54.2 16.5 %collective-permute-start.15 = (bf16[96,1024]{1,0:T(8,128)(2,1)S(1)}, bf16[96,1024]{1,0:T(8,128)(2,1)S(1)}, u32[]{:S(2)}, u32[]{:S(2)}) collective-permute-start(bf16[96,1024]{1,0:T(8,128)(2,1)S(1)} %broadcast_select_fusion), channel_id=1, source_target_pairs={{48,0},{32,48},{16,32},{0,16},{64,112},{80,64},{96,80},{112,96},{4... | collective-permute-start | bytes 589832 | tf_op jit(solution)/shard_map/ppermute | solution.py:248
  58.2 12.9 %collective-permute-start.11 = (bf16[4,128,512]{2,1,0:T(8,128)(2,1)S(1)}, bf16[4,128,512]{2,1,0:T(8,128)(2,1)S(1)}, u32[]{:S(2)}, u32[]{:S(2)}) collective-permute-start(bf16[4,128,512]{2,1,0:T(8,128)(2,1)S(1)} %pad_maximum_fusion.3), channel_id=1, source_target_pairs={{0,12},{4,0},{8,4},{12,8},{1,13},{5,1},{9,5},{13,9},{2,14},{6,2},{... | collective-permute-start | bytes 1572872 | tf_op jit(solution)/shard_map/ppermute | solution.py:247
  88.6 12.0 %collective-permute-start.18 = (bf16[96,1024]{1,0:T(8,128)(2,1)S(1)}, bf16[96,1024]{1,0:T(8,128)(2,1)S(1)}, u32[]{:S(2)}, u32[]{:S(2)}) collective-permute-start(bf16[96,1024]{1,0:T(8,128)(2,1)S(1)} %get-tuple-element.97), channel_id=1, source_target_pairs={{48,0},{32,48},{16,32},{0,16},{64,112},{80,64},{96,80},{112,96},{4... | collective-permute-start | bytes 589832 | tf_op jit(solution)/shard_map/ppermute | solution.py:277
  91.2 12.9 %collective-permute-start.19 = (bf16[96,1024]{1,0:T(8,128)(2,1)S(1)}, bf16[96,1024]{1,0:T(8,128)(2,1)S(1)}, u32[]{:S(2)}, u32[]{:S(2)}) collective-permute-start(bf16[96,1024]{1,0:T(8,128)(2,1)S(1)} %get-tuple-element.96), channel_id=1, source_target_pairs={{48,16},{32,0},{16,48},{0,32},{64,96},{80,112},{96,64},{112,80},{4... | collective-permute-start | bytes 589832 | tf_op jit(solution)/shard_map/ppermute | solution.py:277
  91.4 15.3 %collective-permute-start.21 = (bf16[4,128,512]{2,1,0:T(8,128)(2,1)S(1)}, bf16[4,128,512]{2,1,0:T(8,128)(2,1)S(1)}, u32[]{:S(2)}, u32[]{:S(2)}) collective-permute-start(bf16[4,128,512]{2,1,0:T(8,128)(2,1)S(1)} %get-tuple-element.78), channel_id=1, source_target_pairs={{0,12},{4,0},{8,4},{12,8},{1,13},{5,1},{9,5},{13,9},{2,14},{6,2},{... | collective-permute-start | bytes 1572872 | tf_op jit(solution)/shard_map/ppermute | solution.py:278
  91.8 14.9 %collective-permute-start.22 = (bf16[4,128,512]{2,1,0:T(8,128)(2,1)S(1)}, bf16[4,128,512]{2,1,0:T(8,128)(2,1)S(1)}, u32[]{:S(2)}, u32[]{:S(2)}) collective-permute-start(bf16[4,128,512]{2,1,0:T(8,128)(2,1)S(1)} %get-tuple-element.77), channel_id=1, source_target_pairs={{0,4},{4,8},{8,12},{12,0},{1,5},{5,9},{9,13},{13,1},{2,6},{6,10},{... | collective-permute-start | bytes 1572872 | tf_op jit(solution)/shard_map/ppermute | solution.py:278
  104.1 14.6 %collective-permute-start.23 = (bf16[4,128,512]{2,1,0:T(8,128)(2,1)S(1)}, bf16[4,128,512]{2,1,0:T(8,128)(2,1)S(1)}, u32[]{:S(2)}, u32[]{:S(2)}) collective-permute-start(bf16[4,128,512]{2,1,0:T(8,128)(2,1)S(1)} %get-tuple-element.50), channel_id=1, source_target_pairs={{0,8},{4,12},{8,0},{12,4},{1,9},{5,13},{9,1},{13,5},{2,10},{6,14},... | collective-permute-start | bytes 1572872 | tf_op jit(solution)/shard_map/ppermute | solution.py:280
  119.9 16.2 %collective-permute-start.25 = (bf16[128,512]{1,0:T(8,128)(2,1)}, bf16[128,512]{1,0:T(8,128)(2,1)}, u32[]{:S(2)}, u32[]{:S(2)}) collective-permute-start(bf16[128,512]{1,0:T(8,128)(2,1)} %get-tuple-element.100), channel_id=1, source_target_pairs={{0,2},{2,0},{128,130},{130,128},{1,3},{3,1},{129,131},{131,129},{4... | collective-permute-start | bytes 393224 | tf_op jit(solution)/shard_map/ppermute | solution.py:173
  133.1 7.0 %collective-permute-start.24 = (bf16[96,1024]{1,0:T(8,128)(2,1)S(1)}, bf16[96,1024]{1,0:T(8,128)(2,1)S(1)}, u32[]{:S(2)}, u32[]{:S(2)}) collective-permute-start(bf16[96,1024]{1,0:T(8,128)(2,1)S(1)} %get-tuple-element.57), channel_id=1, source_target_pairs={{48,64},{32,80},{16,96},{0,112},{49,65},{33,81},{17,97},{1,113},{5... | collective-permute-start | bytes 589832 | tf_op jit(solution)/shard_map/ppermute | solution.py:294
  140.4 12.7 %collective-permute-start.33 = (bf16[96,512]{1,0:T(8,128)(2,1)S(1)}, bf16[96,512]{1,0:T(8,128)(2,1)S(1)}, u32[]{:S(2)}, u32[]{:S(2)}) collective-permute-start(bf16[96,512]{1,0:T(8,128)(2,1)S(1)} %get-tuple-element.115), channel_id=1, source_target_pairs={{0,130},{2,128},{128,2},{130,0},{1,131},{3,129},{129,3},{131,1},{4... | collective-permute-start | bytes 294920 | tf_op jit(solution)/shard_map/ppermute | solution.py:173
  141.9 11.1 %collective-permute-start.34 = (bf16[96,512]{1,0:T(8,128)(2,1)S(1)}, bf16[96,512]{1,0:T(8,128)(2,1)S(1)}, u32[]{:S(2)}, u32[]{:S(2)}) collective-permute-start(bf16[96,512]{1,0:T(8,128)(2,1)S(1)} %get-tuple-element.115), channel_id=1, source_target_pairs={{0,2},{2,0},{128,130},{130,128},{1,3},{3,1},{129,131},{131,129},{4... | collective-permute-start | bytes 294920 | tf_op jit(solution)/shard_map/ppermute | solution.py:173
  149.6 8.8 %collective-permute-start.30 = (bf16[256,256]{1,0:T(8,128)(2,1)S(1)}, bf16[256,256]{1,0:T(8,128)(2,1)S(1)}, u32[]{:S(2)}, u32[]{:S(2)}) collective-permute-start(bf16[256,256]{1,0:T(8,128)(2,1)S(1)} %maximum_select_fusion.4), channel_id=1, source_target_pairs={{0,4},{4,8},{8,12},{12,0},{1,5},{5,9},{9,13},{13,1},{2,6},{6,10},{... | collective-permute-start | bytes 393224 | tf_op jit(solution)/shard_map/ppermute | solution.py:315
  150.2 8.2 %collective-permute-start.31 = (bf16[256,256]{1,0:T(8,128)(2,1)S(1)}, bf16[256,256]{1,0:T(8,128)(2,1)S(1)}, u32[]{:S(2)}, u32[]{:S(2)}) collective-permute-start(bf16[256,256]{1,0:T(8,128)(2,1)S(1)} %maximum_select_fusion.4), channel_id=1, source_target_pairs={{0,8},{4,12},{8,0},{12,4},{1,9},{5,13},{9,1},{13,5},{2,10},{6,14},... | collective-permute-start | bytes 393224 | tf_op jit(solution)/shard_map/ppermute | solution.py:315
  151.3 7.7 %collective-permute-start.32 = (bf16[256,256]{1,0:T(8,128)(2,1)S(1)}, bf16[256,256]{1,0:T(8,128)(2,1)S(1)}, u32[]{:S(2)}, u32[]{:S(2)}) collective-permute-start(bf16[256,256]{1,0:T(8,128)(2,1)S(1)} %maximum_select_fusion.4), channel_id=1, source_target_pairs={{0,12},{4,0},{8,4},{12,8},{1,13},{5,1},{9,5},{13,9},{2,14},{6,2},{... | collective-permute-start | bytes 393224 | tf_op jit(solution)/shard_map/ppermute | solution.py:315
  153.4 8.2 %collective-permute-start.35 = (bf16[384,256]{1,0:T(8,128)(2,1)S(1)}, bf16[384,256]{1,0:T(8,128)(2,1)S(1)}, u32[]{:S(2)}, u32[]{:S(2)}) collective-permute-start(bf16[384,256]{1,0:T(8,128)(2,1)S(1)} %get-tuple-element.108), channel_id=1, source_target_pairs={{0,1},{1,0},{2,3},{3,2},{4,5},{5,4},{6,7},{7,6},{8,9},{9,8},{10,11... | collective-permute-start | bytes 589832 | tf_op jit(solution)/shard_map/ppermute | solution.py:26
  165.3 7.1 %collective-permute-start.38 = (bf16[256,256]{1,0:T(8,128)(2,1)S(1)}, bf16[256,256]{1,0:T(8,128)(2,1)S(1)}, u32[]{:S(2)}, u32[]{:S(2)}) collective-permute-start(bf16[256,256]{1,0:T(8,128)(2,1)S(1)} %get-tuple-element.84), channel_id=1, source_target_pairs={{0,4},{4,8},{8,12},{12,0},{1,5},{5,9},{9,13},{13,1},{2,6},{6,10},{... | collective-permute-start | bytes 393224 | tf_op jit(solution)/shard_map/ppermute | solution.py:347
  165.6 9.6 %collective-permute-start.39 = (bf16[256,256]{1,0:T(8,128)(2,1)S(1)}, bf16[256,256]{1,0:T(8,128)(2,1)S(1)}, u32[]{:S(2)}, u32[]{:S(2)}) collective-permute-start(bf16[256,256]{1,0:T(8,128)(2,1)S(1)} %get-tuple-element.86), channel_id=1, source_target_pairs={{0,8},{4,12},{8,0},{12,4},{1,9},{5,13},{9,1},{13,5},{2,10},{6,14},... | collective-permute-start | bytes 393224 | tf_op jit(solution)/shard_map/ppermute | solution.py:347
  199.2 16.6 %all-to-all-start.1 = ((bf16[16,48,256]{2,1,0:T(8,128)(2,1)}), bf16[16,48,256]{2,1,0:T(8,128)(2,1)S(1)}, u32[]{:S(2)}, u32[]{:S(2)}) async-start(bf16[16,48,256]{2,1,0:T(8,128)(2,1)} %broadcast_in_dim.9), calls=%async_computation.1 | async-start | bytes 786432 | tf_op jit(solution)/shard_map/all_to_all | solution.py:30
  215.8 20.2 %collective-permute-start.43 = (bf16[16,48,256]{2,1,0:T(8,128)(2,1)S(1)}, bf16[16,48,256]{2,1,0:T(8,128)(2,1)S(1)}, u32[]{:S(2)}, u32[]{:S(2)}) collective-permute-start(bf16[16,48,256]{2,1,0:T(8,128)(2,1)S(1)} %all-to-all-done.1.first), channel_id=1, source_target_pairs={{0,12},{4,0},{8,4},{12,8},{1,13},{5,1},{9,5},{13,9},{2,14},{6,2},{... | collective-permute-start | bytes 1179656 | tf_op jit(solution)/shard_map/ppermute | solution.py:394
  220.1 15.9 %collective-permute-start.42 = (bf16[16,48,256]{2,1,0:T(8,128)(2,1)S(1)}, bf16[16,48,256]{2,1,0:T(8,128)(2,1)S(1)}, u32[]{:S(2)}, u32[]{:S(2)}) collective-permute-start(bf16[16,48,256]{2,1,0:T(8,128)(2,1)S(1)} %all-to-all-done.1.first), channel_id=1, source_target_pairs={{0,8},{4,12},{8,0},{12,4},{1,9},{5,13},{9,1},{13,5},{2,10},{6,14},... | collective-permute-start | bytes 1179656 | tf_op jit(solution)/shard_map/ppermute | solution.py:394
  220.1 19.3 %collective-permute-start.41 = (bf16[16,48,256]{2,1,0:T(8,128)(2,1)S(1)}, bf16[16,48,256]{2,1,0:T(8,128)(2,1)S(1)}, u32[]{:S(2)}, u32[]{:S(2)}) collective-permute-start(bf16[16,48,256]{2,1,0:T(8,128)(2,1)S(1)} %all-to-all-done.1.first), channel_id=1, source_target_pairs={{0,4},{4,8},{8,12},{12,0},{1,5},{5,9},{9,13},{13,1},{2,6},{6,10},{... | collective-permute-start | bytes 1179656 | tf_op jit(solution)/shard_map/ppermute | solution.py:394
  (19 other events, 80.9 us)

commit v6 on v5

--- a/solution.py
+++ b/solution.py
@@ -11,7 +11,6 @@
 Z = 8
 TEXT_Z = 4
 DP = ("yl", "z", "x")
-STEPS = 4
 
 
 def hidden_rows(features, gain_vec):
@@ -37,81 +36,89 @@
     return high, middle, (rest - middle.astype(F32)).astype(BF16)
 
 
+def tile_rows(emb_i, i):
+    base = 4 * i
+    return jnp.concatenate(
+        [
+            jnp.concatenate([emb_i[base], emb_i[base + 1]], axis=1),
+            jnp.concatenate([emb_i[base + 2], emb_i[base + 3]], axis=1),
+        ],
+        axis=0,
+    )
+
+
 def tile_kernel(
     factors, partner, columns, emb_i, emb_t, out_i, out_t, out_s, acc, sums
 ):
-    step = pl.program_id(0)
     scale, shift = factors[0], factors[1]
-
-    @pl.when(step == 0)
-    def _():
-        acc[...] = jnp.zeros_like(acc)
-        sums[...] = jnp.zeros_like(sums)
-
-    rows = jnp.concatenate(
-        [
-            jnp.concatenate([emb_i[0], emb_i[1]], axis=1),
-            jnp.concatenate([emb_i[2], emb_i[3]], axis=1),
-        ],
-        axis=0,
-    )
-    texts = emb_t[...]
-    high = emb_i.shape[1]
-    half = emb_i.shape[2]
+    high, half = emb_i.shape[1], emb_i.shape[2]
     place = lax.broadcasted_iota(jnp.int32, (2 * high, 1), 0)
     weight = jnp.where(place < high, factors[2], factors[3])
-    similar = lax.dot_general(rows, texts, (((1,), (1,)), ((), ())), preferred_element_type=F32)
-    logits = scale * similar + shift
-    pair = partner[...] == columns[...]
-    signed = jnp.where(pair, -logits, logits)
-    small = jnp.exp(-jnp.abs(signed))
-    total = 1.0 + small
-    inverse = 1.0 / total
-    sigmoid = jnp.where(signed >= 0, inverse, small * inverse)
-    soft = jnp.maximum(signed, 0.0) + jnp.log(total) + (small - (total - 1.0)) * inverse
-    grad = jnp.where(pair, -sigmoid, sigmoid) * weight
-    sums[0:1] += jnp.sum(soft * weight, axis=0, keepdims=True)
-    sums[1:2] += jnp.sum(grad * similar, axis=0, keepdims=True)
-    sums[2:3] += jnp.sum(grad, axis=0, keepdims=True)
-    rounded = grad.astype(BF16)
-    acc[...] += lax.dot_general(rounded, rows, (((0,), (0,)), ((), ())), preferred_element_type=F32)
-    grad_rows = jnp.dot(rounded, texts, preferred_element_type=F32)
-    wide = rows.astype(F32)
-    inner = jnp.sum(wide * grad_rows, axis=1, keepdims=True)
-    result = (scale * (grad_rows - wide * inner)).astype(BF16)
-    out_i[0] = result[:high, :half]
-    out_i[1] = result[:high, half:]
-    out_i[2] = result[high:, :half]
-    out_i[3] = result[high:, half:]
-
-    @pl.when(step == STEPS - 1)
-    def _():
-        texts = emb_t[...].astype(F32)
-        grads = acc[...]
-        inner = jnp.sum(texts * grads, axis=1, keepdims=True)
-        out_t[...] = (scale * (grads - texts * inner)).astype(BF16)
-        out_s[...] = jnp.broadcast_to(jnp.sum(sums[...], axis=1, keepdims=True), out_s.shape)
+    nt = (((1,), (1,)), ((), ()))
+    tn = (((0,), (0,)), ((), ()))
+
+    def grads(similar, i):
+        logits = scale * similar + shift
+        pair = partner[2 * high * i : 2 * high * (i + 1)] == columns[...]
+        signed = jnp.where(pair, -logits, logits)
+        small = jnp.exp(-jnp.abs(signed))
+        total = 1.0 + small
+        inverse = 1.0 / total
+        sigmoid = jnp.where(signed >= 0, inverse, small * inverse)
+        soft = jnp.maximum(signed, 0.0) + jnp.log(total) + (small - (total - 1.0)) * inverse
+        grad = jnp.where(pair, -sigmoid, sigmoid) * weight
+        parts = [
+            jnp.sum(soft * weight, axis=0, keepdims=True),
+            jnp.sum(grad * similar, axis=0, keepdims=True),
+            jnp.sum(grad, axis=0, keepdims=True),
+        ]
+        for j, part in enumerate(parts):
+            if i == 0:
+                sums[j : j + 1] = part
+            else:
+                sums[j : j + 1] += part
+        return grad.astype(BF16)
+
+    def finish_rows(rounded, rows, i):
+        update = lax.dot_general(rounded, rows, tn, preferred_element_type=F32)
+        if i == 0:
+            acc[...] = update
+        else:
+            acc[...] += update
+        grad_rows = jnp.dot(rounded, emb_t[...], preferred_element_type=F32)
+        wide = rows.astype(F32)
+        inner = jnp.sum(wide * grad_rows, axis=1, keepdims=True)
+        result = (scale * (grad_rows - wide * inner)).astype(BF16)
+        out_i[4 * i] = result[:high, :half]
+        out_i[4 * i + 1] = result[:high, half:]
+        out_i[4 * i + 2] = result[high:, :half]
+        out_i[4 * i + 3] = result[high:, half:]
+
+    rows = tile_rows(emb_i, 0)
+    similar = lax.dot_general(rows, emb_t[...], nt, preferred_element_type=F32)
+    for i in range(4):
+        if i < 3:
+            later = tile_rows(emb_i, i + 1)
+            ahead = lax.dot_general(later, emb_t[...], nt, preferred_element_type=F32)
+        rounded = grads(similar, i)
+        finish_rows(rounded, rows, i)
+        if i < 3:
+            rows, similar = later, ahead
+    sums[3:] = jnp.zeros_like(sums[3:])
+    texts = emb_t[...].astype(F32)
+    grads_t = acc[...]
+    inner = jnp.sum(texts * grads_t, axis=1, keepdims=True)
+    out_t[...] = (scale * (grads_t - texts * inner)).astype(BF16)
+    out_s[...] = jnp.broadcast_to(jnp.sum(sums[...], axis=1, keepdims=True), out_s.shape)
 
 
 def tile_grads(factors, partner, columns, emb_i, emb_t):
-    slabs, high, half = emb_i.shape
-    block = slabs // STEPS
     count, width = emb_t.shape
+    whole = pl.BlockSpec(memory_space=pltpu.VMEM)
     return pl.pallas_call(
         tile_kernel,
-        grid=(STEPS,),
-        in_specs=[
-            pl.BlockSpec(memory_space=pltpu.SMEM),
-            pl.BlockSpec((partner.shape[0] // STEPS, 1), lambda i: (i, 0)),
-            pl.BlockSpec((1, count), lambda i: (0, 0)),
-            pl.BlockSpec((block, high, half), lambda i: (i, 0, 0)),
-            pl.BlockSpec((count, width), lambda i: (0, 0)),
-        ],
-        out_specs=[
-            pl.BlockSpec((block, high, half), lambda i: (i, 0, 0)),
-            pl.BlockSpec((count, width), lambda i: (0, 0)),
-            pl.BlockSpec((8, 128), lambda i: (0, 0)),
-        ],
+        in_specs=[pl.BlockSpec(memory_space=pltpu.SMEM)] + [whole] * 4,
+        out_specs=[whole] * 3,
         out_shape=[
             jax.ShapeDtypeStruct(emb_i.shape, BF16),
             jax.ShapeDtypeStruct(emb_t.shape, BF16),
@@ -134,7 +141,7 @@
     ]
 
 
-def finish_kernel(places, first, second, third, fourth, out_i, out_t, rows):
+def finish_kernel(places, first, second, third, fourth, out_i, out_t, out_g, rows):
     image_rows = rows.shape[0] // 16
     text_rows = out_t.shape[0] // 64
     padded = first.shape[1] - text_rows
@@ -145,6 +152,8 @@
             rows[s * image_rows : (s + 1) * image_rows] = values[:image_rows]
             start = pl.multiple_of(place * (16 * text_rows) + s * text_rows, 8)
             out_t[pl.ds(start, text_rows)] = values[padded:]
+            tail = values[image_rows:padded]
+            out_g[place, s : s + 1] = tail[0:1] + tail[1:2] + tail[2:3]
         start = pl.multiple_of(place * (16 * image_rows), 8)
         out_i[pl.ds(start, 16 * image_rows)] = rows[...]
 
@@ -155,10 +164,11 @@
     return pl.pallas_call(
         finish_kernel,
         in_specs=[pl.BlockSpec(memory_space=pltpu.SMEM)] + [whole] * 4,
-        out_specs=[whole] * 2,
+        out_specs=[whole] * 3,
         out_shape=[
             jax.ShapeDtypeStruct((image_total, cols), F32),
             jax.ShapeDtypeStruct((text_total, cols), F32),
+            jax.ShapeDtypeStruct((4, 16, cols), F32),
         ],
         scratch_shapes=[pltpu.VMEM((image_total // 4, cols), F32)],
         compiler_params=pltpu.CompilerParams(vmem_limit_bytes=24 * 1024 * 1024),
@@ -325,27 +335,28 @@
     )
     text_du = join_cores(jnp.where(is_text, text_rows, 0.0).astype(BF16))
     text_weight = lax.dot_general(text_hidden, text_du, transposed, preferred_element_type=F32)
+    text_share = text_weight.shape[0] // 4
+    text_whole = text_weight
+    text_weight = text_weight.reshape(4, text_share, cols)
+    got = [
+        lax.ppermute(pick(text_weight, targets[k]).astype(BF16), "x", ring(k)) for k in range(1, 4)
+    ]
+    got[0], du_x = lax.optimization_barrier((got[0], du_x))
     image_weight = lax.dot_general(
         jnp.concatenate(hidden_x), jnp.concatenate(du_x), transposed, preferred_element_type=F32
     )
-    text_share = text_weight.shape[0] // 4
     img_share, txt_share = share_cols // 16, text_share // 16
     own_weight = lax.dynamic_slice_in_dim(img_weight, x * share_cols, share_cols, 0)
     own_gain = lax.dynamic_slice_in_dim(img_gain, x * share_cols, share_cols, 0)
     small = jnp.concatenate(
         [
             jnp.sum(image_weight * own_weight.astype(F32), axis=1) / own_gain,
-            jnp.sum(text_weight * txt_weight.astype(F32), axis=1) / txt_gain,
+            jnp.sum(text_whole * txt_weight.astype(F32), axis=1) / txt_gain,
             part_sums[:3, 0],
         ]
     )
     small = small + swap(small, "co")
     small = small + swap(small, "yh")
-
-    text_weight = text_weight.reshape(4, text_share, cols)
-    got = [
-        lax.ppermute(pick(text_weight, targets[k]).astype(BF16), "x", ring(k)) for k in range(1, 4)
-    ]
     text_weight = pick(text_weight, x)
     for g in got:
         text_weight = text_weight + g.astype(F32)
@@ -392,18 +403,16 @@
     )
     gathered = exchange(jnp.broadcast_to(ready, (16, *ready.shape)), ("yl", "z"))
     pieces = [gathered] + [lax.ppermute(gathered, "x", ring(k)) for k in range(1, 4)]
-    image_grad, text_grad = finish(
+    image_grad, text_grad, vectors = finish(
         jnp.stack(sources), pieces, img_weight.shape[0], txt_weight.shape[0]
     )
-    vectors = jnp.stack([joined(piece) for piece in pieces])
     total = jnp.sum(vectors[:, :, img_share : used + 3], axis=0)
-    gains = jnp.stack([pick(vectors, jnp.mod(x - a + 4, 4)) for a in range(4)])
     loss_parts = total[0, 4 * txt_share :]
     return (
         loss_parts[0:1] / pair_count,
         image_grad,
         text_grad,
-        gains[:, :, :img_share].reshape(-1),
+        vectors[:, :, :img_share].reshape(-1),
         total[:, : 4 * txt_share].reshape(-1),
         loss_parts[1:2] * logit_scale,
         loss_parts[2:3],

time: 253 us -> 243 us (0.960)
  waiting for transfers between devices: 112 us -> 93.3 us
  blocking collectives: 22.8 us -> 37.3 us
  Pallas kernels: 14.8 us -> 11.3 us
  starting transfers between devices: 71.3 us -> 68 us
    all_to_all x1 -> x2, blocking collectives: 22.8 us -> 37.3 us  [exchange(): return lax.all_to_all(value, axes, split_axis=0, concat_axis=0, tiled=True)]
    ppermute x2, waiting for transfers between devices: 0.01 us -> 12.4 us  [local(): image_near = [lax.ppermute(image_part[k], 'x', ring(-k)) for k in (1, 3)]]
    all_to_all x1 -> x0, waiting for transfers between devices: 11.5 us -> none  [exchange(): return lax.all_to_all(value, axes, split_axis=0, concat_axis=0, tiled=True)]
    ppermute x3, starting transfers between devices: 4.63 us -> 15.5 us  [local(): lax.ppermute(rounded[k], 'z', turn(TEXT_Z - k))]
    ppermute x1, waiting for transfers between devices: 7.99 us -> 0.01 us  [local(): image_far = lax.ppermute(image_far, 'x', ring(-2))]
    ppermute x9, starting transfers between devices: 21.4 us -> 13.6 us  [y_move(): return lax.ppermute(value, ('yl', 'yh'), [(i, i ^ k) for i in range(4)])]
    ppermute x3, waiting for transfers between devices: 14.7 us -> 8.63 us  [local(): lax.ppermute(rounded[k], 'z', turn(TEXT_Z - k))]
    all_to_all x1 -> x0, starting transfers between devices: 5.01 us -> none  [exchange(): return lax.all_to_all(value, axes, split_axis=0, concat_axis=0, tiled=True)]
  transfers between devices with their start and end apart: 45 -> 44, of which waited for: 25 -> 23; matrix products, arithmetic and copies ran while one was open for 4% -> 4% of each run, Pallas kernels for 0% -> 0%
where the time goes in v6:
time: 243 us; the launch traced here: 239 us
  waiting for transfers between devices  93.3 us (38%)
  starting transfers between devices  68 us (28%)
  blocking collectives  37.3 us (15%)
  Pallas kernels  11.3 us (5%)
  other arithmetic  11.2 us (5%)
  between operations  6.54 us (3%)
  local copies, waits for them, and re-layouts  6.47 us (3%)
  matrix products  4.44 us (2%)
    all_to_all x2, blocking collectives, exchange(): return lax.all_to_all(value, axes, split_axis=0, concat_axis=0, tiled=True)  37.3 us
    ppermute x9, waiting for transfers between devices, y_move(): return lax.ppermute(value, ('yl', 'yh'), [(i, i ^ k) for i in range(4)])  16.7 us
    ppermute x3, waiting for transfers between devices, local(): lax.ppermute(gathered, 'x', ring(k))  16.3 us
    ppermute x3, waiting for transfers between devices, local(): lax.ppermute(chunk, 'z', turn(k))  16.1 us
    ppermute x3, starting transfers between devices, local(): lax.ppermute(rounded[k], 'z', turn(TEXT_Z - k))  15.5 us
    ppermute x9, starting transfers between devices, y_move(): return lax.ppermute(value, ('yl', 'yh'), [(i, i ^ k) for i in range(4)])  13.6 us
    ppermute x2, waiting for transfers between devices, local(): image_near = [lax.ppermute(image_part[k], 'x', ring(-k)) for k in (1, 3)]  12.4 us
    ppermute x9, waiting for transfers between devices, swap(): return lax.ppermute(value, axis, [(0, 1), (1, 0)])  9.9 us
  transfers between devices with their start and end apart: 44, of which 23 were waited for; matrix products, arithmetic and copies ran while one was open for 4% of the time, Pallas kernels for 0%

profile of v6, /device:TPU:32, one launch (start us, length us, event | category | flops | bytes accessed | tf_op | source)
XLA Modules:
  0.0 238.6 jit_solution(4262987321685805740)
XLA Ops:
  0.7 2.0 convert_reduce_fusion
  12.4 2.7 %collective-permute-start.7 = (bf16[256,448]{1,0:T(8,128)(2,1)}, bf16[256,448]{1,0:T(8,128)(2,1)}, u32[]{:S(2)}, u32[]{:S(2)}) collective-permute-start(bf16[256,448]{1,0:T(8,128)(2,1)} %get-tuple-element.100), channel_id=1, source_target_pairs={{0,8},{4,12},{8,0},{12,4},{1,9},{5,13},{9,1},{13,5},{2,10},{6,14},... | collective-permute-start | bytes 688136 | tf_op jit(solution)/shard_map/ppermute | solution.py:211
  17.5 3.2 %collective-permute-start.1 = (f32[1024]{0:T(1024)S(1)}, f32[1024]{0:T(1024)S(1)}, u32[]{:S(2)}, u32[]{:S(2)}) collective-permute-start(f32[1024]{0:T(1024)S(1)} %fusion.87), channel_id=1, source_target_pairs={{0,2},{2,0},{1,3},{3,1},{4,6},{6,4},{5,7},{7,5},{8,10},{10,8},{9,1... | collective-permute-start | bytes 12296 | tf_op jit(solution)/shard_map/ppermute | solution.py:25
  24.9 3.3 %collective-permute-start.4 = (bf16[224,512]{1,0:T(8,128)(2,1)S(1)}, bf16[224,512]{1,0:T(8,128)(2,1)S(1)}, u32[]{:S(2)}, u32[]{:S(2)}) collective-permute-start(bf16[224,512]{1,0:T(8,128)(2,1)S(1)} %get-tuple-element.132), channel_id=1, source_target_pairs={{0,2},{2,0},{128,130},{130,128},{1,3},{3,1},{129,131},{131,129},{4... | collective-permute-start | bytes 688136 | tf_op jit(solution)/shard_map/ppermute | solution.py:183
  29.3 5.7 %collective-permute-done.4 = bf16[224,512]{1,0:T(8,128)(2,1)S(1)} collective-permute-done((bf16[224,512]{1,0:T(8,128)(2,1)S(1)}, bf16[224,512]{1,0:T(8,128)(2,1)S(1)}, u32[]{:S(2)}, u32[]{:S(2)}) %collective-permute-start.4) | collective-permute-done | bytes 229408 | tf_op jit(solution)/shard_map/ppermute | solution.py:183
  35.0 4.5 %collective-permute-done.5 = bf16[224,512]{1,0:T(8,128)(2,1)S(1)} collective-permute-done((bf16[224,512]{1,0:T(8,128)(2,1)S(1)}, bf16[224,512]{1,0:T(8,128)(2,1)S(1)}, u32[]{:S(2)}, u32[]{:S(2)}) %collective-permute-start.5) | collective-permute-done | bytes 229408 | tf_op jit(solution)/shard_map/ppermute | solution.py:183
  43.0 8.4 %collective-permute-done.12 = bf16[96,1024]{1,0:T(8,128)(2,1)S(1)} collective-permute-done((bf16[96,1024]{1,0:T(8,128)(2,1)S(1)}, bf16[96,1024]{1,0:T(8,128)(2,1)S(1)}, u32[]{:S(2)}, u32[]{:S(2)}) %collective-permute-start.12) | collective-permute-done | bytes 196640 | tf_op jit(solution)/shard_map/ppermute | solution.py:256
  53.0 5.8 %collective-permute-start.14 = (bf16[96,1024]{1,0:T(8,128)(2,1)S(1)}, bf16[96,1024]{1,0:T(8,128)(2,1)S(1)}, u32[]{:S(2)}, u32[]{:S(2)}) collective-permute-start(bf16[96,1024]{1,0:T(8,128)(2,1)S(1)} %broadcast_select_fusion), channel_id=1, source_target_pairs={{48,16},{32,0},{16,48},{0,32},{64,96},{80,112},{96,64},{112,80},{4... | collective-permute-start | bytes 589832 | tf_op jit(solution)/shard_map/ppermute | solution.py:258
  58.9 3.0 %collective-permute-done.15 = bf16[96,1024]{1,0:T(8,128)(2,1)S(1)} collective-permute-done((bf16[96,1024]{1,0:T(8,128)(2,1)S(1)}, bf16[96,1024]{1,0:T(8,128)(2,1)S(1)}, u32[]{:S(2)}, u32[]{:S(2)}) %collective-permute-start.15) | collective-permute-done | bytes 196640 | tf_op jit(solution)/shard_map/ppermute | solution.py:258
  62.4 8.9 %collective-permute-done.14 = bf16[96,1024]{1,0:T(8,128)(2,1)S(1)} collective-permute-done((bf16[96,1024]{1,0:T(8,128)(2,1)S(1)}, bf16[96,1024]{1,0:T(8,128)(2,1)S(1)}, u32[]{:S(2)}, u32[]{:S(2)}) %collective-permute-start.14) | collective-permute-done | bytes 196640 | tf_op jit(solution)/shard_map/ppermute | solution.py:258
  71.4 4.2 %collective-permute-done.13 = bf16[96,1024]{1,0:T(8,128)(2,1)S(1)} collective-permute-done((bf16[96,1024]{1,0:T(8,128)(2,1)S(1)}, bf16[96,1024]{1,0:T(8,128)(2,1)S(1)}, u32[]{:S(2)}, u32[]{:S(2)}) %collective-permute-start.13) | collective-permute-done | bytes 196640 | tf_op jit(solution)/shard_map/ppermute | solution.py:258
  76.0 2.1 collective-permute-done.16
  78.2 8.8 %shard_map.144 = (bf16[16,128,512]{2,1,0:T(8,128)(2,1)S(1)}, bf16[768,1024]{1,0:T(8,128)(2,1)S(1)}, f32[8,128]{1,0:T(8,128)S(1)}) custom-call(f32[4]{0:T(128)S(1)} %pad_maximum_fusion.12.factors, s32[1024,1]{1,0:T(8,128)S(1)} %copy.16.partner, s32[1,768]{1,0:T(1,128)S(1)} %add.363.columns, bf16[16,128,512]{2,1,0:T(8,128)(2,1)S(1)} %constant_dynamic-update-slice_fusion.emb_i, ...), custom_call_target="tpu_custom_call" | custom-call | tf_op jit(solution)/shard_map/pallas_call | solution.py:118
  87.4 2.2 collective-permute-done.17
  89.9 9.0 %collective-permute-start.18 = (bf16[96,1024]{1,0:T(8,128)(2,1)S(1)}, bf16[96,1024]{1,0:T(8,128)(2,1)S(1)}, u32[]{:S(2)}, u32[]{:S(2)}) collective-permute-start(bf16[96,1024]{1,0:T(8,128)(2,1)S(1)} %get-tuple-element.109), channel_id=1, source_target_pairs={{48,0},{32,48},{16,32},{0,16},{64,112},{80,64},{96,80},{112,96},{4... | collective-permute-start | bytes 589832 | tf_op jit(solution)/shard_map/ppermute | solution.py:287
  98.9 2.3 collective-permute-start.19
  103.5 3.2 %collective-permute-done.18 = bf16[96,1024]{1,0:T(8,128)(2,1)S(1)} collective-permute-done((bf16[96,1024]{1,0:T(8,128)(2,1)S(1)}, bf16[96,1024]{1,0:T(8,128)(2,1)S(1)}, u32[]{:S(2)}, u32[]{:S(2)}) %collective-permute-start.18) | collective-permute-done | bytes 196640 | tf_op jit(solution)/shard_map/ppermute | solution.py:287
  106.7 5.4 %collective-permute-done.19 = bf16[96,1024]{1,0:T(8,128)(2,1)S(1)} collective-permute-done((bf16[96,1024]{1,0:T(8,128)(2,1)S(1)}, bf16[96,1024]{1,0:T(8,128)(2,1)S(1)}, u32[]{:S(2)}, u32[]{:S(2)}) %collective-permute-start.19) | collective-permute-done | bytes 196640 | tf_op jit(solution)/shard_map/ppermute | solution.py:287
  112.1 4.2 %collective-permute-start.20 = (bf16[96,1024]{1,0:T(8,128)(2,1)S(1)}, bf16[96,1024]{1,0:T(8,128)(2,1)S(1)}, u32[]{:S(2)}, u32[]{:S(2)}) collective-permute-start(bf16[96,1024]{1,0:T(8,128)(2,1)S(1)} %get-tuple-element.107), channel_id=1, source_target_pairs={{48,32},{32,16},{16,0},{0,48},{64,80},{80,96},{96,112},{112,64},{4... | collective-permute-start | bytes 589832 | tf_op jit(solution)/shard_map/ppermute | solution.py:287
  116.3 12.4 %collective-permute-done.22 = bf16[4,128,512]{2,1,0:T(8,128)(2,1)S(1)} collective-permute-done((bf16[4,128,512]{2,1,0:T(8,128)(2,1)S(1)}, bf16[4,128,512]{2,1,0:T(8,128)(2,1)S(1)}, u32[]{:S(2)}, u32[]{:S(2)}) %collective-permute-start.22) | collective-permute-done | bytes 524320 | tf_op jit(solution)/shard_map/ppermute | solution.py:288
  129.9 2.8 %collective-permute-start.27 = (bf16[128,512]{1,0:T(8,128)(2,1)}, bf16[128,512]{1,0:T(8,128)(2,1)}, u32[]{:S(2)}, u32[]{:S(2)}) collective-permute-start(bf16[128,512]{1,0:T(8,128)(2,1)} %get-tuple-element.113), channel_id=1, source_target_pairs={{0,130},{2,128},{128,2},{130,0},{1,131},{3,129},{129,3},{131,1},{4... | collective-permute-start | bytes 393224 | tf_op jit(solution)/shard_map/ppermute | solution.py:183
  134.8 2.9 %collective-permute-start.24 = (bf16[96,1024]{1,0:T(8,128)(2,1)S(1)}, bf16[96,1024]{1,0:T(8,128)(2,1)S(1)}, u32[]{:S(2)}, u32[]{:S(2)}) collective-permute-start(bf16[96,1024]{1,0:T(8,128)(2,1)S(1)} %get-tuple-element.63), channel_id=1, source_target_pairs={{48,64},{32,80},{16,96},{0,112},{49,65},{33,81},{17,97},{1,113},{5... | collective-permute-start | bytes 589832 | tf_op jit(solution)/shard_map/ppermute | solution.py:304
  143.0 2.8 %collective-permute-start.30 = (bf16[96,512]{1,0:T(8,128)(2,1)S(1)}, bf16[96,512]{1,0:T(8,128)(2,1)S(1)}, u32[]{:S(2)}, u32[]{:S(2)}) collective-permute-start(bf16[96,512]{1,0:T(8,128)(2,1)S(1)} %get-tuple-element.127), channel_id=1, source_target_pairs={{0,130},{2,128},{128,2},{130,0},{1,131},{3,129},{129,3},{131,1},{4... | collective-permute-start | bytes 294920 | tf_op jit(solution)/shard_map/ppermute | solution.py:183
  145.8 4.6 %collective-permute-done.28 = bf16[96,512]{1,0:T(8,128)(2,1)S(1)} collective-permute-done((bf16[96,512]{1,0:T(8,128)(2,1)S(1)}, bf16[96,512]{1,0:T(8,128)(2,1)S(1)}, u32[]{:S(2)}, u32[]{:S(2)}) %collective-permute-start.28) | collective-permute-done | bytes 98336 | tf_op jit(solution)/shard_map/ppermute | solution.py:183
  156.2 2.7 %collective-permute-start.40 = (bf16[256,256]{1,0:T(8,128)(2,1)S(1)}, bf16[256,256]{1,0:T(8,128)(2,1)S(1)}, u32[]{:S(2)}, u32[]{:S(2)}) collective-permute-start(bf16[256,256]{1,0:T(8,128)(2,1)S(1)} %get-tuple-element.97), channel_id=1, source_target_pairs={{0,12},{4,0},{8,4},{12,8},{1,13},{5,1},{9,5},{13,9},{2,14},{6,2},{... | collective-permute-start | bytes 393224 | tf_op jit(solution)/shard_map/ppermute | solution.py:342
  158.9 2.4 collective-permute-done.34
  166.7 2.2 collective-permute-start.38
  169.0 2.9 %collective-permute-done.38 = f32[1475]{0:T(1024)S(1)} collective-permute-done((f32[1475]{0:T(1024)S(1)}, f32[1475]{0:T(1024)S(1)}, u32[]{:S(2)}, u32[]{:S(2)}) %collective-permute-start.38) | collective-permute-done | bytes 5932 | tf_op jit(solution)/shard_map/ppermute | solution.py:25
  172.5 20.9 %all_to_all.10 = bf16[16,48,256]{2,1,0:T(8,128)(2,1)S(1)} all-to-all(bf16[16,48,256]{2,1,0:T(8,128)(2,1)S(1)} %pad_maximum_fusion.4), channel_id=1, replica_groups=mesh['yl'=2,'z'=8,'x'=4,'yh'=2,'co'=2] {'yl','z'}, dimensions={0} | all-to-all | bytes 786432 | tf_op jit(solution)/shard_map/all_to_all | solution.py:29
  193.7 16.4 %all_to_all.11.first = bf16[16,48,256]{2,1,0:T(8,128)(2,1)S(1)} all-to-all(bf16[16,48,256]{2,1,0:T(8,128)(2,1)S(1)} %broadcast_in_dim.9), channel_id=1, replica_groups=mesh['yl'=2,'z'=8,'x'=4,'yh'=2,'co'=2] {'yl','z'}, dimensions={0} | all-to-all | bytes 786432 | tf_op jit(solution)/shard_map/all_to_all | solution.py:29
  214.0 15.7 %collective-permute-done.41.second = bf16[16,48,256]{2,1,0:T(8,128)(2,1)S(1)} collective-permute-done((bf16[16,48,256]{2,1,0:T(8,128)(2,1)S(1)}, bf16[16,48,256]{2,1,0:T(8,128)(2,1)S(1)}, u32[]{:S(2)}, u32[]{:S(2)}) %collective-permute-start.41) | collective-permute-done | bytes 393248 | tf_op jit(solution)/shard_map/ppermute | solution.py:405
  230.3 2.5 %shard_map.145 = (f32[1792,256]{1,0:T(8,128)}, f32[1024,256]{1,0:T(8,128)}, f32[4,16,256]{2,1,0:T(8,128)S(1)}) custom-call(s32[4]{0:T(128)S(1)} %pad_add_fusion.1.places, bf16[16,48,256]{2,1,0:T(8,128)(2,1)S(1)} %all_to_all.11.first, bf16[16,48,256]{2,1,0:T(8,128)(2,1)S(1)} %collective-permute-done.41.second, ...), custom_call_target="tpu_custom_call" | custom-call | tf_op jit(solution)/shard_map/pallas_call | solution.py:164
  (189 shorter events, 51.9 us)
Async XLA Ops:
  7.9 8.9 %collective-permute-start = (f32[1024]{0:T(1024)}, f32[1024]{0:T(1024)}, u32[]{:S(2)}, u32[]{:S(2)}) collective-permute-start(f32[1024]{0:T(1024)} %pad_maximum_fusion.11), channel_id=1, source_target_pairs={{0,1},{1,0},{2,3},{3,2},{4,5},{5,4},{6,7},{7,6},{8,9},{9,8},{10,11... | collective-permute-start | bytes 12296 | tf_op jit(solution)/shard_map/ppermute | solution.py:25
  10.9 11.7 %collective-permute-start.2 = (bf16[256,448]{1,0:T(8,128)(2,1)}, bf16[256,448]{1,0:T(8,128)(2,1)}, u32[]{:S(2)}, u32[]{:S(2)}) collective-permute-start(bf16[256,448]{1,0:T(8,128)(2,1)} %get-tuple-element.102), channel_id=1, source_target_pairs={{0,4},{4,8},{8,12},{12,0},{1,5},{5,9},{9,13},{13,1},{2,6},{6,10},{... | collective-permute-start | bytes 688136 | tf_op jit(solution)/shard_map/ppermute | solution.py:211
  12.4 16.9 %collective-permute-start.7 = (bf16[256,448]{1,0:T(8,128)(2,1)}, bf16[256,448]{1,0:T(8,128)(2,1)}, u32[]{:S(2)}, u32[]{:S(2)}) collective-permute-start(bf16[256,448]{1,0:T(8,128)(2,1)} %get-tuple-element.100), channel_id=1, source_target_pairs={{0,8},{4,12},{8,0},{12,4},{1,9},{5,13},{9,1},{13,5},{2,10},{6,14},... | collective-permute-start | bytes 688136 | tf_op jit(solution)/shard_map/ppermute | solution.py:211
  15.2 14.2 %collective-permute-start.8 = (bf16[256,448]{1,0:T(8,128)(2,1)}, bf16[256,448]{1,0:T(8,128)(2,1)}, u32[]{:S(2)}, u32[]{:S(2)}) collective-permute-start(bf16[256,448]{1,0:T(8,128)(2,1)} %get-tuple-element.99), channel_id=1, source_target_pairs={{0,12},{4,0},{8,4},{12,8},{1,13},{5,1},{9,5},{13,9},{2,14},{6,2},{... | collective-permute-start | bytes 688136 | tf_op jit(solution)/shard_map/ppermute | solution.py:211
  24.9 10.0 %collective-permute-start.4 = (bf16[224,512]{1,0:T(8,128)(2,1)S(1)}, bf16[224,512]{1,0:T(8,128)(2,1)S(1)}, u32[]{:S(2)}, u32[]{:S(2)}) collective-permute-start(bf16[224,512]{1,0:T(8,128)(2,1)S(1)} %get-tuple-element.132), channel_id=1, source_target_pairs={{0,2},{2,0},{128,130},{130,128},{1,3},{3,1},{129,131},{131,129},{4... | collective-permute-start | bytes 688136 | tf_op jit(solution)/shard_map/ppermute | solution.py:183
  28.2 11.3 %collective-permute-start.5 = (bf16[224,512]{1,0:T(8,128)(2,1)S(1)}, bf16[224,512]{1,0:T(8,128)(2,1)S(1)}, u32[]{:S(2)}, u32[]{:S(2)}) collective-permute-start(bf16[224,512]{1,0:T(8,128)(2,1)S(1)} %get-tuple-element.131), channel_id=1, source_target_pairs={{0,128},{2,130},{128,0},{130,2},{1,129},{3,131},{129,1},{131,3},{4... | collective-permute-start | bytes 688136 | tf_op jit(solution)/shard_map/ppermute | solution.py:183
  28.9 10.6 %collective-permute-start.6 = (bf16[224,512]{1,0:T(8,128)(2,1)S(1)}, bf16[224,512]{1,0:T(8,128)(2,1)S(1)}, u32[]{:S(2)}, u32[]{:S(2)}) collective-permute-start(bf16[224,512]{1,0:T(8,128)(2,1)S(1)} %get-tuple-element.130), channel_id=1, source_target_pairs={{0,130},{2,128},{128,2},{130,0},{1,131},{3,129},{129,3},{131,1},{4... | collective-permute-start | bytes 688136 | tf_op jit(solution)/shard_map/ppermute | solution.py:183
  39.6 11.9 %collective-permute-start.12 = (bf16[96,1024]{1,0:T(8,128)(2,1)S(1)}, bf16[96,1024]{1,0:T(8,128)(2,1)S(1)}, u32[]{:S(2)}, u32[]{:S(2)}) collective-permute-start(bf16[96,1024]{1,0:T(8,128)(2,1)S(1)} %pad_maximum_fusion.9), channel_id=1, source_target_pairs={{64,48},{80,32},{96,16},{112,0},{65,49},{81,33},{97,17},{113,1},{6... | collective-permute-start | bytes 589832 | tf_op jit(solution)/shard_map/ppermute | solution.py:256
  41.0 34.9 %collective-permute-start.9 = (bf16[4,128,512]{2,1,0:T(8,128)(2,1)S(1)}, bf16[4,128,512]{2,1,0:T(8,128)(2,1)S(1)}, u32[]{:S(2)}, u32[]{:S(2)}) collective-permute-start(bf16[4,128,512]{2,1,0:T(8,128)(2,1)S(1)} %pad_maximum_fusion.3), channel_id=1, source_target_pairs={{0,4},{4,8},{8,12},{12,0},{1,5},{5,9},{9,13},{13,1},{2,6},{6,10},{... | collective-permute-start | bytes 1572872 | tf_op jit(solution)/shard_map/ppermute | solution.py:257
  41.6 34.2 %collective-permute-start.10 = (bf16[4,128,512]{2,1,0:T(8,128)(2,1)S(1)}, bf16[4,128,512]{2,1,0:T(8,128)(2,1)S(1)}, u32[]{:S(2)}, u32[]{:S(2)}) collective-permute-start(bf16[4,128,512]{2,1,0:T(8,128)(2,1)S(1)} %pad_maximum_fusion.3), channel_id=1, source_target_pairs={{0,8},{4,12},{8,0},{12,4},{1,9},{5,13},{9,1},{13,5},{2,10},{6,14},... | collective-permute-start | bytes 1572872 | tf_op jit(solution)/shard_map/ppermute | solution.py:257
  51.5 10.5 %collective-permute-start.15 = (bf16[96,1024]{1,0:T(8,128)(2,1)S(1)}, bf16[96,1024]{1,0:T(8,128)(2,1)S(1)}, u32[]{:S(2)}, u32[]{:S(2)}) collective-permute-start(bf16[96,1024]{1,0:T(8,128)(2,1)S(1)} %broadcast_select_fusion), channel_id=1, source_target_pairs={{48,0},{32,48},{16,32},{0,16},{64,112},{80,64},{96,80},{112,96},{4... | collective-permute-start | bytes 589832 | tf_op jit(solution)/shard_map/ppermute | solution.py:258
  53.0 18.4 %collective-permute-start.14 = (bf16[96,1024]{1,0:T(8,128)(2,1)S(1)}, bf16[96,1024]{1,0:T(8,128)(2,1)S(1)}, u32[]{:S(2)}, u32[]{:S(2)}) collective-permute-start(bf16[96,1024]{1,0:T(8,128)(2,1)S(1)} %broadcast_select_fusion), channel_id=1, source_target_pairs={{48,16},{32,0},{16,48},{0,32},{64,96},{80,112},{96,64},{112,80},{4... | collective-permute-start | bytes 589832 | tf_op jit(solution)/shard_map/ppermute | solution.py:258
  58.8 16.7 %collective-permute-start.13 = (bf16[96,1024]{1,0:T(8,128)(2,1)S(1)}, bf16[96,1024]{1,0:T(8,128)(2,1)S(1)}, u32[]{:S(2)}, u32[]{:S(2)}) collective-permute-start(bf16[96,1024]{1,0:T(8,128)(2,1)S(1)} %broadcast_select_fusion), channel_id=1, source_target_pairs={{48,32},{32,16},{16,0},{0,48},{64,80},{80,96},{96,112},{112,64},{4... | collective-permute-start | bytes 589832 | tf_op jit(solution)/shard_map/ppermute | solution.py:258
  61.9 14.0 %collective-permute-start.11 = (bf16[4,128,512]{2,1,0:T(8,128)(2,1)S(1)}, bf16[4,128,512]{2,1,0:T(8,128)(2,1)S(1)}, u32[]{:S(2)}, u32[]{:S(2)}) collective-permute-start(bf16[4,128,512]{2,1,0:T(8,128)(2,1)S(1)} %pad_maximum_fusion.3), channel_id=1, source_target_pairs={{0,12},{4,0},{8,4},{12,8},{1,13},{5,1},{9,5},{13,9},{2,14},{6,2},{... | collective-permute-start | bytes 1572872 | tf_op jit(solution)/shard_map/ppermute | solution.py:257
  89.9 16.7 %collective-permute-start.18 = (bf16[96,1024]{1,0:T(8,128)(2,1)S(1)}, bf16[96,1024]{1,0:T(8,128)(2,1)S(1)}, u32[]{:S(2)}, u32[]{:S(2)}) collective-permute-start(bf16[96,1024]{1,0:T(8,128)(2,1)S(1)} %get-tuple-element.109), channel_id=1, source_target_pairs={{48,0},{32,48},{16,32},{0,16},{64,112},{80,64},{96,80},{112,96},{4... | collective-permute-start | bytes 589832 | tf_op jit(solution)/shard_map/ppermute | solution.py:287
  98.9 13.2 %collective-permute-start.19 = (bf16[96,1024]{1,0:T(8,128)(2,1)S(1)}, bf16[96,1024]{1,0:T(8,128)(2,1)S(1)}, u32[]{:S(2)}, u32[]{:S(2)}) collective-permute-start(bf16[96,1024]{1,0:T(8,128)(2,1)S(1)} %get-tuple-element.108), channel_id=1, source_target_pairs={{48,16},{32,0},{16,48},{0,32},{64,96},{80,112},{96,64},{112,80},{4... | collective-permute-start | bytes 589832 | tf_op jit(solution)/shard_map/ppermute | solution.py:287
  101.4 14.9 %collective-permute-start.21 = (bf16[4,128,512]{2,1,0:T(8,128)(2,1)S(1)}, bf16[4,128,512]{2,1,0:T(8,128)(2,1)S(1)}, u32[]{:S(2)}, u32[]{:S(2)}) collective-permute-start(bf16[4,128,512]{2,1,0:T(8,128)(2,1)S(1)} %get-tuple-element.90), channel_id=1, source_target_pairs={{0,12},{4,0},{8,4},{12,8},{1,13},{5,1},{9,5},{13,9},{2,14},{6,2},{... | collective-permute-start | bytes 1572872 | tf_op jit(solution)/shard_map/ppermute | solution.py:288
  103.1 25.6 %collective-permute-start.22 = (bf16[4,128,512]{2,1,0:T(8,128)(2,1)S(1)}, bf16[4,128,512]{2,1,0:T(8,128)(2,1)S(1)}, u32[]{:S(2)}, u32[]{:S(2)}) collective-permute-start(bf16[4,128,512]{2,1,0:T(8,128)(2,1)S(1)} %get-tuple-element.89), channel_id=1, source_target_pairs={{0,4},{4,8},{8,12},{12,0},{1,5},{5,9},{9,13},{13,1},{2,6},{6,10},{... | collective-permute-start | bytes 1572872 | tf_op jit(solution)/shard_map/ppermute | solution.py:288
  112.1 16.6 %collective-permute-start.23 = (bf16[4,128,512]{2,1,0:T(8,128)(2,1)S(1)}, bf16[4,128,512]{2,1,0:T(8,128)(2,1)S(1)}, u32[]{:S(2)}, u32[]{:S(2)}) collective-permute-start(bf16[4,128,512]{2,1,0:T(8,128)(2,1)S(1)} %get-tuple-element.56), channel_id=1, source_target_pairs={{0,8},{4,12},{8,0},{12,4},{1,9},{5,13},{9,1},{13,5},{2,10},{6,14},... | collective-permute-start | bytes 1572872 | tf_op jit(solution)/shard_map/ppermute | solution.py:290
  112.1 16.6 %collective-permute-start.20 = (bf16[96,1024]{1,0:T(8,128)(2,1)S(1)}, bf16[96,1024]{1,0:T(8,128)(2,1)S(1)}, u32[]{:S(2)}, u32[]{:S(2)}) collective-permute-start(bf16[96,1024]{1,0:T(8,128)(2,1)S(1)} %get-tuple-element.107), channel_id=1, source_target_pairs={{48,32},{32,16},{16,0},{0,48},{64,80},{80,96},{96,112},{112,64},{4... | collective-permute-start | bytes 589832 | tf_op jit(solution)/shard_map/ppermute | solution.py:287
  129.9 7.8 %collective-permute-start.27 = (bf16[128,512]{1,0:T(8,128)(2,1)}, bf16[128,512]{1,0:T(8,128)(2,1)}, u32[]{:S(2)}, u32[]{:S(2)}) collective-permute-start(bf16[128,512]{1,0:T(8,128)(2,1)} %get-tuple-element.113), channel_id=1, source_target_pairs={{0,130},{2,128},{128,2},{130,0},{1,131},{3,129},{129,3},{131,1},{4... | collective-permute-start | bytes 393224 | tf_op jit(solution)/shard_map/ppermute | solution.py:183
  141.2 9.2 %collective-permute-start.31 = (bf16[96,512]{1,0:T(8,128)(2,1)S(1)}, bf16[96,512]{1,0:T(8,128)(2,1)S(1)}, u32[]{:S(2)}, u32[]{:S(2)}) collective-permute-start(bf16[96,512]{1,0:T(8,128)(2,1)S(1)} %get-tuple-element.127), channel_id=1, source_target_pairs={{0,2},{2,0},{128,130},{130,128},{1,3},{3,1},{129,131},{131,129},{4... | collective-permute-start | bytes 294920 | tf_op jit(solution)/shard_map/ppermute | solution.py:183
  143.0 7.5 %collective-permute-start.30 = (bf16[96,512]{1,0:T(8,128)(2,1)S(1)}, bf16[96,512]{1,0:T(8,128)(2,1)S(1)}, u32[]{:S(2)}, u32[]{:S(2)}) collective-permute-start(bf16[96,512]{1,0:T(8,128)(2,1)S(1)} %get-tuple-element.127), channel_id=1, source_target_pairs={{0,130},{2,128},{128,2},{130,0},{1,131},{3,129},{129,3},{131,1},{4... | collective-permute-start | bytes 294920 | tf_op jit(solution)/shard_map/ppermute | solution.py:183
  150.8 10.4 %collective-permute-start.34 = (bf16[256,256]{1,0:T(8,128)(2,1)S(1)}, bf16[256,256]{1,0:T(8,128)(2,1)S(1)}, u32[]{:S(2)}, u32[]{:S(2)}) collective-permute-start(bf16[256,256]{1,0:T(8,128)(2,1)S(1)} %maximum_select_fusion.4), channel_id=1, source_target_pairs={{0,4},{4,8},{8,12},{12,0},{1,5},{5,9},{9,13},{13,1},{2,6},{6,10},{... | collective-permute-start | bytes 393224 | tf_op jit(solution)/shard_map/ppermute | solution.py:325
  150.9 10.3 %collective-permute-start.35 = (bf16[256,256]{1,0:T(8,128)(2,1)S(1)}, bf16[256,256]{1,0:T(8,128)(2,1)S(1)}, u32[]{:S(2)}, u32[]{:S(2)}) collective-permute-start(bf16[256,256]{1,0:T(8,128)(2,1)S(1)} %maximum_select_fusion.4), channel_id=1, source_target_pairs={{0,8},{4,12},{8,0},{12,4},{1,9},{5,13},{9,1},{13,5},{2,10},{6,14},... | collective-permute-start | bytes 393224 | tf_op jit(solution)/shard_map/ppermute | solution.py:325
  152.6 9.5 %collective-permute-start.36 = (bf16[256,256]{1,0:T(8,128)(2,1)S(1)}, bf16[256,256]{1,0:T(8,128)(2,1)S(1)}, u32[]{:S(2)}, u32[]{:S(2)}) collective-permute-start(bf16[256,256]{1,0:T(8,128)(2,1)S(1)} %maximum_select_fusion.4), channel_id=1, source_target_pairs={{0,12},{4,0},{8,4},{12,8},{1,13},{5,1},{9,5},{13,9},{2,14},{6,2},{... | collective-permute-start | bytes 393224 | tf_op jit(solution)/shard_map/ppermute | solution.py:325
  155.1 8.4 %collective-permute-start.33 = (bf16[256,256]{1,0:T(8,128)(2,1)S(1)}, bf16[256,256]{1,0:T(8,128)(2,1)S(1)}, u32[]{:S(2)}, u32[]{:S(2)}) collective-permute-start(bf16[256,256]{1,0:T(8,128)(2,1)S(1)} %get-tuple-element.96), channel_id=1, source_target_pairs={{0,4},{4,8},{8,12},{12,0},{1,5},{5,9},{9,13},{13,1},{2,6},{6,10},{... | collective-permute-start | bytes 393224 | tf_op jit(solution)/shard_map/ppermute | solution.py:342
  156.2 12.7 %collective-permute-start.40 = (bf16[256,256]{1,0:T(8,128)(2,1)S(1)}, bf16[256,256]{1,0:T(8,128)(2,1)S(1)}, u32[]{:S(2)}, u32[]{:S(2)}) collective-permute-start(bf16[256,256]{1,0:T(8,128)(2,1)S(1)} %get-tuple-element.97), channel_id=1, source_target_pairs={{0,12},{4,0},{8,4},{12,8},{1,13},{5,1},{9,5},{13,9},{2,14},{6,2},{... | collective-permute-start | bytes 393224 | tf_op jit(solution)/shard_map/ppermute | solution.py:342
  161.2 7.6 %collective-permute-start.39 = (bf16[256,256]{1,0:T(8,128)(2,1)S(1)}, bf16[256,256]{1,0:T(8,128)(2,1)S(1)}, u32[]{:S(2)}, u32[]{:S(2)}) collective-permute-start(bf16[256,256]{1,0:T(8,128)(2,1)S(1)} %get-tuple-element.98), channel_id=1, source_target_pairs={{0,8},{4,12},{8,0},{12,4},{1,9},{5,13},{9,1},{13,5},{2,10},{6,14},... | collective-permute-start | bytes 393224 | tf_op jit(solution)/shard_map/ppermute | solution.py:342
  210.1 19.6 %collective-permute-start.41 = (bf16[16,48,256]{2,1,0:T(8,128)(2,1)S(1)}, bf16[16,48,256]{2,1,0:T(8,128)(2,1)S(1)}, u32[]{:S(2)}, u32[]{:S(2)}) collective-permute-start(bf16[16,48,256]{2,1,0:T(8,128)(2,1)S(1)} %all_to_all.11.first), channel_id=1, source_target_pairs={{0,4},{4,8},{8,12},{12,0},{1,5},{5,9},{9,13},{13,1},{2,6},{6,10},{... | collective-permute-start | bytes 1179656 | tf_op jit(solution)/shard_map/ppermute | solution.py:405
  210.1 19.6 %collective-permute-start.42 = (bf16[16,48,256]{2,1,0:T(8,128)(2,1)S(1)}, bf16[16,48,256]{2,1,0:T(8,128)(2,1)S(1)}, u32[]{:S(2)}, u32[]{:S(2)}) collective-permute-start(bf16[16,48,256]{2,1,0:T(8,128)(2,1)S(1)} %all_to_all.11.first), channel_id=1, source_target_pairs={{0,8},{4,12},{8,0},{12,4},{1,9},{5,13},{9,1},{13,5},{2,10},{6,14},... | collective-permute-start | bytes 1179656 | tf_op jit(solution)/shard_map/ppermute | solution.py:405
  212.1 18.2 %collective-permute-start.43 = (bf16[16,48,256]{2,1,0:T(8,128)(2,1)S(1)}, bf16[16,48,256]{2,1,0:T(8,128)(2,1)S(1)}, u32[]{:S(2)}, u32[]{:S(2)}) collective-permute-start(bf16[16,48,256]{2,1,0:T(8,128)(2,1)S(1)} %all_to_all.11.first), channel_id=1, source_target_pairs={{0,12},{4,0},{8,4},{12,8},{1,13},{5,1},{9,5},{13,9},{2,14},{6,2},{... | collective-permute-start | bytes 1179656 | tf_op jit(solution)/shard_map/ppermute | solution.py:405
  (23 other events, 107.2 us)
